TPU v7x, 32 devices: a whole 2x2x4 slice. The times are simulated.
32 devices in a mesh: macro: 8 (over z, y), micro: 4 (over x, core).
Axes of the slice: x: 2, y: 2, z: 4, core: 2. Of those that a mesh axis runs over, the one named last changes fastest.
Arguments:
- motion: float32 [3, 64, 32, 128], P(None, 'macro', 'micro'), may hold values from -6 to 6
- stiffness: bfloat16 [64, 32, 128], P('macro', 'micro'), may hold values from 0.5 to 5
- point_elem: int32 [4096], P(('macro', 'micro')), may hold values from 0 to 7039, as said below
- point_owner: int32 [4096], P(('macro', 'micro')), may hold values from 0 to 7, as said below
- point_pattern: int32 [4096], P(('macro', 'micro')), may hold values from 0 to 63
- history: bfloat16 [256, 4096], P(None, ('macro', 'micro')), may hold values from -6 to 6
- basis: bfloat16 [8, 6144, 256], P('macro'), may hold values from -0.375 to 0.375
- mode_map: bfloat16 [256, 6], replicated, may hold values from -2.5 to 2.5
- weights: float32 [1024], replicated, may hold values from 0.005 to 0.05
- patterns: int32 [64, 35], replicated, may hold values from 0 to 1073741823
Outputs:
- force: float32 [3, 64, 32, 128], P(None, 'macro', 'micro')
- tangent: float32 [36, 4096], P(None, ('macro', 'micro'))
Inputs may be any that keep to these rules, and one draw needn't show every extreme that they name: `point_elem`: each row names an element of the block of the device that holds the row, with i < 7 and j < 7; the rows of one device name distinct elements. `point_owner`: the RVE of a row is hosted by the device with this macro index and the same micro index as the row's device; at most 32 rows of one device name the same host.
All inputs are finite; a program needn't handle non-finite values.
Results may differ from a plain program's by a relative error of at most 0.0004.
Values may be sent and summed in bfloat16 or wider, within the bound.
No kernel may reach another device: no remote copies, remote signals or barrier semaphores. Data moves between devices by JAX's collectives and lax.ppermute only.
A program may use at most 64 MiB of HBM per device.

v0:
```python
import jax
import jax.numpy as jnp
import numpy as np
from jax import lax
from jax.sharding import PartitionSpec as P

BULK_MODULUS = 1.0
SHEAR_MODULUS = 0.5
YIELD_STRESS = 1.5
HARDENING = 0.2
DEVIATOR = np.array(
    [
        [2.0 / 3, -1.0 / 3, -1.0 / 3, 0, 0, 0],
        [-1.0 / 3, 2.0 / 3, -1.0 / 3, 0, 0, 0],
        [-1.0 / 3, -1.0 / 3, 2.0 / 3, 0, 0, 0],
        [0, 0, 0, 0.5, 0, 0],
        [0, 0, 0, 0, 0.5, 0],
        [0, 0, 0, 0, 0, 0.5],
    ],
    np.float32,
)
UPPER_ENTRIES = np.array([6 * i + j for i in range(6) for j in range(i, 6)], np.int32)
MIRROR_ENTRIES = np.array(
    [[6 * min(i, j) + max(i, j) for j in range(6)] for i in range(6)]
).reshape(-1)
MIRROR_ENTRIES = np.array(
    [int(np.where(UPPER_ENTRIES == entry)[0][0]) for entry in MIRROR_ENTRIES], np.int32
)


def padded_2(block, sides, width):
    for axis, dim in sides:
        count = lax.axis_size(axis)
        forward = [(i, i + 1) for i in range(count - 1)]
        backward = [(target, source) for source, target in forward]
        low = lax.ppermute(
            lax.slice_in_dim(block, block.shape[dim] - width, None, axis=dim), axis, forward
        )
        high = lax.ppermute(lax.slice_in_dim(block, 0, width, axis=dim), axis, backward)
        block = jnp.concatenate([low, block, high], axis=dim)
    return block


def element_strains(node_field):
    diff_x = node_field[:, 1:, :, :] - node_field[:, :-1, :, :]
    grad_x = (
        diff_x[:, :, :-1, :-1]
        + diff_x[:, :, 1:, :-1]
        + diff_x[:, :, :-1, 1:]
        + diff_x[:, :, 1:, 1:]
    ) * 0.25
    diff_y = node_field[:, :, 1:, :] - node_field[:, :, :-1, :]
    grad_y = (
        diff_y[:, :-1, :, :-1]
        + diff_y[:, 1:, :, :-1]
        + diff_y[:, :-1, :, 1:]
        + diff_y[:, 1:, :, 1:]
    ) * 0.25
    diff_z = node_field[:, :, :, 1:] - node_field[:, :, :, :-1]
    grad_z = (
        diff_z[:, :-1, :-1, :]
        + diff_z[:, 1:, :-1, :]
        + diff_z[:, :-1, 1:, :]
        + diff_z[:, 1:, 1:, :]
    ) * 0.25
    return jnp.stack(
        [
            grad_x[0],
            grad_y[1],
            grad_z[2],
            grad_z[1] + grad_y[2],
            grad_z[0] + grad_x[2],
            grad_y[0] + grad_x[1],
        ]
    )


def elastic_stress(strain, stiff_field):
    volume = strain[0] + strain[1] + strain[2]
    normal = [
        stiff_field * (BULK_MODULUS * volume + 2.0 * SHEAR_MODULUS * (strain[c] - volume / 3.0))
        for c in range(3)
    ]
    shears = [stiff_field * (SHEAR_MODULUS * strain[c]) for c in range(3, 6)]
    return jnp.stack(normal + shears)


def nodal_forces(padded_stress):
    shape_x, shape_y, shape_z = (
        padded_stress.shape[1],
        padded_stress.shape[2],
        padded_stress.shape[3],
    )
    force_x = 0.0
    force_y = 0.0
    force_z = 0.0
    for a in (0, 1):
        for b in (0, 1):
            for c in (0, 1):
                corner_stress = padded_stress[
                    :, 1 - a : shape_x - a, 1 - b : shape_y - b, 1 - c : shape_z - c
                ]
                sign_x, sign_y, sign_z = (2.0 * a - 1.0, 2.0 * b - 1.0, 2.0 * c - 1.0)
                force_x = (
                    force_x
                    + sign_x * corner_stress[0]
                    + sign_y * corner_stress[5]
                    + sign_z * corner_stress[4]
                )
                force_y = (
                    force_y
                    + sign_x * corner_stress[5]
                    + sign_y * corner_stress[1]
                    + sign_z * corner_stress[3]
                )
                force_z = (
                    force_z
                    + sign_x * corner_stress[4]
                    + sign_y * corner_stress[3]
                    + sign_z * corner_stress[2]
                )
    return 0.25 * jnp.stack([force_x, force_y, force_z])


def model_tables(basis_rows, mode_map, weights):
    hyper_count = weights.shape[0]
    localized = jnp.dot(basis_rows, mode_map, preferred_element_type=jnp.float32).reshape(
        6, hyper_count, 6
    )
    shaped = jnp.einsum(
        "cd,dqj->cqj", jnp.asarray(DEVIATOR), localized, precision=lax.Precision.HIGHEST
    )
    deviator_table = jnp.einsum(
        "cqi,cqj->ijq", localized, shaped, precision=lax.Precision.HIGHEST
    ).reshape(36, hyper_count)
    traced = localized[0] + localized[1] + localized[2]
    volume_table = jnp.einsum(
        "q,qi,qj->ij", weights, traced, traced, precision=lax.Precision.HIGHEST
    ).reshape(36)
    return (deviator_table, volume_table)


def branch_flags(pattern_ids, patterns, hyper_count):
    matches = pattern_ids[None, :] == jnp.arange(patterns.shape[0], dtype=jnp.int32)[:, None]
    packed = jnp.sum(jnp.where(matches[:, None, :], patterns[:, :, None], 0), axis=0)
    spread = jnp.repeat(packed, 30, axis=0)[:hyper_count]
    offset = (jnp.arange(hyper_count, dtype=jnp.int32) % 30)[:, None]
    return jnp.bitwise_and(jnp.right_shift(spread, offset), 1).astype(jnp.float32)


def modal_coefficients(mode_map, macro_strain, history):
    mapped = jnp.dot(mode_map, macro_strain, preferred_element_type=jnp.float32)
    return (mapped + history.astype(jnp.float32)).astype(jnp.bfloat16)


def micro_response(
    basis_rows, coefficients, pattern_ids, patterns, deviator_table, volume_table, weights
):
    hyper_count = weights.shape[0]
    columns = coefficients.shape[1]
    point_strain = jnp.dot(basis_rows, coefficients, preferred_element_type=jnp.float32).reshape(
        6, hyper_count, columns
    )
    flag_bits = branch_flags(pattern_ids, patterns, hyper_count)
    volume = point_strain[0] + point_strain[1] + point_strain[2]
    deviator = [2.0 * SHEAR_MODULUS * (point_strain[c] - volume / 3.0) for c in range(3)]
    deviator = deviator + [SHEAR_MODULUS * point_strain[c] for c in range(3, 6)]
    magnitude = jnp.sqrt(
        deviator[0] ** 2
        + deviator[1] ** 2
        + deviator[2] ** 2
        + 2.0 * (deviator[3] ** 2 + deviator[4] ** 2 + deviator[5] ** 2)
    )
    bounded = jnp.maximum(magnitude, YIELD_STRESS)
    factor = (YIELD_STRESS + HARDENING * (bounded - YIELD_STRESS)) / bounded
    secant = 1.0 + flag_bits * (factor - 1.0)
    micro_stress = jnp.stack(
        [BULK_MODULUS * volume + secant * deviator[c] for c in range(3)]
        + [secant * deviator[c] for c in range(3, 6)]
    )
    plastic_stress = jnp.einsum("chr,h->cr", micro_stress, weights, precision=lax.Precision.HIGHEST)
    tangent = BULK_MODULUS * volume_table[:, None] + 2.0 * SHEAR_MODULUS * jnp.dot(
        deviator_table, weights[:, None] * secant, precision=lax.Precision.HIGHEST
    )
    return jnp.concatenate([plastic_stress, tangent], axis=0)


def host_blocks(
    basis_rows, coefficients, pattern_ids, patterns, deviator_table, volume_table, weights
):
    columns = coefficients.shape[1]
    block_size = 256
    block_total = columns // block_size
    mode_count = coefficients.shape[0]
    coeff_blocks = coefficients.reshape(mode_count, block_total, block_size).transpose(1, 0, 2)
    id_blocks = pattern_ids.reshape(block_total, block_size)

    def one_block(block_items):
        return micro_response(
            basis_rows,
            block_items[0],
            block_items[1],
            patterns,
            deviator_table,
            volume_table,
            weights,
        )

    outcome = lax.map(one_block, (coeff_blocks, id_blocks))
    return outcome.transpose(1, 0, 2).reshape(outcome.shape[1], columns)


def on_device(
    motion,
    stiffness,
    point_elem,
    point_owner,
    point_pattern,
    history,
    basis,
    mode_map,
    weights,
    patterns,
):
    size_x, size_y, size_z = (motion.shape[1], motion.shape[2], motion.shape[3])
    fields = jnp.concatenate([motion, stiffness.astype(jnp.float32)[None]], axis=0)
    padded = padded_2(fields, (("macro", 1), ("micro", 2)), 1)
    node_field = jnp.pad(padded[:3], ((0, 0), (0, 0), (0, 0), (0, 1)))
    strain = element_strains(node_field)
    stress = elastic_stress(strain, padded[3, : size_x + 1, : size_y + 1, :])
    point_count = point_elem.shape[0]
    hosts = lax.axis_size("macro")
    capacity = 2 * point_count // hosts
    slot_total = capacity * hosts
    positions = jnp.arange(point_count, dtype=jnp.int32)
    earlier = positions[None, :] < positions[:, None]
    same_host = point_owner[None, :] == point_owner[:, None]
    position = jnp.sum(jnp.where(same_host & earlier, 1, 0), axis=1).astype(jnp.int32)
    slot_index = position * hosts + point_owner
    own_strain = strain[:, 1:, 1:, :].reshape(6, -1)
    macro_strain = own_strain[:, point_elem].astype(jnp.bfloat16)
    outgoing = jnp.concatenate([macro_strain, history], axis=0)
    row_count = outgoing.shape[0]
    payload = jnp.zeros((row_count, slot_total), jnp.bfloat16).at[:, slot_index].set(outgoing)
    payload = payload.reshape(row_count, capacity, hosts)
    pattern_slots = jnp.zeros((1, slot_total), jnp.int32).at[0, slot_index].set(point_pattern)
    pattern_slots = pattern_slots.reshape(1, capacity, hosts)
    basis_rows = basis[0]
    deviator_table, volume_table = model_tables(basis_rows, mode_map, weights)
    data_rows = lax.all_to_all(payload, "macro", split_axis=2, concat_axis=2, tiled=True)
    id_rows = lax.all_to_all(pattern_slots, "macro", split_axis=2, concat_axis=2, tiled=True)
    items = data_rows.shape[1]
    flat_rows = data_rows.reshape(data_rows.shape[0], items * hosts)
    coefficients = modal_coefficients(mode_map, flat_rows[:6], flat_rows[6:])
    outcome = host_blocks(
        basis_rows,
        coefficients,
        id_rows.reshape(items * hosts),
        patterns,
        deviator_table,
        volume_table,
        weights,
    )
    answered = outcome.reshape(outcome.shape[0], items, hosts)
    returned_rows = lax.all_to_all(answered, "macro", split_axis=2, concat_axis=2, tiled=True)
    returned_rows = returned_rows.reshape(returned_rows.shape[0], slot_total)[:, slot_index]
    plastic_stress = returned_rows[:6]
    tangent = returned_rows[6:]
    own_stress = stress[:, 1:, 1:, :].reshape(6, -1).at[:, point_elem].set(plastic_stress)
    stress = stress.at[:, 1:, 1:, :].set(own_stress.reshape(6, size_x, size_y, size_z))
    padded_stress = jnp.pad(stress, ((0, 0), (0, 0), (0, 0), (1, 0)))
    force = nodal_forces(padded_stress)
    return (force, tangent)


def solution(mesh):
    return jax.shard_map(
        on_device,
        mesh=mesh,
        in_specs=(
            P(None, "macro", "micro", None),
            P("macro", "micro", None),
            P(("macro", "micro")),
            P(("macro", "micro")),
            P(("macro", "micro")),
            P(None, ("macro", "micro")),
            P("macro", None, None),
            P(),
            P(),
            P(),
        ),
        out_specs=(P(None, "macro", "micro", None), P(None, ("macro", "micro"))),
        check_vma=False,
    )
```

profile of v0, /device:TPU:2, one launch (start us, length us, event | category | flops | bytes accessed | tf_op | source)
XLA Modules:
  0.0 160.6 jit_solution(11403280573682112617)
XLA Ops:
  3.5 3.4 %collective-permute-start = (f32[4,1,8,128]{3,2,1,0:T(8,128)}, f32[4,1,8,128]{3,2,1,0:T(8,128)S(1)}, u32[]{:S(2)}, u32[]{:S(2)}) collective-permute-start(f32[4,1,8,128]{3,2,1,0:T(8,128)} %get-tuple-element.63), channel_id=1, source_target_pairs={{0,4},{4,8},{8,12},{12,16},{16,20},{20,24},{24,28},{1,5},{5,9},{9,... | collective-permute-start | bytes 49160 | tf_op jit(solution)/shard_map/ppermute | solution.py:36
  11.6 7.5 %all-to-all-start.1 = ((s32[1,32,8]{1,0,2:T(1,128)}), s32[1,32,8]{1,0,2:T(1,128)}, u32[]{:S(2)}, u32[]{:S(2)}) async-start(s32[1,32,8]{1,0,2:T(1,128)} %copy.77), calls=%async_computation.1 | async-start | bytes 8192 | tf_op jit(solution)/shard_map/all_to_all | solution.py:251
  21.0 1.6 fusion.8
  22.7 2.7 %copy.81 = f32[6,1024,6]{2,0,1:T(8,128)} copy(f32[6,1024,6]{1,0,2:T(8,128)S(1)} %reshape.245) | data formatting | bytes 294912 | tf_op jit(solution)/shard_map/reshape | solution.py:127
  25.5 1.7 %fusion.90 = f32[6,1024,6]{1,0,2:T(8,128)} fusion(f32[6,6,1]{1,0,2:T(8,128)} %constant.114, f32[6,1024,6]{1,0,2:T(8,128)S(1)} %reshape.245), kind=kOutput, calls=%fused_computation.223 | convolution fusion | flops 2654208 | bytes 295056 | tf_op jit(solution)/shard_map/cd,dqj->cqj/dot_general | solution.py:130
  27.1 3.6 %copy.80 = f32[6,1024,6]{0,2,1:T(8,128)} copy(f32[6,1024,6]{1,0,2:T(8,128)} %fusion.90) | data formatting | bytes 294912 | tf_op jit(solution)/shard_map/cd,dqj->cqj/dot_general | solution.py:130
  31.5 12.2 %convolution_bitcast_fusion.1 = f32[6,6,1024]{0,1,2:T(8,128)} fusion(f32[6,1024,6]{0,2,1:T(8,128)} %copy.80, f32[6,1024,6]{2,0,1:T(8,128)} %copy.81), kind=kOutput, calls=%fused_computation.48 | convolution fusion | flops 2654208 | bytes 442368 | tf_op jit(solution)/shard_map/cqi,cqj->ijq/dot_general | solution.py:133
  44.3 2.9 %copy.82 = f32[6,6,1024]{2,1,0:T(8,128)S(1)} copy(f32[6,6,1024]{0,1,2:T(8,128)} %convolution_bitcast_fusion.1) | data formatting | bytes 294912 | tf_op jit(solution)/shard_map/cqi,cqj->ijq/transpose | solution.py:133
  50.3 1.9 %collective-permute-start.2 = (f32[4,10,1,128]{3,2,1,0:T(1,128)S(1)}, f32[4,10,1,128]{3,2,1,0:T(1,128)S(1)}, u32[]{:S(2)}, u32[]{:S(2)}) collective-permute-start(f32[4,10,1,128]{3,2,1,0:T(1,128)S(1)} %get-tuple-element.61), channel_id=1, source_target_pairs={{0,1},{1,2},{2,3},{4,5},{5,6},{6,7},{8,9},{9,10},{10,11},{12,13},{... | collective-permute-start | bytes 61448 | tf_op jit(solution)/shard_map/ppermute | solution.py:36
  52.2 3.8 %collective-permute-start.3 = (f32[4,10,1,128]{3,2,1,0:T(1,128)S(1)}, f32[4,10,1,128]{3,2,1,0:T(1,128)S(1)}, u32[]{:S(2)}, u32[]{:S(2)}) collective-permute-start(f32[4,10,1,128]{3,2,1,0:T(1,128)S(1)} %get-tuple-element.62), channel_id=1, source_target_pairs={{1,0},{2,1},{3,2},{5,4},{6,5},{7,6},{9,8},{10,9},{11,10},{13,12},{... | collective-permute-start | bytes 61448 | tf_op jit(solution)/shard_map/ppermute | solution.py:39
  57.8 2.4 %reshape.244 = s32[1050,256]{1,0:T(8,128)} reshape(s32[35,30,256]{2,1,0:T(8,128)} %broadcast_in_dim.91) | data formatting | bytes 2150400 | tf_op jit(solution)/shard_map/while/body/eval_jaxpr/reshape | solution.py:146
  60.1 2.3 %slice.571 = s32[1024,256]{1,0:T(8,128)} slice(s32[1050,256]{1,0:T(8,128)} %reshape.244), slice={[0:1024], [0:256]} | slice | bytes 2097152 | tf_op jit(solution)/shard_map/while/body/eval_jaxpr/slice | solution.py:146
  62.4 2.6 %copy.89 = s32[1024,256]{0,1:T(8,128)} copy(s32[1024,256]{1,0:T(8,128)} %slice.571) | data formatting | bytes 2097152
  68.5 1.9 %copy.71 = bf16[6,8,8,128]{0,3,2,1:T(8,128)(2,1)} copy(bf16[6,8,8,128]{3,2,1,0:T(8,128)(2,1)S(1)} %slice.565) | data formatting | bytes 196608 | tf_op jit(solution)/shard_map/slice | solution.py:240
  70.4 2.6 %gather_fusion = bf16[128,6]{1,0:T(8,128)(2,1)S(1)} fusion(bf16[6,8192]{0,1:T(8,128)(2,1)} %bitcast.97, s32[1024]{0:T(1024)} %get-tuple-element.68), kind=kCustom, calls=%fused_computation | custom fusion | bytes 3584 | tf_op jit(solution)/shard_map/gather | solution.py:241
  74.8 2.0 %scatter_custom_fusion = bf16[262,256]{0,1:T(8,128)(2,1)} fusion(s32[128]{0:T(128)} %copy-done.17, bf16[128,262]{1,0:T(8,128)(2,1)} %copy.73, bf16[]{:T(256)} %constant.92.clone.1), kind=kCustom, calls=%fused_computation.99 | custom fusion | bytes 134656 | tf_op jit(solution)/shard_map/scatter | solution.py:244
  76.8 1.6 %copy.74 = bf16[262,32,8]{0,1,2:T(8,128)(2,1)} copy(bf16[262,32,8]{0,2,1:T(8,128)(2,1)} %bitcast.99) | data formatting | bytes 268288 | tf_op jit(solution)/shard_map/reshape | solution.py:245
  78.4 6.0 %all-to-all-start = ((bf16[262,32,8]{0,1,2:T(8,128)(2,1)}), bf16[262,32,8]{0,1,2:T(8,128)(2,1)}, u32[]{:S(2)}, u32[]{:S(2)}) async-start(bf16[262,32,8]{0,1,2:T(8,128)(2,1)} %copy.74), calls=%async_computation | async-start | bytes 393216 | tf_op jit(solution)/shard_map/all_to_all | solution.py:250
  84.4 1.6 multiply_dynamic-update-slice_fusion.4
  90.6 1.8 %all-to-all-done = bf16[262,32,8]{0,1,2:T(8,128)(2,1)} async-done(((bf16[262,32,8]{0,1,2:T(8,128)(2,1)}), bf16[262,32,8]{0,1,2:T(8,128)(2,1)}, u32[]{:S(2)}, u32[]{:S(2)}) %all-to-all-start) | async-done | bytes 134176 | tf_op jit(solution)/shard_map/all_to_all | solution.py:250
  94.7 4.5 %convolution_bitcast_fusion = f32[6144,256]{0,1:T(8,128)} fusion(bf16[1,6144,256]{2,1,0:T(8,128)(2,1)S(1)} %copy-done, bf16[6,256]{1,0:T(8,128)(2,1)S(1)} %slice.475, bf16[256,6]{0,1:T(8,128)(2,1)} %param.20, f32[256,32,8]{0,1,2:T(8,128)S(1)} %slice_convert_fusion), kind=kOutput, calls=%fused_computation.5 | convolution fusion | flops 806223872 | bytes 9705472 | tf_op jit(solution)/shard_map/while/body/eval_jaxpr/dot_general | solution.py:161
  99.2 4.7 %bitcast_dynamic-update-slice_fusion.5 = (f32[6,1024,256]{1,2,0:T(8,128)S(1)}, f32[1024,256]{0,1:T(8,128)S(1)}, f32[1024,256]{0,1:T(8,128)S(1)}) fusion(f32[6144,256]{0,1:T(8,128)} %convolution_bitcast_fusion, s32[1024,256]{0,1:T(8,128)} %copy.89, s32[1024]{0:T(1024)S(1)} %copy-done.11), kind=kLoop, calls=%fused_computation.61 | loop fusion | flops 8912895 | bytes 10489856
  105.7 5.4 %fusion.89 = f32[1,6,256]{2,0,1:T(1,128)S(1)} fusion(f32[6,1024,256]{1,2,0:T(8,128)S(1)} %bitcast_dynamic-update-slice_fusion, f32[1024,1,1]{0,1,2:T(1,128)S(1)} %bitcast.107), kind=kOutput, calls=%fused_computation.222 | convolution fusion | flops 18874368 | bytes 6301696 | tf_op jit(solution)/shard_map/while/body/eval_jaxpr/chr,h->cr/dot_general | solution.py:181
  113.1 4.3 %all-to-all-start.2 = ((f32[8,1,1344]{2,1,0:T(1,128)}), f32[8,1,1344]{2,1,0:T(1,128)S(1)}, u32[]{:S(2)}, u32[]{:S(2)}) async-start(f32[8,1,1344]{2,1,0:T(1,128)} %reshape.314), calls=%async_computation.2 | async-start | bytes 90112 | tf_op jit(solution)/shard_map/all_to_all | solution.py:265
  120.0 2.7 %copy.70 = f32[6,8,8,128]{0,3,2,1:T(8,128)} copy(f32[6,8,8,128]{3,2,1,0:T(8,128)S(1)} %slice.564) | data formatting | bytes 393216 | tf_op jit(solution)/shard_map/slice | solution.py:269
  126.5 5.1 %scatter_custom_fusion.2 = f32[6,8192]{0,1:T(8,128)} fusion(f32[6,8192]{0,1:T(8,128)} %bitcast.95, s32[128]{0:T(128)} %copy-done.16, f32[42,128]{0,1:T(8,128)S(1)} %bitcast.104), kind=kCustom, calls=%fused_computation.117 | custom fusion | bytes 218112 | tf_op jit(solution)/shard_map/scatter | solution.py:269
  131.6 18.1 %fusion.7 = (f32[8192]{0:T(1024)S(1)}, f32[8192]{0:T(1024)S(1)}, f32[8192]{0:T(1024)S(1)}) fusion(f32[6,8192]{0,1:T(8,128)} %scatter_custom_fusion.2), kind=kLoop, calls=%fused_computation.43 | loop fusion | flops 98304 | bytes 294912 | tf_op jit(solution)/shard_map/add | solution.py:105
  149.8 2.9 %copy.86 = f32[6,8,8,128]{3,2,1,0:T(8,128)S(1)} copy(f32[6,8,8,128]{0,3,2,1:T(8,128)} %bitcast.96) | data formatting | bytes 393216 | tf_op jit(solution)/shard_map/reshape.44
  152.7 1.8 %scatter.29 = f32[6,9,9,128]{3,2,1,0:T(8,128)} dynamic-update-slice(f32[6,9,9,128]{3,2,1,0:T(8,128)} %multiply_dynamic-update-slice_fusion, f32[6,8,8,128]{3,2,1,0:T(8,128)S(1)} %copy.86, s32[]{:T(128)} %constant.90.clone.1, s32[]{:T(128)} %constant.93.clone.1, s32[]{:T(128)} %constant.93.clone.1, s32[]{:T(128)} %constant.90.clone.1) | dynamic-update-slice | bytes 393220 | tf_op jit(solution)/shard_map/scatter | solution.py:270
  154.5 1.6 fusion.82
  156.1 1.6 fusion.40
  157.7 1.6 fusion.36
  (107 shorter events, 39.1 us)
Async XLA Ops:
  0.6 20.4 %copy-start = (bf16[1,6144,256]{2,1,0:T(8,128)(2,1)S(1)}, bf16[1,6144,256]{2,1,0:T(8,128)(2,1)}, u32[]{:S(2)}) copy-start(bf16[1,6144,256]{2,1,0:T(8,128)(2,1)} %param.19) | copy-start | bytes 9437188
  1.5 0.6 copy-start.5
  3.5 46.0 %collective-permute-start = (f32[4,1,8,128]{3,2,1,0:T(8,128)}, f32[4,1,8,128]{3,2,1,0:T(8,128)S(1)}, u32[]{:S(2)}, u32[]{:S(2)}) collective-permute-start(f32[4,1,8,128]{3,2,1,0:T(8,128)} %get-tuple-element.63), channel_id=1, source_target_pairs={{0,4},{4,8},{8,12},{12,16},{16,20},{20,24},{24,28},{1,5},{5,9},{9,... | collective-permute-start | bytes 49160 | tf_op jit(solution)/shard_map/ppermute | solution.py:36
  6.9 42.6 %collective-permute-start.1 = (f32[4,1,8,128]{3,2,1,0:T(8,128)}, f32[4,1,8,128]{3,2,1,0:T(8,128)}, u32[]{:S(2)}, u32[]{:S(2)}) collective-permute-start(f32[4,1,8,128]{3,2,1,0:T(8,128)} %get-tuple-element.64), channel_id=1, source_target_pairs={{4,0},{8,4},{12,8},{16,12},{20,16},{24,20},{28,24},{5,1},{9,5},{13... | collective-permute-start | bytes 49160 | tf_op jit(solution)/shard_map/ppermute | solution.py:39
  9.8 11.3 %copy-start.17 = (s32[128]{0:T(128)}, s32[128]{0:T(128)S(1)}, u32[]{:S(2)}) copy-start(s32[128]{0:T(128)S(1)} %compare_select_fusion) | copy-start | bytes 1540
  11.6 36.9 %all-to-all-start.1 = ((s32[1,32,8]{1,0,2:T(1,128)}), s32[1,32,8]{1,0,2:T(1,128)}, u32[]{:S(2)}, u32[]{:S(2)}) async-start(s32[1,32,8]{1,0,2:T(1,128)} %copy.77), calls=%async_computation.1 | async-start | bytes 8192 | tf_op jit(solution)/shard_map/all_to_all | solution.py:251
  19.8 0.6 copy-start.16
  27.1 3.6 %copy-start.12 = (f32[1024]{0:T(1024)S(1)}, f32[1024]{0:T(1024)}, u32[]{:S(2)}) copy-start(f32[1024]{0:T(1024)} %param.21) | copy-start | bytes 12292
  43.7 4.2 %copy-start.14 = (f32[6,6]{1,0:T(8,128)S(1)}, f32[6,6]{1,0:T(8,128)}, u32[]{:S(2)}) copy-start(f32[6,6]{1,0:T(8,128)} %fusion.27) | copy-start | bytes 436
  43.7 5.7 %copy-start.4 = (f32[3,8,8,128]{3,2,1,0:T(8,128)S(1)}, f32[3,8,8,128]{3,2,1,0:T(8,128)}, u32[]{:S(2)}) copy-start(f32[3,8,8,128]{3,2,1,0:T(8,128)} %param.13) | copy-start | bytes 294916
  43.7 5.7 %copy-start.6 = (f32[1,8,8,128]{3,2,1,0:T(8,128)S(1)}, f32[1,8,8,128]{3,2,1,0:T(8,128)}, u32[]{:S(2)}) copy-start(f32[1,8,8,128]{3,2,1,0:T(8,128)} %copy-done.5) | copy-start | bytes 98308
  43.7 12.3 %copy-start.10 = (s32[64,35]{0,1:T(8,128)S(1)}, s32[64,35]{0,1:T(8,128)}, u32[]{:S(2)}) copy-start(s32[64,35]{0,1:T(8,128)} %param.22) | copy-start | bytes 26884
  50.3 14.7 %collective-permute-start.2 = (f32[4,10,1,128]{3,2,1,0:T(1,128)S(1)}, f32[4,10,1,128]{3,2,1,0:T(1,128)S(1)}, u32[]{:S(2)}, u32[]{:S(2)}) collective-permute-start(f32[4,10,1,128]{3,2,1,0:T(1,128)S(1)} %get-tuple-element.61), channel_id=1, source_target_pairs={{0,1},{1,2},{2,3},{4,5},{5,6},{6,7},{8,9},{9,10},{10,11},{12,13},{... | collective-permute-start | bytes 61448 | tf_op jit(solution)/shard_map/ppermute | solution.py:36
  52.2 12.7 %collective-permute-start.3 = (f32[4,10,1,128]{3,2,1,0:T(1,128)S(1)}, f32[4,10,1,128]{3,2,1,0:T(1,128)S(1)}, u32[]{:S(2)}, u32[]{:S(2)}) collective-permute-start(f32[4,10,1,128]{3,2,1,0:T(1,128)S(1)} %get-tuple-element.62), channel_id=1, source_target_pairs={{1,0},{2,1},{3,2},{5,4},{6,5},{7,6},{9,8},{10,9},{11,10},{13,12},{... | collective-permute-start | bytes 61448 | tf_op jit(solution)/shard_map/ppermute | solution.py:39
  65.0 2.1 %copy-start.7 = (f32[1,8,8,128]{3,2,1,0:T(8,128)S(1)}, f32[1,8,8,128]{3,2,1,0:T(8,128)}, u32[]{:S(2)}) copy-start(f32[1,8,8,128]{3,2,1,0:T(8,128)} %copy-done.5) | copy-start | bytes 98308
  65.0 1.2 copy-start.9
  66.2 2.3 %copy-start.3 = (f32[3,9,9,128]{3,2,1,0:T(8,128)}, f32[3,9,9,128]{3,2,1,0:T(8,128)S(1)}, u32[]{:S(2)}) copy-start(f32[3,9,9,128]{3,2,1,0:T(8,128)S(1)} %fusion.22) | copy-start | bytes 373252
  66.4 0.7 copy-start.2
  78.4 13.9 %all-to-all-start = ((bf16[262,32,8]{0,1,2:T(8,128)(2,1)}), bf16[262,32,8]{0,1,2:T(8,128)(2,1)}, u32[]{:S(2)}, u32[]{:S(2)}) async-start(bf16[262,32,8]{0,1,2:T(8,128)(2,1)} %copy.74), calls=%async_computation | async-start | bytes 393216 | tf_op jit(solution)/shard_map/all_to_all | solution.py:250
  94.7 4.5 %copy-start.11 = (s32[1024]{0:T(1024)S(1)}, s32[1024]{0:T(1024)}, u32[]{:S(2)}) copy-start(s32[1024]{0:T(1024)} %add_select_fusion) | copy-start | bytes 12292
  99.2 5.0 %copy-start.1 = (f32[6144,256]{0,1:T(8,128)S(1)}, f32[6144,256]{0,1:T(8,128)}, u32[]{:S(2)}) copy-start(f32[6144,256]{0,1:T(8,128)} %convolution_bitcast_fusion) | copy-start | bytes 18874372
  105.0 0.7 copy-start.13
  105.4 5.7 %copy-start.8 = (f32[36,1024]{1,0:T(8,128)S(1)}, f32[36,1024]{1,0:T(8,128)}, u32[]{:S(2)}) copy-start(f32[36,1024]{1,0:T(8,128)} %reshape.246) | copy-start | bytes 442372
  105.5 5.7 %copy-start.15 = (f32[36]{0:T(128)S(1)}, f32[36]{0:T(128)}, u32[]{:S(2)}) copy-start(f32[36]{0:T(128)} %add.532) | copy-start | bytes 436
  113.1 11.0 %all-to-all-start.2 = ((f32[8,1,1344]{2,1,0:T(1,128)}), f32[8,1,1344]{2,1,0:T(1,128)S(1)}, u32[]{:S(2)}, u32[]{:S(2)}) async-start(f32[8,1,1344]{2,1,0:T(1,128)} %reshape.314), calls=%async_computation.2 | async-start | bytes 90112 | tf_op jit(solution)/shard_map/all_to_all | solution.py:265
where the time goes:
time: 162 us; the launch traced here: 161 us
  local copies, waits for them, and re-layouts  50.9 us (31%)
  other arithmetic  49.9 us (31%)
  starting transfers between devices  28.2 us (17%)
  matrix products  27.3 us (17%)
  waiting for transfers between devices  3.27 us (2%)
    add x2, other arithmetic, nodal_forces(): force_x + sign_x * corner_stress[0] + sign_y * corner_stress[5]  19.7 us
    unnamed x12, other arithmetic  13.5 us
    dot_general x1, matrix products, model_tables(): jnp.einsum('cqi,cqj->ijq', localized, shaped, precision=lax.Precision.HIG...  12.2 us
    all_to_all x1, starting transfers between devices, on_device(): lax.all_to_all(pattern_slots, 'macro', split_axis=2, concat_axis=2, tiled...  7.54 us
    unnamed x43, local copies, waits for them, and re-layouts  6.37 us
    all_to_all x1, starting transfers between devices, on_device(): lax.all_to_all(payload, 'macro', split_axis=2, concat_axis=2, tiled=True)  6 us
    dot_general x1, matrix products, micro_response(): jnp.einsum('chr,h->cr', micro_stress, weights, precision=lax.Precision.HI...  5.41 us
    ppermute x2, starting transfers between devices, padded_2(): lax.ppermute(lax.slice_in_dim(block, block.shape[dim] - width, None, axis...  5.33 us
  transfers between devices with their start and end apart: 7, of which 2 were waited for; matrix products, arithmetic and copies ran while one was open for 33% of the time, Pallas kernels for 0%

commit v1 on v0

v1 whole, which is shorter than its diff:
```python
import functools

import jax
import jax.numpy as jnp
from jax import lax
from jax.experimental import pallas as pl
from jax.experimental.pallas import tpu as pltpu
from jax.sharding import PartitionSpec as P

YIELD_STRESS = 1.5
HARDENING = 0.2
F32 = jnp.float32
BF16 = jnp.bfloat16
VMEM = pltpu.VMEM
ROWS = 32
UPPER = [(i, j) for i in range(6) for j in range(i, 6)]


def whole(*arrays):
    return [pl.BlockSpec(value.shape, lambda s, n=len(value.shape): (0,) * n) for value in arrays]


def iota(shape, dim):
    return lax.broadcasted_iota(jnp.int32, shape, dim)


def dot_t(left, right):
    return lax.dot_general(left, right, (((1,), (1,)), ((), ())), preferred_element_type=F32)


def pieces(value, count):
    out = []
    for _ in range(count):
        piece = value.astype(BF16)
        out.append(piece)
        value = value - piece.astype(F32)
    return out


def next_z(field):
    last = field.ndim - 1
    size = field.shape[last]
    rolled = pltpu.roll(field, size - 1, last)
    return jnp.where(iota(field.shape, last) == size - 1, 0.0, rolled)


def previous_z(field):
    last = field.ndim - 1
    rolled = pltpu.roll(field, 1, last)
    return jnp.where(iota(field.shape, last) == 0, 0.0, rolled)


def strains(here, y_up):
    grads = []
    for base, upper in zip(here, y_up):
        base_z, upper_z = next_z(base), next_z(upper)
        four = [base, upper, base_z, upper_z]
        dx = [value[1:] - value[:-1] for value in four]
        grad_x = (dx[0] + dx[1] + dx[2] + dx[3]) * 0.25
        dy, dy_z = upper - base, upper_z - base_z
        grad_y = (dy[:-1] + dy[1:] + dy_z[:-1] + dy_z[1:]) * 0.25
        dz, dz_y = base_z - base, upper_z - upper
        grad_z = (dz[:-1] + dz[1:] + dz_y[:-1] + dz_y[1:]) * 0.25
        grads.append((grad_x, grad_y, grad_z))
    return [
        grads[0][0],
        grads[1][1],
        grads[2][2],
        grads[1][2] + grads[2][1],
        grads[0][2] + grads[2][0],
        grads[0][1] + grads[1][0],
    ]


def slots_of(owner, hosts, capacity):
    points = owner.shape[1]
    chosen = iota((hosts, points), 0) == owner
    host_hot = jnp.where(chosen, 1.0, 0.0)
    before = jnp.where(iota((points, points), 0) < iota((points, points), 1), 1.0, 0.0)
    counts = jnp.dot(host_hot.astype(BF16), before.astype(BF16), preferred_element_type=F32)
    position = jnp.sum(host_hot * counts, axis=0, keepdims=True).astype(jnp.int32)
    return host_hot, position, owner * capacity + position


def dispatch_kernel(
    hosts,
    capacity,
    direct,
    motion_ref,
    stiff_ref,
    elem_ref,
    owner_ref,
    pattern_ref,
    history_ref,
    map_ref,
    payload_ref,
    *rest,
):
    size_x, size_y, size_z = motion_ref.shape[1:]
    elem, owner = elem_ref[...], owner_ref[...]
    points = elem.shape[1]
    here = [motion_ref[m] for m in range(3)]
    y_up = [pltpu.roll(field, size_y - 1, 1) for field in here]
    strain = strains(here, y_up)
    rows = (size_x - 1) * size_y
    field = jnp.concatenate([value.reshape(rows, size_z) for value in strain], axis=0)
    column = elem // size_z
    depth = elem - column * size_z
    depth_hot = jnp.where(iota((size_z, points), 0) == depth, 1.0, 0.0).astype(BF16)
    picked = jnp.dot(field.astype(BF16), depth_hot, preferred_element_type=F32)
    column_hot = iota((rows, points), 0) == column
    macro_strain = jnp.concatenate(
        [
            jnp.sum(
                jnp.where(column_hot, picked[c * rows : (c + 1) * rows], 0.0),
                axis=0,
                keepdims=True,
            )
            for c in range(6)
        ],
        axis=0,
    ).astype(BF16)
    mapped = jnp.dot(map_ref[...], macro_strain, preferred_element_type=F32)
    coefficients = (mapped + history_ref[...].astype(F32)).astype(BF16)
    host_hot, position, slot = slots_of(owner, hosts, capacity)
    slot_total = hosts * capacity
    slot_hot = jnp.where(iota((slot_total, points), 0) == slot, 1.0, 0.0).astype(BF16)
    sent = dot_t(slot_hot, coefficients).astype(BF16)
    place = position + lax.axis_index("macro") * capacity
    modes = sent.shape[1]
    place_hot = jnp.where(iota((modes, points), 0) == place, 1.0, 0.0).astype(BF16)
    ids = dot_t((host_hot * pattern_ref[...].astype(F32)).astype(BF16), place_hot)
    if direct:
        for h in range(hosts):
            payload_ref[h, :capacity, :] = sent[h * capacity : (h + 1) * capacity]
            payload_ref[h, capacity:, :] = jnp.broadcast_to(ids[h : h + 1], (16, modes)).astype(BF16)
    else:
        payload_ref[...] = sent
        rest[0][...] = ids.astype(BF16)
        rest = rest[1:]
    up_ref, down_ref = rest
    stiffness = stiff_ref[...].astype(F32)
    for i in range(size_x):
        for m in range(3):
            up_ref[m, i : i + 1, :] = motion_ref[m, i, size_y - 1 : size_y, :]
            down_ref[m, i : i + 1, :] = motion_ref[m, i, 0:1, :]
        up_ref[3, i : i + 1, :] = stiffness[i, size_y - 1 : size_y, :]


def table_kernel(basis_ref, map_ref, weights_ref, patterns_ref, table_ref, const_ref, column_ref, bits_ref):
    hyper = basis_ref.shape[1]
    lanes = 128
    modes_map = map_ref[...]
    sums = jnp.zeros((48, lanes), F32)
    patterns = patterns_ref[...]
    parts = [((patterns >> (8 * k)) & 255).astype(F32).astype(BF16) for k in range(4)]
    words = patterns.shape[1]
    for b in range(hyper // lanes):
        part = pl.ds(b * lanes, lanes)
        local = [dot_t(modes_map, basis_ref[c, part, :]) for c in range(6)]
        trace = local[0] + local[1] + local[2]
        third = trace / 3.0
        shaped = [local[c] - third for c in range(3)] + [0.5 * local[c] for c in range(3, 6)]
        weight = weights_ref[b : b + 1, :]
        weighted_trace = weight * trace
        blocks = []
        for i in range(6):
            entry = local[0][i : i + 1] * shaped[0]
            for c in range(1, 6):
                entry = entry + local[c][i : i + 1] * shaped[c]
            entry = entry * weight
            blocks.append(entry)
            sums_i = entry + trace[i : i + 1] * weighted_trace
            sums = sums + jnp.concatenate(
                [jnp.zeros((8 * i, lanes), F32)] * (i > 0)
                + [sums_i]
                + [jnp.zeros((8 * (5 - i), lanes), F32)] * (i < 5),
                axis=0,
            )
        block = jnp.concatenate(blocks, axis=0)
        high, low = pieces(block, 2)
        table_ref[0:48, part] = high
        table_ref[48:96, part] = low
        square = (lanes, lanes)
        diagonal = jnp.where(iota(square, 0) == iota(square, 1), weight, 0.0)
        column_ref[part, :] = jnp.broadcast_to(jnp.sum(diagonal, axis=1, keepdims=True), square)
        start = 30 * iota((lanes, words), 1)
        index = iota((lanes, words), 0) + b * lanes
        word_hot = jnp.where((index >= start) & (index < start + 30), 1.0, 0.0).astype(BF16)
        bytes_of = [dot_t(word_hot, part_k) for part_k in parts]
        count = patterns.shape[0]
        row = iota((lanes, count), 0) + b * lanes
        offset = row - 30 * ((row * 2185) >> 16)
        value = jnp.where(
            offset < 16,
            jnp.where(offset < 8, bytes_of[0], bytes_of[1]),
            jnp.where(offset < 24, bytes_of[2], bytes_of[3]),
        ).astype(jnp.int32)
        bits_ref[part, :] = ((value >> (offset & 7)) & 1).astype(F32).astype(BF16)
    const_ref[...] = jnp.broadcast_to(jnp.sum(sums, axis=1, keepdims=True), const_ref.shape)


def micro_kernel(
    packed,
    capacity,
    received_ref,
    basis_ref,
    bits_ref,
    column_ref,
    table_ref,
    const_ref,
    answer_ref,
    state_ref,
    hot_ref,
    strain_ref,
    high_ref,
    low_ref,
    stress_ref,
    tangent_ref,
    result_ref,
):
    step = pl.program_id(0)
    hosts = received_ref.shape[0]
    slots = hosts * capacity
    block = basis_ref.shape[1]

    @pl.when(step == 0)
    def _():
        ids = jnp.zeros((1, slots), F32)
        for h in range(hosts):
            state_ref[h * capacity : (h + 1) * capacity, :] = received_ref[h, :capacity, :]
            ids = ids + received_ref[h, capacity:, :].astype(F32)[0:1]
        shape = hot_ref.shape
        hot_ref[...] = jnp.where(iota(shape, 0) == ids.astype(jnp.int32), 1.0, 0.0).astype(BF16)
        stress_ref[...] = jnp.zeros_like(stress_ref)
        tangent_ref[...] = jnp.zeros_like(tangent_ref)

    state = state_ref[...]
    rows = basis_ref[...].reshape(6 * block, basis_ref.shape[2])
    strain_ref[...] = dot_t(rows, state).reshape(6, block, slots)
    flags = jnp.dot(bits_ref[...], hot_ref[...], preferred_element_type=F32)
    strip = 16
    sums = [jnp.zeros((8, slots), F32)] * 7
    for r in range(0, block, strip):
        part = pl.ds(r, strip)
        e = [strain_ref[c, part, :] for c in range(6)]
        volume = e[0] + e[1] + e[2]
        third = volume * (1.0 / 3.0)
        d = [e[c] - third for c in range(3)]
        normal = d[0] * d[0] + d[1] * d[1] + d[2] * d[2]
        shear = e[3] * e[3] + e[4] * e[4] + e[5] * e[5]
        square = jnp.maximum(normal + 0.5 * shear, YIELD_STRESS * YIELD_STRESS)
        factor = (YIELD_STRESS * (1.0 - HARDENING)) * lax.rsqrt(square) + (HARDENING - 1.0)
        change = flags[r : r + strip] * factor
        high = change.astype(BF16)
        high_ref[part, :] = high
        low_ref[part, :] = (change - high.astype(F32)).astype(BF16)
        column = column_ref[part, :]
        weight = jnp.concatenate([column] * (slots // column.shape[1]), axis=1)
        scaled = weight + weight * change
        terms = [scaled * d[c] for c in range(3)] + [scaled * e[c] for c in range(3, 6)]
        terms.append(weight * volume)
        for n in range(7):
            sums[n] = sums[n] + (terms[n][:8] + terms[n][8:])
    for n in range(7):
        stress_ref[n] += sums[n]
    table = table_ref[...]
    first = jnp.dot(table, high_ref[...], preferred_element_type=F32)
    second = jnp.dot(table[:48], low_ref[...], preferred_element_type=F32)
    tangent_ref[...] += first[:48] + (first[48:] + second)

    @pl.when(step == pl.num_programs(0) - 1)
    def _():
        volume = jnp.sum(stress_ref[6], axis=0, keepdims=True)
        for c in range(6):
            total = jnp.sum(stress_ref[c], axis=0, keepdims=True)
            result_ref[c : c + 1, :] = total + volume if c < 3 else 0.5 * total
        const = const_ref[...]
        const = jnp.concatenate([const] * (slots // const.shape[1]), axis=1)
        tangent = tangent_ref[...] + const
        at = 6
        for i in range(6):
            result_ref[at : at + 6 - i, :] = tangent[8 * i + i : 8 * i + 6]
            at += 6 - i
        result_ref[at:, :] = jnp.zeros((ROWS - at, slots), F32)
        if packed:
            group_of = iota((8, 128), 1) // capacity
            for h in range(hosts):
                chunk = jnp.zeros((8, 128), F32)
                tile, place = divmod(h * capacity, 128)
                for g in range(4):
                    piece = result_ref[8 * g : 8 * g + 8, tile * 128 : (tile + 1) * 128]
                    shift = (g * capacity - place) % 128
                    if shift:
                        piece = pltpu.roll(piece, shift, 1)
                    chunk = jnp.where(group_of == g, piece, chunk)
                answer_ref[h] = chunk
        else:
            answer_ref[...] = result_ref[...]


def face_kernel(motion_ref, stiff_ref, low_ref, high_ref, up_ref, down_ref):
    size_x, size_y, _ = motion_ref.shape[1:]
    last = size_x - 1
    up_ref[...] = jnp.zeros_like(up_ref)
    down_ref[...] = jnp.zeros_like(down_ref)
    for m in range(3):
        up_ref[m, :size_y, :] = motion_ref[m, last]
        up_ref[m, size_y : size_y + 1, :] = low_ref[m, last : last + 1, :]
        up_ref[m, size_y + 1 : size_y + 2, :] = high_ref[m, last : last + 1, :]
        down_ref[m, :size_y, :] = motion_ref[m, 0]
        down_ref[m, size_y : size_y + 1, :] = low_ref[m, 0:1, :]
        down_ref[m, size_y + 1 : size_y + 2, :] = high_ref[m, 0:1, :]
    up_ref[3, :size_y, :] = stiff_ref[last].astype(F32)
    up_ref[3, size_y : size_y + 1, :] = low_ref[3, last : last + 1, :]


def assemble(stress):
    lower, upper = [], []
    for here, low in stress:
        here_z, low_z = previous_z(here), previous_z(low)
        lower.append((here, low, here_z, low_z))
    def at(c, sign_x, sign_y, sign_z):
        here, low, here_z, low_z = lower[c]
        if sign_z:
            near, far = here_z - here, low_z - low
        else:
            near, far = here_z + here, low_z + low
        both = far - near if sign_y else far + near
        return both[:-1] - both[1:] if sign_x else both[:-1] + both[1:]
    force = [
        at(0, 1, 0, 0) + at(5, 0, 1, 0) + at(4, 0, 0, 1),
        at(5, 1, 0, 0) + at(1, 0, 1, 0) + at(3, 0, 0, 1),
        at(4, 1, 0, 0) + at(3, 0, 1, 0) + at(2, 0, 0, 1),
    ]
    return [0.25 * value for value in force]


def elastic_kernel(
    motion_ref,
    stiff_ref,
    elem_ref,
    y_low_ref,
    y_high_ref,
    x_low_ref,
    x_high_ref,
    force_ref,
    node_ref,
    stiff_wide_ref,
    stress_ref,
):
    size_x, size_y, size_z = motion_ref.shape[1:]
    wide = node_ref.shape[2]
    node_ref[...] = jnp.zeros_like(node_ref)
    stiff_wide_ref[...] = jnp.zeros_like(stiff_wide_ref)
    stiffness = stiff_ref[...].astype(F32)
    for m in range(3):
        for i in range(size_x):
            node_ref[m, i + 1, 1 : size_y + 1, :] = motion_ref[m, i]
            node_ref[m, i + 1, 0:1, :] = y_low_ref[m, i : i + 1, :]
            node_ref[m, i + 1, size_y + 1 : size_y + 2, :] = y_high_ref[m, i : i + 1, :]
        for at, ref in ((0, x_low_ref), (size_x + 1, x_high_ref)):
            node_ref[m, at, 1 : size_y + 1, :] = ref[m, :size_y, :]
            node_ref[m, at, 0:1, :] = ref[m, size_y : size_y + 1, :]
            node_ref[m, at, size_y + 1 : size_y + 2, :] = ref[m, size_y + 1 : size_y + 2, :]
    for i in range(size_x):
        stiff_wide_ref[i + 1, 1 : size_y + 1, :] = stiffness[i]
        stiff_wide_ref[i + 1, 0:1, :] = y_low_ref[3, i : i + 1, :]
    stiff_wide_ref[0, 1 : size_y + 1, :] = x_low_ref[3, :size_y, :]
    stiff_wide_ref[0, 0:1, :] = x_low_ref[3, size_y : size_y + 1, :]
    here = [node_ref[m] for m in range(3)]
    y_up = [pltpu.roll(value, wide - 1, 1) for value in here]
    strain = strains(here, y_up)
    stiff = stiff_wide_ref[...]
    volume = strain[0] + strain[1] + strain[2]
    rest = volume - volume * (1.0 / 3.0)
    elem = elem_ref[...]
    points = elem.shape[1]
    column = elem // size_z
    depth = elem - column * size_z
    depth_hot = jnp.where(iota((size_z, points), 0) == depth, 1.0, 0.0).astype(BF16)
    column_hot = jnp.where(iota((size_x * size_y, points), 0) == column, 1.0, 0.0).astype(BF16)
    listed = dot_t(column_hot, depth_hot)
    for i in range(size_x):
        keep = 1.0 - listed[i * size_y : (i + 1) * size_y]
        stiff_wide_ref[i + 1, 1 : size_y + 1, :] = stiffness[i] * keep
    stiff = stiff_wide_ref[...]
    for c in range(6):
        value = stiff * (rest + strain[c]) if c < 3 else stiff * (0.5 * strain[c])
        stress_ref[c] = value
    pairs = [
        (stress_ref[c, :, 1 : size_y + 1, :], stress_ref[c, :, 0:size_y, :]) for c in range(6)
    ]
    force = assemble(pairs)
    for m in range(3):
        force_ref[m] = force[m]


def final_kernel(
    packed,
    hosts,
    capacity,
    answer_ref,
    elem_ref,
    owner_ref,
    elastic_ref,
    force_ref,
    tangent_ref,
    result_ref,
):
    size_x, size_y, size_z = elastic_ref.shape[1:]
    elem, owner = elem_ref[...], owner_ref[...]
    points = elem.shape[1]
    slot_total = hosts * capacity
    _, _, slot = slots_of(owner, hosts, capacity)
    if packed:
        group_of = iota((8, 128), 1) // capacity
        per_tile = 128 // capacity
        groups = []
        for g in range(4):
            tiles = []
            for t in range(hosts // per_tile):
                tile = jnp.zeros((8, 128), F32)
                for n in range(per_tile):
                    piece = answer_ref[t * per_tile + n]
                    shift = ((n - g) * capacity) % 128
                    if shift:
                        piece = pltpu.roll(piece, shift, 1)
                    tile = jnp.where(group_of == n, piece, tile)
                tiles.append(tile)
            groups.append(jnp.concatenate(tiles, axis=1))
        answer = jnp.concatenate(groups, axis=0)
    else:
        answer = answer_ref[...]
    slot_hot = jnp.where(iota((slot_total, points), 0) == slot, 1.0, 0.0).astype(BF16)
    parts = jnp.concatenate(pieces(answer, 3), axis=0)
    chosen = jnp.dot(parts, slot_hot, preferred_element_type=F32)
    result = chosen[:ROWS] + (chosen[ROWS : 2 * ROWS] + chosen[2 * ROWS :])
    result_ref[...] = result
    for i in range(6):
        for j in range(6):
            at = 6 + UPPER.index((min(i, j), max(i, j)))
            tangent_ref[6 * i + j : 6 * i + j + 1, :] = result_ref[at : at + 1, :]
    column = elem // size_z
    depth = elem - column * size_z
    columns = size_x * size_y
    depth_hot = jnp.where(iota((size_z, points), 0) == depth, 1.0, 0.0).astype(BF16)
    column_hot = iota((columns, points), 0) == column
    stress = []
    for c in range(6):
        placed = jnp.where(column_hot, result[c : c + 1], 0.0)
        high, low = pieces(placed, 2)
        field = dot_t(high, depth_hot) + dot_t(low, depth_hot)
        field = field.reshape(size_x, size_y, size_z)
        field = jnp.concatenate([jnp.zeros((1, size_y, size_z), F32), field], axis=0)
        low_y = pltpu.roll(field, 1, 1)
        low_y = jnp.where(iota(low_y.shape, 1) == 0, 0.0, low_y)
        stress.append((field, low_y))
    force = assemble(stress)
    for m in range(3):
        force_ref[m] = elastic_ref[m] + force[m]


def shape_of(shape, dtype=F32):
    return jax.ShapeDtypeStruct(shape, dtype)


def cost(flops, size):
    return pl.CostEstimate(flops=flops, bytes_accessed=size, transcendentals=0)


PARAMS = pltpu.CompilerParams(vmem_limit_bytes=40 * 2**20)


def call(kernel, name, out_shape, args, scratch=(), flops=10**8):
    return pl.pallas_call(
        kernel,
        grid=(1,),
        out_shape=out_shape,
        in_specs=whole(*args),
        out_specs=whole(*out_shape),
        scratch_shapes=scratch,
        compiler_params=PARAMS,
        cost_estimate=cost(flops, 2**20),
        name=name,
    )(*args)


def on_device(
    motion,
    stiffness,
    point_elem,
    point_owner,
    point_pattern,
    history,
    basis,
    mode_map,
    weights,
    patterns,
):
    size_x, size_y, size_z = motion.shape[1:]
    points = point_elem.shape[0]
    hosts = lax.axis_size("macro")
    sides = lax.axis_size("micro")
    capacity = 2 * points // hosts
    slots = capacity * hosts
    modes = mode_map.shape[0]
    hyper = weights.shape[0]
    lanes = 128
    direct = capacity % 16 == 0
    packed = capacity * 4 == lanes and slots % lanes == 0
    elem = point_elem.reshape(1, points)
    owner = point_owner.reshape(1, points)
    pattern = point_pattern.reshape(1, points)

    sent = (
        [shape_of((hosts, capacity + 16, modes), BF16)]
        if direct
        else [shape_of((slots, modes), BF16), shape_of((hosts, modes), BF16)]
    )
    *payload, y_up, y_down = call(
        functools.partial(dispatch_kernel, hosts, capacity, direct),
        "dispatch",
        sent + [shape_of((4, size_x, size_z)), shape_of((3, size_x, size_z))],
        (motion, stiffness, elem, owner, pattern, history, mode_map),
    )

    if direct:
        received = lax.all_to_all(payload[0], "macro", 0, 0, tiled=True)
        groups, group = hosts, capacity
    else:
        joined = jnp.concatenate(
            [payload[0].reshape(hosts, capacity, modes), payload[1][:, None, :]], axis=1
        )
        joined = lax.all_to_all(joined, "macro", 0, 0, tiled=True)
        ids = jnp.sum(joined[:, capacity, :].astype(F32), axis=0).astype(BF16)
        received = jnp.concatenate(
            [
                joined[:, :capacity, :].reshape(1, slots, modes),
                jnp.broadcast_to(ids[None, None, :], (1, 16, modes)),
            ],
            axis=1,
        )
        groups, group = 1, slots

    forward = [(i, i + 1) for i in range(sides - 1)]
    backward = [(i + 1, i) for i in range(sides - 1)]
    y_low = lax.ppermute(y_up, "micro", forward)
    y_high = lax.ppermute(y_down, "micro", backward)

    rows = basis.reshape(6, hyper, modes)
    map_rows = jnp.pad(mode_map.T, ((0, 2), (0, 0)))
    table, const, column, bits = call(
        table_kernel,
        "tables",
        [
            shape_of((96, hyper), BF16),
            shape_of((48, lanes)),
            shape_of((hyper, lanes)),
            shape_of((hyper, patterns.shape[0]), BF16),
        ],
        (rows, map_rows, weights.reshape(hyper // lanes, lanes), patterns),
    )

    x_up, x_down = call(
        face_kernel,
        "faces",
        [shape_of((4, 16, size_z)), shape_of((3, 16, size_z))],
        (motion, stiffness, y_low, y_high),
    )

    steps = 4
    block = hyper // steps
    answer = pl.pallas_call(
        functools.partial(micro_kernel, packed, group),
        grid=(steps,),
        out_shape=shape_of((hosts, 8, lanes)) if packed else shape_of((ROWS, slots)),
        in_specs=[
            pl.BlockSpec((groups, group + 16, modes), lambda s: (0, 0, 0)),
            pl.BlockSpec((6, block, modes), lambda s: (0, s, 0)),
            pl.BlockSpec((block, patterns.shape[0]), lambda s: (s, 0)),
            pl.BlockSpec((block, lanes), lambda s: (s, 0)),
            pl.BlockSpec((96, block), lambda s: (0, s)),
            pl.BlockSpec((48, lanes), lambda s: (0, 0)),
        ],
        out_specs=pl.BlockSpec((hosts, 8, lanes), lambda s: (0, 0, 0))
        if packed
        else pl.BlockSpec((ROWS, slots), lambda s: (0, 0)),
        scratch_shapes=[
            VMEM((slots, modes), BF16),
            VMEM((patterns.shape[0], slots), BF16),
            VMEM((6, block, slots), F32),
            VMEM((block, slots), BF16),
            VMEM((block, slots), BF16),
            VMEM((7, 8, slots), F32),
            VMEM((48, slots), F32),
            VMEM((ROWS, slots), F32),
        ],
        compiler_params=PARAMS,
        cost_estimate=cost(2 * 10**9, 4 * 2**20),
        name="micro_response",
    )(received, rows, bits, column, table, const)

    if packed:
        answered = lax.all_to_all(answer, "macro", 0, 0, tiled=True)
    else:
        answered = answer.reshape(ROWS, hosts, capacity).transpose(1, 0, 2)
        answered = lax.all_to_all(answered, "macro", 0, 0, tiled=True)
        answered = answered.transpose(1, 0, 2).reshape(ROWS, slots)

    forward = [(i, i + 1) for i in range(hosts - 1)]
    backward = [(i + 1, i) for i in range(hosts - 1)]
    x_low = lax.ppermute(x_up, "macro", forward)
    x_high = lax.ppermute(x_down, "macro", backward)

    (elastic,) = call(
        elastic_kernel,
        "elastic_forces",
        [shape_of(motion.shape)],
        (motion, stiffness, elem, y_low, y_high, x_low, x_high),
        [
            VMEM((3, size_x + 2, 16, size_z), F32),
            VMEM((size_x + 1, 16, size_z), F32),
            VMEM((6, size_x + 1, 16, size_z), F32),
        ],
    )

    force, tangent = call(
        functools.partial(final_kernel, packed, hosts, capacity),
        "final_forces",
        [shape_of(motion.shape), shape_of((36, points))],
        (answered, elem, owner, elastic),
        [VMEM((ROWS, points), F32)],
    )
    return (force, tangent)


def solution(mesh):
    return jax.shard_map(
        on_device,
        mesh=mesh,
        in_specs=(
            P(None, "macro", "micro", None),
            P("macro", "micro", None),
            P(("macro", "micro")),
            P(("macro", "micro")),
            P(("macro", "micro")),
            P(None, ("macro", "micro")),
            P("macro", None, None),
            P(),
            P(),
            P(),
        ),
        out_specs=(P(None, "macro", "micro", None), P(None, ("macro", "micro"))),
        check_vma=False,
    )
```

time: 162 us -> 53 us (0.33)
  the two profiles are of different devices: /device:TPU:2 before, /device:TPU:6 now
where the time goes in v1:
time: 53 us; the launch traced here: 52.2 us
  starting transfers between devices  23.7 us (45%)
  local copies, waits for them, and re-layouts  14.4 us (27%)
  Pallas kernels  9.1 us (17%)
  waiting for transfers between devices  4.16 us (8%)
  between operations  0.74 us (1%)
    unnamed x40, local copies, waits for them, and re-layouts  13.7 us
    all_to_all x1, starting transfers between devices, on_device(): received = lax.all_to_all(payload[0], 'macro', 0, 0, tiled=True)  6.34 us
    all_to_all x1, starting transfers between devices, on_device(): answered = lax.all_to_all(answer, 'macro', 0, 0, tiled=True)  5.99 us
    pallas_call x5, Pallas kernels, call(): pl.pallas_call(kernel, grid=(1,), out_shape=out_shape, in_specs=whole(*ar...  4.61 us
    pallas_call x1, Pallas kernels, on_device(): pl.pallas_call(functools.partial(micro_kernel, packed, group), grid=(step...  4.49 us
    ppermute x1, waiting for transfers between devices, on_device(): x_high = lax.ppermute(x_down, 'macro', backward)  4.14 us
    ppermute x1, starting transfers between devices, on_device(): y_high = lax.ppermute(y_down, 'micro', backward)  3.64 us
    ppermute x1, starting transfers between devices, on_device(): x_low = lax.ppermute(x_up, 'macro', forward)  3.37 us
  transfers between devices with their start and end apart: 6, of which 1 were waited for; matrix products, arithmetic and copies ran while one was open for 3% of the time, Pallas kernels for 12%

profile of v1, /device:TPU:6, one launch (start us, length us, event | category | flops | bytes accessed | tf_op | source)
XLA Modules:
  0.0 52.2 jit_solution(972348958125828939)
XLA Ops:
  0.6 0.8 %copy.12.map_ref = bf16[256,6]{1,0:T(8,128)(2,1)S(1)} copy(bf16[256,6]{0,1:T(8,128)(2,1)} %param.17) | data formatting | bytes 6144 | tf_op args[7]
  1.5 0.9 %copy-done.9 = f32[3,8,8,128]{3,2,1,0:T(8,128)S(1)} copy-done((f32[3,8,8,128]{3,2,1,0:T(8,128)S(1)}, f32[3,8,8,128]{3,2,1,0:T(8,128)}, u32[]{:S(2)}) %copy-start.9) | copy-done | bytes 98328
  2.4 0.8 %copy-done.11 = bf16[256,128]{1,0:T(8,128)(2,1)S(1)} copy-done((bf16[256,128]{1,0:T(8,128)(2,1)S(1)}, bf16[256,128]{1,0:T(8,128)(2,1)}, u32[]{:S(2)}) %copy-start.11) | copy-done | bytes 65560
  3.2 0.7 %copy-done.12 = bf16[8,8,128]{2,1,0:T(8,128)(2,1)S(1)} copy-done((bf16[8,8,128]{2,1,0:T(8,128)(2,1)S(1)}, bf16[8,8,128]{2,1,0:T(8,128)(2,1)}, u32[]{:S(2)}) %copy-start.12) | copy-done | bytes 16408
  3.9 0.7 %copy-done.14 = s32[128]{0:T(128)S(1)} copy-done((s32[128]{0:T(128)S(1)}, s32[128]{0:T(128)}, u32[]{:S(2)}) %copy-start.14) | copy-done | bytes 536
  4.6 0.7 %copy-done.15 = s32[128]{0:T(128)S(1)} copy-done((s32[128]{0:T(128)S(1)}, s32[128]{0:T(128)}, u32[]{:S(2)}) %copy-start.15) | copy-done | bytes 536
  5.2 0.7 %copy-done.17 = s32[128]{0:T(128)S(1)} copy-done((s32[128]{0:T(128)S(1)}, s32[128]{0:T(128)}, u32[]{:S(2)}) %copy-start.17) | copy-done | bytes 536
  5.9 1.3 %dispatch.1 = (bf16[8,48,256]{2,1,0:T(8,128)(2,1)}, f32[4,8,128]{2,1,0:T(8,128)S(1)}, f32[3,8,128]{2,1,0:T(8,128)S(1)}) custom-call(f32[3,8,8,128]{3,2,1,0:T(8,128)S(1)} %copy-done.9, bf16[8,8,128]{2,1,0:T(8,128)(2,1)S(1)} %copy-done.12, s32[1,128]{1,0:T(1,128)S(1)} %bitcast.10, s32[1,128]{1,0:T(1,128)S(1)} %bitcast.13, s32[1,128]{1,0:T(1,128)S(1)} %bitcast.9, ...), custom_call_target="tpu_custom_call" | custom-call | flops 100000000 | bytes 1048576 | tf_op jit(solution)/shard_map/dispatch/pallas_call | solution.py:476
  7.2 6.3 %all-to-all-start = ((bf16[8,48,256]{2,1,0:T(8,128)(2,1)}), bf16[8,48,256]{2,1,0:T(8,128)(2,1)S(1)}, u32[]{:S(2)}, u32[]{:S(2)}) async-start(bf16[8,48,256]{2,1,0:T(8,128)(2,1)} %get-tuple-element.11), calls=%async_computation | async-start | bytes 393216 | tf_op jit(solution)/shard_map/all_to_all | solution.py:529
  13.5 1.9 %collective-permute-start = (f32[4,8,128]{2,1,0:T(8,128)S(1)}, f32[4,8,128]{2,1,0:T(8,128)S(1)}, u32[]{:S(2)}, u32[]{:S(2)}) collective-permute-start(f32[4,8,128]{2,1,0:T(8,128)S(1)} %get-tuple-element.16), channel_id=1, source_target_pairs={{0,1},{1,2},{2,3},{4,5},{5,6},{6,7},{8,9},{9,10},{10,11},{12,13},{... | collective-permute-start | bytes 49160 | tf_op jit(solution)/shard_map/ppermute | solution.py:548
  15.5 3.6 %collective-permute-start.1 = (f32[3,8,128]{2,1,0:T(8,128)S(1)}, f32[3,8,128]{2,1,0:T(8,128)S(1)}, u32[]{:S(2)}, u32[]{:S(2)}) collective-permute-start(f32[3,8,128]{2,1,0:T(8,128)S(1)} %get-tuple-element.17), channel_id=1, source_target_pairs={{1,0},{2,1},{3,2},{5,4},{6,5},{7,6},{9,8},{10,9},{11,10},{13,12},{... | collective-permute-start | bytes 36872 | tf_op jit(solution)/shard_map/ppermute | solution.py:549
  19.1 0.8 %copy.13.patterns_ref = s32[64,35]{1,0:T(8,128)S(1)} copy(s32[64,35]{0,1:T(8,128)} %param.19) | data formatting | bytes 17920 | tf_op args[9]
  19.9 0.7 %pad.4.map_ref = bf16[8,256]{1,0:T(8,128)(2,1)S(1)} pad(bf16[6,256]{1,0:T(8,128)(2,1)} %bitcast.15, bf16[]{:T(256)} %constant.2.clone.1), padding=0_2x0_0 | pad | bytes 7170 | tf_op jit(solution)/shard_map/jit(_pad)/pad | solution.py:552
  20.6 1.9 %copy-done = bf16[1,6144,256]{2,1,0:T(8,128)(2,1)S(1)} copy-done((bf16[1,6144,256]{2,1,0:T(8,128)(2,1)S(1)}, bf16[1,6144,256]{2,1,0:T(8,128)(2,1)}, u32[]{:S(2)}) %copy-start) | copy-done | bytes 3145752
  22.5 0.7 %copy-done.2 = f32[1024]{0:T(1024)S(1)} copy-done((f32[1024]{0:T(1024)S(1)}, f32[1024]{0:T(1024)}, u32[]{:S(2)}) %copy-start.2) | copy-done | bytes 4120
  23.2 1.4 %tables.1 = (bf16[96,1024]{1,0:T(8,128)(2,1)S(1)}, f32[48,128]{1,0:T(8,128)S(1)}, f32[1024,128]{1,0:T(8,128)S(1)}, bf16[1024,64]{1,0:T(8,128)(2,1)S(1)}) custom-call(bf16[6,1024,256]{2,1,0:T(8,128)(2,1)S(1)} %bitcast.6, bf16[8,256]{1,0:T(8,128)(2,1)S(1)} %pad.4.map_ref, f32[8,128]{1,0:T(8,128)S(1)} %bitcast.8, s32[64,35]{1,0:T(8,128)S(1)} %copy.13.patterns_ref), custom_call_target="tpu_custom_call" | custom-call | flops 100000000 | bytes 1048576 | tf_op jit(solution)/shard_map/tables/pallas_call | solution.py:476
  24.6 0.8 %copy-done.3 = f32[1024,128]{1,0:T(8,128)} copy-done((f32[1024,128]{1,0:T(8,128)}, f32[1024,128]{1,0:T(8,128)S(1)}, u32[]{:S(2)}) %copy-start.3) | copy-done | bytes 524312
  25.4 0.7 %copy-done.5 = bf16[1024,64]{1,0:T(8,128)(2,1)} copy-done((bf16[1024,64]{1,0:T(8,128)(2,1)}, bf16[1024,64]{1,0:T(8,128)(2,1)S(1)}, u32[]{:S(2)}) %copy-start.5) | copy-done | bytes 131096
  26.1 0.7 %copy-done.7 = bf16[96,1024]{1,0:T(8,128)(2,1)} copy-done((bf16[96,1024]{1,0:T(8,128)(2,1)}, bf16[96,1024]{1,0:T(8,128)(2,1)S(1)}, u32[]{:S(2)}) %copy-start.7) | copy-done | bytes 196632
  26.8 1.0 %copy-done.4 = f32[1024,128]{1,0:T(8,128)S(1)} copy-done((f32[1024,128]{1,0:T(8,128)S(1)}, f32[1024,128]{1,0:T(8,128)}, u32[]{:S(2)}) %copy-start.4) | copy-done | bytes 524312
  27.8 0.9 %copy-done.6 = bf16[1024,64]{1,0:T(8,128)(2,1)S(1)} copy-done((bf16[1024,64]{1,0:T(8,128)(2,1)S(1)}, bf16[1024,64]{1,0:T(8,128)(2,1)}, u32[]{:S(2)}) %copy-start.6) | copy-done | bytes 131096
  28.8 0.9 %copy-done.8 = bf16[96,1024]{1,0:T(8,128)(2,1)S(1)} copy-done((bf16[96,1024]{1,0:T(8,128)(2,1)S(1)}, bf16[96,1024]{1,0:T(8,128)(2,1)}, u32[]{:S(2)}) %copy-start.8) | copy-done | bytes 196632
  29.7 4.5 %micro_response.1 = f32[8,8,128]{2,1,0:T(8,128)} custom-call(bf16[8,48,256]{2,1,0:T(8,128)(2,1)S(1)} %all-to-all-done.received_ref, bf16[6,1024,256]{2,1,0:T(8,128)(2,1)S(1)} %bitcast.7, bf16[1024,64]{1,0:T(8,128)(2,1)S(1)} %copy-done.6, f32[1024,128]{1,0:T(8,128)S(1)} %copy-done.4, bf16[96,1024]{1,0:T(8,128)(2,1)S(1)} %copy-done.8, ...), custom_call_target="tpu_custom_call" | custom-call | flops 2000000000 | bytes 4194304 | tf_op jit(solution)/shard_map/micro_response/pallas_call | solution.py:574
  34.2 6.0 %all-to-all-start.1 = ((f32[8,8,128]{2,1,0:T(8,128)}), f32[8,8,128]{2,1,0:T(8,128)S(1)}, u32[]{:S(2)}, u32[]{:S(2)}) async-start(f32[8,8,128]{2,1,0:T(8,128)} %micro_response.1), calls=%async_computation.1 | async-start | bytes 65536 | tf_op jit(solution)/shard_map/all_to_all | solution.py:605
  40.2 0.0 collective-permute-done.1.high_ref.y_high_ref
  40.2 0.0 collective-permute-done.low_ref.y_low_ref
  40.2 3.4 %collective-permute-start.2 = (f32[4,16,128]{2,1,0:T(8,128)S(1)}, f32[4,16,128]{2,1,0:T(8,128)S(1)}, u32[]{:S(2)}, u32[]{:S(2)}) collective-permute-start(f32[4,16,128]{2,1,0:T(8,128)S(1)} %get-tuple-element.18), channel_id=1, source_target_pairs={{0,4},{4,8},{8,12},{12,16},{16,20},{20,24},{24,28},{1,5},{5,9},{9,... | collective-permute-start | bytes 98312 | tf_op jit(solution)/shard_map/ppermute | solution.py:613
  43.6 2.5 %collective-permute-start.3 = (f32[3,16,128]{2,1,0:T(8,128)S(1)}, f32[3,16,128]{2,1,0:T(8,128)S(1)}, u32[]{:S(2)}, u32[]{:S(2)}) collective-permute-start(f32[3,16,128]{2,1,0:T(8,128)S(1)} %get-tuple-element.19), channel_id=1, source_target_pairs={{4,0},{8,4},{12,8},{16,12},{20,16},{24,20},{28,24},{5,1},{9,5},{13... | collective-permute-start | bytes 73736 | tf_op jit(solution)/shard_map/ppermute | solution.py:614
  46.1 4.1 %collective-permute-done.3.x_high_ref = f32[3,16,128]{2,1,0:T(8,128)S(1)} collective-permute-done((f32[3,16,128]{2,1,0:T(8,128)S(1)}, f32[3,16,128]{2,1,0:T(8,128)S(1)}, u32[]{:S(2)}, u32[]{:S(2)}) %collective-permute-start.3) | collective-permute-done | bytes 24608 | tf_op jit(solution)/shard_map/ppermute | solution.py:614
  50.2 0.0 collective-permute-done.2.x_low_ref
  50.2 0.5 elastic_forces.1.elastic_ref
  50.8 1.4 %final_forces.1 = (f32[3,8,8,128]{3,2,1,0:T(8,128)}, f32[36,128]{1,0:T(8,128)}) custom-call(f32[8,8,128]{2,1,0:T(8,128)S(1)} %all-to-all-done.1.answer_ref, s32[1,128]{1,0:T(1,128)S(1)} %bitcast.12, s32[1,128]{1,0:T(1,128)S(1)} %bitcast.14, f32[3,8,8,128]{3,2,1,0:T(8,128)S(1)} %elastic_forces.1.elastic_ref), custom_call_target="tpu_custom_call" | custom-call | flops 100000000 | bytes 1048576 | tf_op jit(solution)/shard_map/final_forces/pallas_call | solution.py:476
  (27 shorter events, 0.1 us)
Async XLA Ops:
  1.5 0.9 %copy-start.9 = (f32[3,8,8,128]{3,2,1,0:T(8,128)S(1)}, f32[3,8,8,128]{3,2,1,0:T(8,128)}, u32[]{:S(2)}) copy-start(f32[3,8,8,128]{3,2,1,0:T(8,128)} %motion_ref.5) | copy-start | bytes 294916
  2.4 0.8 %copy-start.11 = (bf16[256,128]{1,0:T(8,128)(2,1)S(1)}, bf16[256,128]{1,0:T(8,128)(2,1)}, u32[]{:S(2)}) copy-start(bf16[256,128]{1,0:T(8,128)(2,1)} %history_ref.1) | copy-start | bytes 196612
  3.2 0.7 %copy-start.12 = (bf16[8,8,128]{2,1,0:T(8,128)(2,1)S(1)}, bf16[8,8,128]{2,1,0:T(8,128)(2,1)}, u32[]{:S(2)}) copy-start(bf16[8,8,128]{2,1,0:T(8,128)(2,1)} %stiff_ref.5) | copy-start | bytes 49156
  3.9 0.7 %copy-start.14 = (s32[128]{0:T(128)S(1)}, s32[128]{0:T(128)}, u32[]{:S(2)}) copy-start(s32[128]{0:T(128)} %param.14) | copy-start | bytes 1540
  4.6 0.7 %copy-start.15 = (s32[128]{0:T(128)S(1)}, s32[128]{0:T(128)}, u32[]{:S(2)}) copy-start(s32[128]{0:T(128)} %param.12) | copy-start | bytes 1540
  5.2 0.7 %copy-start.17 = (s32[128]{0:T(128)S(1)}, s32[128]{0:T(128)}, u32[]{:S(2)}) copy-start(s32[128]{0:T(128)} %param.13) | copy-start | bytes 1540
  7.2 19.6 %all-to-all-start = ((bf16[8,48,256]{2,1,0:T(8,128)(2,1)}), bf16[8,48,256]{2,1,0:T(8,128)(2,1)S(1)}, u32[]{:S(2)}, u32[]{:S(2)}) async-start(bf16[8,48,256]{2,1,0:T(8,128)(2,1)} %get-tuple-element.11), calls=%async_computation | async-start | bytes 393216 | tf_op jit(solution)/shard_map/all_to_all | solution.py:529
  13.5 26.7 %collective-permute-start = (f32[4,8,128]{2,1,0:T(8,128)S(1)}, f32[4,8,128]{2,1,0:T(8,128)S(1)}, u32[]{:S(2)}, u32[]{:S(2)}) collective-permute-start(f32[4,8,128]{2,1,0:T(8,128)S(1)} %get-tuple-element.16), channel_id=1, source_target_pairs={{0,1},{1,2},{2,3},{4,5},{5,6},{6,7},{8,9},{9,10},{10,11},{12,13},{... | collective-permute-start | bytes 49160 | tf_op jit(solution)/shard_map/ppermute | solution.py:548
  15.5 24.7 %collective-permute-start.1 = (f32[3,8,128]{2,1,0:T(8,128)S(1)}, f32[3,8,128]{2,1,0:T(8,128)S(1)}, u32[]{:S(2)}, u32[]{:S(2)}) collective-permute-start(f32[3,8,128]{2,1,0:T(8,128)S(1)} %get-tuple-element.17), channel_id=1, source_target_pairs={{1,0},{2,1},{3,2},{5,4},{6,5},{7,6},{9,8},{10,9},{11,10},{13,12},{... | collective-permute-start | bytes 36872 | tf_op jit(solution)/shard_map/ppermute | solution.py:549
  20.6 1.9 %copy-start = (bf16[1,6144,256]{2,1,0:T(8,128)(2,1)S(1)}, bf16[1,6144,256]{2,1,0:T(8,128)(2,1)}, u32[]{:S(2)}) copy-start(bf16[1,6144,256]{2,1,0:T(8,128)(2,1)} %param.16) | copy-start | bytes 9437188
  22.5 0.7 %copy-start.2 = (f32[1024]{0:T(1024)S(1)}, f32[1024]{0:T(1024)}, u32[]{:S(2)}) copy-start(f32[1024]{0:T(1024)} %param.18) | copy-start | bytes 12292
  23.2 3.6 %copy-start.1 = (bf16[1,6144,256]{2,1,0:T(8,128)(2,1)S(1)}, bf16[1,6144,256]{2,1,0:T(8,128)(2,1)}, u32[]{:S(2)}) copy-start(bf16[1,6144,256]{2,1,0:T(8,128)(2,1)} %param.16) | copy-start | bytes 9437188
  24.6 0.8 %copy-start.3 = (f32[1024,128]{1,0:T(8,128)}, f32[1024,128]{1,0:T(8,128)S(1)}, u32[]{:S(2)}) copy-start(f32[1024,128]{1,0:T(8,128)S(1)} %get-tuple-element.13.column_ref) | copy-start | bytes 1572868
  25.4 0.7 %copy-start.5 = (bf16[1024,64]{1,0:T(8,128)(2,1)}, bf16[1024,64]{1,0:T(8,128)(2,1)S(1)}, u32[]{:S(2)}) copy-start(bf16[1024,64]{1,0:T(8,128)(2,1)S(1)} %get-tuple-element.12.bits_ref) | copy-start | bytes 393220
  26.1 0.7 %copy-start.7 = (bf16[96,1024]{1,0:T(8,128)(2,1)}, bf16[96,1024]{1,0:T(8,128)(2,1)S(1)}, u32[]{:S(2)}) copy-start(bf16[96,1024]{1,0:T(8,128)(2,1)S(1)} %get-tuple-element.14.table_ref) | copy-start | bytes 589828
  26.8 1.0 %copy-start.4 = (f32[1024,128]{1,0:T(8,128)S(1)}, f32[1024,128]{1,0:T(8,128)}, u32[]{:S(2)}) copy-start(f32[1024,128]{1,0:T(8,128)} %copy-done.3) | copy-start | bytes 1572868
  27.8 0.9 %copy-start.6 = (bf16[1024,64]{1,0:T(8,128)(2,1)S(1)}, bf16[1024,64]{1,0:T(8,128)(2,1)}, u32[]{:S(2)}) copy-start(bf16[1024,64]{1,0:T(8,128)(2,1)} %copy-done.5) | copy-start | bytes 393220
  28.8 0.9 %copy-start.8 = (bf16[96,1024]{1,0:T(8,128)(2,1)S(1)}, bf16[96,1024]{1,0:T(8,128)(2,1)}, u32[]{:S(2)}) copy-start(bf16[96,1024]{1,0:T(8,128)(2,1)} %copy-done.7) | copy-start | bytes 589828
  29.7 10.5 %copy-start.10 = (f32[3,8,8,128]{3,2,1,0:T(8,128)S(1)}, f32[3,8,8,128]{3,2,1,0:T(8,128)}, u32[]{:S(2)}) copy-start(f32[3,8,8,128]{3,2,1,0:T(8,128)} %motion_ref.5) | copy-start | bytes 294916
  29.7 10.5 %copy-start.13 = (bf16[8,8,128]{2,1,0:T(8,128)(2,1)S(1)}, bf16[8,8,128]{2,1,0:T(8,128)(2,1)}, u32[]{:S(2)}) copy-start(bf16[8,8,128]{2,1,0:T(8,128)(2,1)} %stiff_ref.5) | copy-start | bytes 49156
  29.7 20.5 %copy-start.16 = (s32[128]{0:T(128)S(1)}, s32[128]{0:T(128)}, u32[]{:S(2)}) copy-start(s32[128]{0:T(128)} %param.12) | copy-start | bytes 1540
  29.7 21.1 %copy-start.18 = (s32[128]{0:T(128)S(1)}, s32[128]{0:T(128)}, u32[]{:S(2)}) copy-start(s32[128]{0:T(128)} %param.13) | copy-start | bytes 1540
  34.2 16.6 %all-to-all-start.1 = ((f32[8,8,128]{2,1,0:T(8,128)}), f32[8,8,128]{2,1,0:T(8,128)S(1)}, u32[]{:S(2)}, u32[]{:S(2)}) async-start(f32[8,8,128]{2,1,0:T(8,128)} %micro_response.1), calls=%async_computation.1 | async-start | bytes 65536 | tf_op jit(solution)/shard_map/all_to_all | solution.py:605
  40.2 10.0 %collective-permute-start.2 = (f32[4,16,128]{2,1,0:T(8,128)S(1)}, f32[4,16,128]{2,1,0:T(8,128)S(1)}, u32[]{:S(2)}, u32[]{:S(2)}) collective-permute-start(f32[4,16,128]{2,1,0:T(8,128)S(1)} %get-tuple-element.18), channel_id=1, source_target_pairs={{0,4},{4,8},{8,12},{12,16},{16,20},{20,24},{24,28},{1,5},{5,9},{9,... | collective-permute-start | bytes 98312 | tf_op jit(solution)/shard_map/ppermute | solution.py:613
  43.6 6.6 %collective-permute-start.3 = (f32[3,16,128]{2,1,0:T(8,128)S(1)}, f32[3,16,128]{2,1,0:T(8,128)S(1)}, u32[]{:S(2)}, u32[]{:S(2)}) collective-permute-start(f32[3,16,128]{2,1,0:T(8,128)S(1)} %get-tuple-element.19), channel_id=1, source_target_pairs={{4,0},{8,4},{12,8},{16,12},{20,16},{24,20},{28,24},{5,1},{9,5},{13... | collective-permute-start | bytes 73736 | tf_op jit(solution)/shard_map/ppermute | solution.py:614

commit v2 on v1

v2 whole, which is shorter than its diff:
```python
import functools

import jax
import jax.numpy as jnp
from jax import lax
from jax.experimental import pallas as pl
from jax.experimental.pallas import tpu as pltpu
from jax.sharding import PartitionSpec as P

YIELD_STRESS = 1.5
HARDENING = 0.2
F32 = jnp.float32
BF16 = jnp.bfloat16
VMEM = pltpu.VMEM
ROWS = 32
UPPER = [(i, j) for i in range(6) for j in range(i, 6)]


def whole(*arrays):
    return [pl.BlockSpec(value.shape, lambda s, n=len(value.shape): (0,) * n) for value in arrays]


def in_hbm(value):
    return pltpu.with_memory_space_constraint(value, pltpu.HBM)


def iota(shape, dim):
    return lax.broadcasted_iota(jnp.int32, shape, dim)


def dot_t(left, right):
    return lax.dot_general(left, right, (((1,), (1,)), ((), ())), preferred_element_type=F32)


def pieces(value, count):
    out = []
    for _ in range(count):
        piece = value.astype(BF16)
        out.append(piece)
        value = value - piece.astype(F32)
    return out


def next_z(field):
    last = field.ndim - 1
    size = field.shape[last]
    rolled = pltpu.roll(field, size - 1, last)
    return jnp.where(iota(field.shape, last) == size - 1, 0.0, rolled)


def previous_z(field):
    last = field.ndim - 1
    rolled = pltpu.roll(field, 1, last)
    return jnp.where(iota(field.shape, last) == 0, 0.0, rolled)


def corners(field):
    y_up = pltpu.roll(field, field.shape[1] - 1, 1)
    return [field, y_up, next_z(field), next_z(y_up)]


def strains(lower, upper):
    grads = []
    for low, high in zip(lower, upper):
        dx = [b - a for a, b in zip(low, high)]
        grad_x = (dx[0] + dx[1] + dx[2] + dx[3]) * 0.25
        dy = [value[1] - value[0] for value in (low, high)]
        dy_z = [value[3] - value[2] for value in (low, high)]
        grad_y = (dy[0] + dy[1] + dy_z[0] + dy_z[1]) * 0.25
        dz = [value[2] - value[0] for value in (low, high)]
        dz_y = [value[3] - value[1] for value in (low, high)]
        grad_z = (dz[0] + dz[1] + dz_y[0] + dz_y[1]) * 0.25
        grads.append((grad_x, grad_y, grad_z))
    return [
        grads[0][0],
        grads[1][1],
        grads[2][2],
        grads[1][2] + grads[2][1],
        grads[0][2] + grads[2][0],
        grads[0][1] + grads[1][0],
    ]


def block_strains(fields):
    nodes = [corners(field) for field in fields]
    return strains(
        [[value[:-1] for value in four] for four in nodes],
        [[value[1:] for value in four] for four in nodes],
    )


def elastic_of(strain, stiffness):
    volume = strain[0] + strain[1] + strain[2]
    rest = volume - volume * (1.0 / 3.0)
    normal = [stiffness * (rest + strain[c]) for c in range(3)]
    return normal + [stiffness * (0.5 * strain[c]) for c in range(3, 6)]


def slots_of(owner, hosts, capacity):
    points = owner.shape[1]
    chosen = iota((hosts, points), 0) == owner
    host_hot = jnp.where(chosen, 1.0, 0.0)
    before = jnp.where(iota((points, points), 0) < iota((points, points), 1), 1.0, 0.0)
    counts = jnp.dot(host_hot.astype(BF16), before.astype(BF16), preferred_element_type=F32)
    position = jnp.sum(host_hot * counts, axis=0, keepdims=True).astype(jnp.int32)
    return host_hot, position, owner * capacity + position


def dispatch_kernel(
    hosts,
    capacity,
    direct,
    motion_ref,
    stiff_ref,
    elem_ref,
    owner_ref,
    pattern_ref,
    history_ref,
    map_ref,
    payload_ref,
    *rest,
):
    size_x, size_y, size_z = motion_ref.shape[1:]
    elem, owner = elem_ref[...], owner_ref[...]
    points = elem.shape[1]
    strain = block_strains([motion_ref[m] for m in range(3)])
    rows = (size_x - 1) * size_y
    field = jnp.concatenate([value.reshape(rows, size_z) for value in strain], axis=0)
    column = elem // size_z
    depth = elem - column * size_z
    depth_hot = jnp.where(iota((size_z, points), 0) == depth, 1.0, 0.0).astype(BF16)
    picked = jnp.dot(field.astype(BF16), depth_hot, preferred_element_type=F32)
    column_hot = iota((rows, points), 0) == column
    macro_strain = jnp.concatenate(
        [
            jnp.sum(
                jnp.where(column_hot, picked[c * rows : (c + 1) * rows], 0.0),
                axis=0,
                keepdims=True,
            )
            for c in range(6)
        ],
        axis=0,
    ).astype(BF16)
    mapped = lax.dot_general(
        map_ref[...], macro_strain, (((0,), (0,)), ((), ())), preferred_element_type=F32
    )
    coefficients = (mapped + history_ref[...].astype(F32)).astype(BF16)
    host_hot, position, slot = slots_of(owner, hosts, capacity)
    slot_total = hosts * capacity
    slot_hot = jnp.where(iota((slot_total, points), 0) == slot, 1.0, 0.0).astype(BF16)
    sent = dot_t(slot_hot, coefficients).astype(BF16)
    place = position + lax.axis_index("macro") * capacity
    modes = sent.shape[1]
    half = modes // 2
    place_hot = jnp.where(iota((modes, points), 0) == place, 1.0, 0.0).astype(BF16)
    ids = dot_t((host_hot * pattern_ref[...].astype(F32)).astype(BF16), place_hot)
    if direct:
        for h in range(hosts):
            mine = sent[h * capacity : (h + 1) * capacity]
            payload_ref[h, :capacity, :] = mine[:, :half]
            payload_ref[h, capacity : 2 * capacity, :] = mine[:, half:]
            row = iota((8, half), 0)
            low, high = ids[h : h + 1, :half], ids[h : h + 1, half:]
            tile = jnp.where(row == 0, low, jnp.where(row == 1, high, 0.0))
            payload_ref[h, 2 * capacity :, :] = tile.astype(BF16)
    else:
        payload_ref[...] = sent
        rest[0][...] = ids.astype(BF16)
        rest = rest[1:]
    first_ref, second_ref, face_ref = rest
    stiffness = stiff_ref[...].astype(F32)
    even = lax.rem(lax.axis_index("micro"), 2) == 0
    for i in range(size_x):
        for m in range(4):
            if m < 3:
                up, down = motion_ref[m, i, size_y - 1 : size_y, :], motion_ref[m, i, 0:1, :]
            else:
                up = down = stiffness[i, size_y - 1 : size_y, :]
            first_ref[m, i : i + 1, :] = jnp.where(even, up, down)
            second_ref[m, i : i + 1, :] = jnp.where(even, down, up)
    for m in range(3):
        face_ref[m] = motion_ref[m, size_x - 1]
        face_ref[4 + m] = motion_ref[m, 0]
    face_ref[3] = stiffness[size_x - 1]
    face_ref[7] = jnp.zeros_like(face_ref[7])


def table_kernel(
    map_ref,
    weights_ref,
    patterns_ref,
    basis_ref,
    table_ref,
    const_ref,
    column_ref,
    bits_ref,
    blocks_ref,
    sems,
):
    hyper = basis_ref.shape[1]
    lanes = 128
    count = hyper // lanes
    copies = [
        pltpu.make_async_copy(
            basis_ref.at[:, pl.ds(b * lanes, lanes), :], blocks_ref.at[b], sems.at[b]
        )
        for b in range(count)
    ]
    for copy in copies:
        copy.start()
    modes_map = map_ref[...]
    modes_map = jnp.concatenate(
        [modes_map.astype(F32), jnp.zeros((2, modes_map.shape[1]), F32)], axis=0
    ).astype(BF16)
    sums = jnp.zeros((48, lanes), F32)
    patterns = patterns_ref[...]
    parts = [((patterns >> (8 * k)) & 255).astype(F32).astype(BF16) for k in range(4)]
    words, total = patterns.shape
    for b in range(count):
        part = pl.ds(b * lanes, lanes)
        weight = weights_ref[b : b + 1, :]
        square = (lanes, lanes)
        diagonal = jnp.where(iota(square, 0) == iota(square, 1), weight, 0.0)
        column_ref[part, :] = jnp.broadcast_to(jnp.sum(diagonal, axis=1, keepdims=True), square)
        start = 30 * iota((lanes, words), 1)
        index = iota((lanes, words), 0) + b * lanes
        word_hot = jnp.where((index >= start) & (index < start + 30), 1.0, 0.0).astype(BF16)
        bytes_of = [
            jnp.dot(word_hot, part_k, preferred_element_type=F32) for part_k in parts
        ]
        row = iota((lanes, total), 0) + b * lanes
        offset = row - 30 * ((row * 2185) >> 16)
        value = jnp.where(
            offset < 16,
            jnp.where(offset < 8, bytes_of[0], bytes_of[1]),
            jnp.where(offset < 24, bytes_of[2], bytes_of[3]),
        ).astype(jnp.int32)
        bits_ref[part, :] = ((value >> (offset & 7)) & 1).astype(F32).astype(BF16)
    for b in range(count):
        part = pl.ds(b * lanes, lanes)
        copies[b].wait()
        local = [dot_t(modes_map, blocks_ref[b, c]) for c in range(6)]
        trace = local[0] + local[1] + local[2]
        third = trace / 3.0
        shaped = [local[c] - third for c in range(3)] + [0.5 * local[c] for c in range(3, 6)]
        weight = weights_ref[b : b + 1, :]
        weighted_trace = weight * trace
        blocks, adds = [], []
        for i in range(6):
            entry = local[0][i : i + 1] * shaped[0]
            for c in range(1, 6):
                entry = entry + local[c][i : i + 1] * shaped[c]
            entry = entry * weight
            blocks.append(entry)
            adds.append(entry + trace[i : i + 1] * weighted_trace)
        sums = sums + jnp.concatenate(adds, axis=0)
        high, low = pieces(jnp.concatenate(blocks, axis=0), 2)
        table_ref[0:48, part] = high
        table_ref[48:96, part] = low
    const_ref[...] = jnp.broadcast_to(jnp.sum(sums, axis=1, keepdims=True), const_ref.shape)


def sides_of(first_ref, second_ref, m, at):
    even = lax.rem(lax.axis_index("micro"), 2) == 0
    first, second = first_ref[m, at : at + 1, :], second_ref[m, at : at + 1, :]
    return jnp.where(even, second, first), jnp.where(even, first, second)


def micro_kernel(
    packed,
    hosts,
    capacity,
    received_ref,
    first_ref,
    second_ref,
    face_ref,
    const_ref,
    basis_ref,
    bits_ref,
    column_ref,
    table_ref,
    answer_ref,
    *rest,
):
    if packed:
        faces_ref = None
    else:
        faces_ref, *rest = rest
    (
        state_ref,
        hot_ref,
        basis_buf,
        bits_buf,
        column_buf,
        table_buf,
        even_ref,
        odd_ref,
        high_ref,
        low_ref,
        stress_ref,
        tangent_ref,
        result_ref,
        sems,
    ) = rest
    groups = received_ref.shape[0]
    slots = groups * capacity
    count, _, block, modes = basis_buf.shape
    half = modes // 2

    def basis_copy(n):
        return pltpu.make_async_copy(
            basis_ref.at[:, pl.ds(n * block, block), :], basis_buf.at[n], sems.at[n]
        )

    others = [
        pltpu.make_async_copy(bits_ref, bits_buf, sems.at[count]),
        pltpu.make_async_copy(column_ref, column_buf, sems.at[count + 1]),
        pltpu.make_async_copy(table_ref, table_buf, sems.at[count + 2]),
    ]
    basis_copy(0).start()
    for copy in others:
        copy.start()
    for n in range(1, count):
        basis_copy(n).start()

    ids = jnp.zeros((8, half), F32)
    for h in range(groups):
        own = pl.ds(h * capacity, capacity)
        state_ref[own, :half] = received_ref[h, :capacity, :]
        state_ref[own, half:] = received_ref[h, capacity : 2 * capacity, :]
        ids = ids + received_ref[h, 2 * capacity :, :].astype(F32)
    ids = jnp.concatenate([ids[0:1], ids[1:2]], axis=1).astype(jnp.int32)
    hot_ref[...] = jnp.where(iota(hot_ref.shape, 0) == ids, 1.0, 0.0).astype(BF16)
    stress_ref[...] = jnp.zeros_like(stress_ref)
    tangent_ref[...] = jnp.zeros_like(tangent_ref)

    def rows_of(n, target):
        rows = basis_buf[n].reshape(6 * block, modes)
        target[...] = dot_t(rows, state_ref[...]).reshape(6, block, slots)

    def respond(n, strain_ref):
        part = pl.ds(pl.multiple_of(n * block, block), block)
        flags = jnp.dot(bits_buf[part, :], hot_ref[...], preferred_element_type=F32)
        strip = 16
        sums = [jnp.zeros((8, slots), F32)] * 7
        for r in range(0, block, strip):
            at = pl.ds(r, strip)
            e = [strain_ref[c, at, :] for c in range(6)]
            volume = e[0] + e[1] + e[2]
            third = volume * (1.0 / 3.0)
            d = [e[c] - third for c in range(3)]
            normal = d[0] * d[0] + d[1] * d[1] + d[2] * d[2]
            shear = e[3] * e[3] + e[4] * e[4] + e[5] * e[5]
            square = jnp.maximum(normal + 0.5 * shear, YIELD_STRESS * YIELD_STRESS)
            factor = (YIELD_STRESS * (1.0 - HARDENING)) * lax.rsqrt(square) + (HARDENING - 1.0)
            change = flags[r : r + strip] * factor
            high = change.astype(BF16)
            high_ref[at, :] = high
            low_ref[at, :] = (change - high.astype(F32)).astype(BF16)
            column = column_buf[pl.ds(pl.multiple_of(n * block, block) + r, strip), :]
            weight = jnp.concatenate([column] * (slots // column.shape[1]), axis=1)
            scaled = weight + weight * change
            terms = [scaled * d[c] for c in range(3)] + [scaled * e[c] for c in range(3, 6)]
            terms.append(weight * volume)
            for k in range(7):
                sums[k] = sums[k] + (terms[k][:8] + terms[k][8:])
        for k in range(7):
            stress_ref[k] += sums[k]
        table = table_buf[:, part]
        one = jnp.dot(table, high_ref[...], preferred_element_type=F32)
        two = jnp.dot(table[:48], low_ref[...], preferred_element_type=F32)
        tangent_ref[...] += one[:48] + (one[48:] + two)

    basis_copy(0).wait()
    rows_of(0, even_ref)
    for copy in others:
        copy.wait()

    def pair(i, carry):
        n = 2 * i
        basis_copy(n + 1).wait()
        rows_of(n + 1, odd_ref)
        respond(n, even_ref)

        @pl.when(n + 2 < count)
        def _():
            basis_copy(n + 2).wait()

        rows_of(jnp.minimum(n + 2, count - 1), even_ref)
        respond(n + 1, odd_ref)
        return carry

    lax.fori_loop(0, count // 2, pair, 0)

    volume = jnp.sum(stress_ref[6], axis=0, keepdims=True)
    for c in range(6):
        total = jnp.sum(stress_ref[c], axis=0, keepdims=True)
        result_ref[c : c + 1, :] = total + volume if c < 3 else 0.5 * total
    const = const_ref[...]
    const = jnp.concatenate([const] * (slots // const.shape[1]), axis=1)
    tangent = tangent_ref[...] + const
    at = 6
    for i in range(6):
        result_ref[at : at + 6 - i, :] = tangent[8 * i + i : 8 * i + 6]
        at += 6 - i
    result_ref[at:, :] = jnp.zeros((ROWS - at, slots), F32)

    last = first_ref.shape[1] - 1

    def faces(write):
        for m in range(4):
            write(0, 8 * m, 8, face_ref[m])
            write(1, 8 * m, 8, face_ref[4 + m])
            up = sides_of(first_ref, second_ref, m, last)
            down = sides_of(first_ref, second_ref, m, 0)
            for n in range(2):
                write(0, 32 + 2 * m + n, 1, up[n])
                write(1, 32 + 2 * m + n, 1, down[n])

    if packed:
        here = lax.axis_index("macro")
        group_of = iota((8, 128), 1) // capacity
        for h in range(hosts):
            chunk = jnp.zeros((8, 128), F32)
            tile, place = divmod(h * capacity, 128)
            for g in range(4):
                piece = result_ref[8 * g : 8 * g + 8, tile * 128 : (tile + 1) * 128]
                shift = (g * capacity - place) % 128
                if shift:
                    piece = pltpu.roll(piece, shift, 1)
                chunk = jnp.where(group_of == g, piece, chunk)
            answer_ref[h, 0:8, :] = chunk
        chunks = [jnp.minimum(here + 1, hosts - 1), jnp.maximum(here - 1, 0)]

        def write(side, row, size, value):
            answer_ref[chunks[side], 8 + row : 8 + row + size, :] = value
    else:
        answer_ref[...] = result_ref[...]

        def write(side, row, size, value):
            faces_ref[side, row : row + size, :] = value

    faces(write)


def assemble(stress):
    ready = []
    for here, low in stress:
        ready.append((here, low, previous_z(here), previous_z(low)))

    def at(c, sign_x, sign_y, sign_z):
        here, low, here_z, low_z = ready[c]
        if sign_z:
            near, far = here_z - here, low_z - low
        else:
            near, far = here_z + here, low_z + low
        both = far - near if sign_y else far + near
        return both[:-1] - both[1:] if sign_x else both[:-1] + both[1:]

    force = [
        at(0, 1, 0, 0) + at(5, 0, 1, 0) + at(4, 0, 0, 1),
        at(5, 1, 0, 0) + at(1, 0, 1, 0) + at(3, 0, 0, 1),
        at(4, 1, 0, 0) + at(3, 0, 1, 0) + at(2, 0, 0, 1),
    ]
    return [0.25 * value for value in force]


def elastic_kernel(
    hosts,
    capacity,
    motion_ref,
    stiff_ref,
    elem_ref,
    owner_ref,
    first_ref,
    second_ref,
    force_ref,
    edge_ref,
    index_ref,
    node_ref,
    wide_ref,
    stress_ref,
):
    size_x, size_y, size_z = motion_ref.shape[1:]
    node_ref[...] = jnp.zeros_like(node_ref)
    wide_ref[...] = jnp.zeros_like(wide_ref)
    stiffness = stiff_ref[...].astype(F32)
    elem, owner = elem_ref[...], owner_ref[...]
    points = elem.shape[1]
    column = elem // size_z
    depth = elem - column * size_z
    index_ref[0:1, :] = slots_of(owner, hosts, capacity)[2]
    index_ref[1:2, :] = column
    index_ref[2:3, :] = depth
    index_ref[3:, :] = jnp.zeros((5, points), jnp.int32)
    depth_hot = jnp.where(iota((size_z, points), 0) == depth, 1.0, 0.0).astype(BF16)
    column_hot = jnp.where(iota((size_x * size_y, points), 0) == column, 1.0, 0.0).astype(BF16)
    listed = dot_t(column_hot, depth_hot)
    for i in range(size_x):
        for m in range(3):
            low, high = sides_of(first_ref, second_ref, m, i)
            node_ref[m, i, 0:1, :] = low
            node_ref[m, i, 1 : size_y + 1, :] = motion_ref[m, i]
            node_ref[m, i, size_y + 1 : size_y + 2, :] = high
        low, _ = sides_of(first_ref, second_ref, 3, i)
        wide_ref[i, 0:1, :] = low
        keep = 1.0 - listed[i * size_y : (i + 1) * size_y]
        wide_ref[i, 1 : size_y + 1, :] = stiffness[i] * keep
    for m in range(3):
        edge_ref[m] = node_ref[m, 0]
        edge_ref[3 + m] = node_ref[m, size_x - 1]
    edge_ref[6] = wide_ref[size_x - 1]
    strain = block_strains([node_ref[m] for m in range(3)])
    stress = elastic_of(strain, wide_ref[: size_x - 1])
    for c in range(6):
        stress_ref[c, 0] = jnp.zeros(stress_ref.shape[2:], F32)
        stress_ref[c, 1:size_x] = stress[c]
        stress_ref[c, size_x] = jnp.zeros(stress_ref.shape[2:], F32)
    force = assemble(
        [(stress_ref[c, :, 1 : size_y + 1, :], stress_ref[c, :, 0:size_y, :]) for c in range(6)]
    )
    for m in range(3):
        force_ref[m] = force[m]


def final_kernel(packed, hosts, capacity, answer_ref, *rest):
    if packed:
        faces_ref = None
    else:
        faces_ref, *rest = rest
    (
        elastic_ref,
        edge_ref,
        index_ref,
        force_ref,
        tangent_ref,
        result_ref,
        node_ref,
        wide_ref,
        stress_ref,
    ) = rest
    size_x, size_y, size_z = elastic_ref.shape[1:]
    slot, column, depth = index_ref[0:1, :], index_ref[1:2, :], index_ref[2:3, :]
    points = slot.shape[1]
    slot_total = hosts * capacity
    if packed:
        group_of = iota((8, 128), 1) // capacity
        per_tile = 128 // capacity
        groups = []
        for g in range(4):
            tiles = []
            for t in range(hosts // per_tile):
                tile = jnp.zeros((8, 128), F32)
                for n in range(per_tile):
                    piece = answer_ref[t * per_tile + n, 0:8, :]
                    shift = ((n - g) * capacity) % 128
                    if shift:
                        piece = pltpu.roll(piece, shift, 1)
                    tile = jnp.where(group_of == n, piece, tile)
                tiles.append(tile)
            groups.append(jnp.concatenate(tiles, axis=1))
        answer = jnp.concatenate(groups, axis=0)
    else:
        answer = answer_ref[...]
    slot_hot = jnp.where(iota((slot_total, points), 0) == slot, 1.0, 0.0).astype(BF16)
    parts = jnp.concatenate(pieces(answer, 3), axis=0)
    chosen = jnp.dot(parts, slot_hot, preferred_element_type=F32)
    result = chosen[:ROWS] + (chosen[ROWS : 2 * ROWS] + chosen[2 * ROWS :])
    result_ref[...] = result
    for i in range(6):
        for j in range(6):
            at = 6 + UPPER.index((min(i, j), max(i, j)))
            tangent_ref[6 * i + j : 6 * i + j + 1, :] = result_ref[at : at + 1, :]

    here = lax.axis_index("macro")
    inner = [here > 0, here < hosts - 1]
    from_chunk = [jnp.maximum(here - 1, 0), jnp.minimum(here + 1, hosts - 1)]

    def face(side, row, size):
        if packed:
            value = answer_ref[from_chunk[side], 8 + row : 8 + row + size, :]
        else:
            value = faces_ref[side, row : row + size, :]
        return jnp.where(inner[side], value, 0.0)

    node_ref[...] = jnp.zeros_like(node_ref)
    wide_ref[...] = jnp.zeros_like(wide_ref)
    for m in range(3):
        for side, at in ((0, 0), (1, 3)):
            node_ref[m, at, 0:1, :] = face(side, 32 + 2 * m, 1)
            node_ref[m, at, 1 : size_y + 1, :] = face(side, 8 * m, 8)
            node_ref[m, at, size_y + 1 : size_y + 2, :] = face(side, 33 + 2 * m, 1)
        node_ref[m, 1] = edge_ref[m]
        node_ref[m, 2] = edge_ref[3 + m]
    wide_ref[0, 0:1, :] = face(0, 38, 1)
    wide_ref[0, 1 : size_y + 1, :] = face(0, 24, 8)
    wide_ref[1] = edge_ref[6]
    lower, upper = [], []
    for m in range(3):
        four = corners(node_ref[m])
        lower.append([jnp.stack([value[0], value[2]]) for value in four])
        upper.append([jnp.stack([value[1], value[3]]) for value in four])
    edge = elastic_of(strains(lower, upper), wide_ref[...])
    rows = (size_x - 1) * size_y
    depth_hot = jnp.where(iota((size_z, points), 0) == depth, 1.0, 0.0).astype(BF16)
    column_hot = iota((rows, points), 0) == column
    stress_ref[:, 1:size_x, 0:1, :] = jnp.zeros((6, size_x - 1, 1, size_z), F32)
    for c in range(6):
        placed = jnp.where(column_hot, result[c : c + 1], 0.0)
        high, low = pieces(placed, 2)
        field = dot_t(high, depth_hot) + dot_t(low, depth_hot)
        stress_ref[c, 1:size_x, 1 : size_y + 1, :] = field.reshape(size_x - 1, size_y, size_z)
        stress_ref[c, 0] = edge[c][0]
        stress_ref[c, size_x] = edge[c][1]
    force = assemble(
        [(stress_ref[c, :, 1 : size_y + 1, :], stress_ref[c, :, 0:size_y, :]) for c in range(6)]
    )
    for m in range(3):
        force_ref[m] = elastic_ref[m] + force[m]


def shape_of(shape, dtype=F32):
    return jax.ShapeDtypeStruct(shape, dtype)


def call(kernel, name, out_shape, args, scratch=(), flops=10**8, raw=0):
    specs = whole(*args[: len(args) - raw]) + [pl.BlockSpec(memory_space=pl.ANY)] * raw
    return pl.pallas_call(
        kernel,
        grid=(1,),
        out_shape=out_shape,
        in_specs=specs,
        out_specs=whole(*out_shape),
        scratch_shapes=scratch,
        compiler_params=pltpu.CompilerParams(vmem_limit_bytes=24 * 2**20),
        cost_estimate=pl.CostEstimate(flops=flops, bytes_accessed=2**20, transcendentals=0),
        name=name,
    )(*args)


def on_device(
    motion,
    stiffness,
    point_elem,
    point_owner,
    point_pattern,
    history,
    basis,
    mode_map,
    weights,
    patterns,
):
    size_x, size_y, size_z = motion.shape[1:]
    points = point_elem.shape[0]
    hosts = lax.axis_size("macro")
    sides = lax.axis_size("micro")
    capacity = 2 * points // hosts
    slots = capacity * hosts
    modes = mode_map.shape[0]
    half = modes // 2
    hyper = weights.shape[0]
    lanes = 128
    direct = capacity % 16 == 0
    packed = capacity * 4 == lanes and slots % lanes == 0
    motion = in_hbm(motion)
    stiffness = in_hbm(stiffness)
    elem = in_hbm(point_elem.reshape(1, points))
    owner = in_hbm(point_owner.reshape(1, points))
    pattern = in_hbm(point_pattern.reshape(1, points))
    history = in_hbm(history)
    map_rows = in_hbm(mode_map.T)

    sent = (
        [shape_of((hosts, 2 * capacity + 8, half), BF16)]
        if direct
        else [shape_of((slots, modes), BF16), shape_of((hosts, modes), BF16)]
    )
    swap = shape_of((4, size_x, size_z))
    *payload, first, second, face = call(
        functools.partial(dispatch_kernel, hosts, capacity, direct),
        "dispatch",
        sent + [swap, swap, shape_of((8, size_y, size_z))],
        (motion, stiffness, elem, owner, pattern, history, map_rows),
    )

    if direct:
        received = lax.all_to_all(payload[0], "macro", 0, 0, tiled=True)
        groups, group = hosts, capacity
    else:
        rows, ids = payload
        joined = jnp.concatenate(
            [
                rows[:, :half].reshape(hosts, capacity, half),
                rows[:, half:].reshape(hosts, capacity, half),
                ids.reshape(hosts, 2, half),
            ],
            axis=1,
        )
        joined = lax.all_to_all(joined, "macro", 0, 0, tiled=True)
        ids = jnp.sum(joined[:, 2 * capacity :].astype(F32), axis=0).astype(BF16)
        received = jnp.concatenate(
            [
                joined[:, :capacity].reshape(1, slots, half),
                joined[:, capacity : 2 * capacity].reshape(1, slots, half),
                jnp.pad(ids, ((0, 6), (0, 0)))[None],
            ],
            axis=1,
        )
        groups, group = 1, slots

    def swapped(value, start):
        pairs = [(i, i + 1) for i in range(start, sides - 1, 2)]
        return lax.ppermute(value, "micro", pairs + [(b, a) for a, b in pairs])

    first, second = swapped(first, 0), swapped(second, 1)

    rows = in_hbm(basis.reshape(6, hyper, modes))
    count = hyper // lanes
    table, const, column, bits = call(
        table_kernel,
        "tables",
        [
            shape_of((96, hyper), BF16),
            shape_of((48, lanes)),
            shape_of((hyper, lanes)),
            shape_of((hyper, patterns.shape[0]), BF16),
        ],
        (map_rows, in_hbm(weights.reshape(count, lanes)), in_hbm(patterns.T), rows),
        [VMEM((count, 6, lanes, modes), BF16), pltpu.SemaphoreType.DMA((count,))],
        raw=1,
    )

    answer = call(
        functools.partial(micro_kernel, packed, hosts, group),
        "micro_response",
        [shape_of((hosts, 48, lanes))]
        if packed
        else [shape_of((ROWS, slots)), shape_of((2, 40, lanes))],
        (
            received,
            first,
            second,
            face,
            const,
            rows,
            bits,
            column,
            table,
        ),
        [
            VMEM((slots, modes), BF16),
            VMEM((patterns.shape[0], slots), BF16),
            VMEM((count, 6, lanes, modes), BF16),
            VMEM(bits.shape, BF16),
            VMEM(column.shape, F32),
            VMEM(table.shape, BF16),
            VMEM((6, lanes, slots), F32),
            VMEM((6, lanes, slots), F32),
            VMEM((lanes, slots), BF16),
            VMEM((lanes, slots), BF16),
            VMEM((7, 8, slots), F32),
            VMEM((48, slots), F32),
            VMEM((ROWS, slots), F32),
            pltpu.SemaphoreType.DMA((count + 3,)),
        ],
        raw=4,
    )

    if packed:
        answered = [lax.all_to_all(answer[0], "macro", 0, 0, tiled=True)]
    else:
        result, faces = answer
        here = lax.axis_index("macro")
        order = jnp.arange(hosts)[:, None, None]
        flat = result.reshape(ROWS, hosts, capacity).transpose(1, 0, 2).reshape(hosts, -1)
        tiles = pl.cdiv(flat.shape[1], lanes)
        flat = jnp.pad(flat, ((0, 0), (0, tiles * lanes - flat.shape[1])))
        joined = jnp.concatenate(
            [flat.reshape(hosts, tiles, lanes), jnp.where(order > here, faces[0], faces[1])], axis=1
        )
        joined = lax.all_to_all(joined, "macro", 0, 0, tiled=True)
        flat = joined[:, :tiles].reshape(hosts, -1)[:, : ROWS * capacity]
        result = flat.reshape(hosts, ROWS, capacity).transpose(1, 0, 2).reshape(ROWS, slots)
        low = lax.dynamic_index_in_dim(joined, jnp.maximum(here - 1, 0), 0, False)
        high = lax.dynamic_index_in_dim(joined, jnp.minimum(here + 1, hosts - 1), 0, False)
        answered = [result, jnp.stack([low[tiles:], high[tiles:]])]

    elastic = call(
        functools.partial(elastic_kernel, hosts, capacity),
        "elastic_forces",
        [shape_of(motion.shape), shape_of((7, 16, size_z)), shape_of((8, points), jnp.int32)],
        (motion, stiffness, elem, owner, first, second),
        [
            VMEM((3, size_x, 16, size_z), F32),
            VMEM((size_x, 16, size_z), F32),
            VMEM((6, size_x + 1, 16, size_z), F32),
        ],
    )

    force, tangent = call(
        functools.partial(final_kernel, packed, hosts, capacity),
        "final_forces",
        [shape_of(motion.shape), shape_of((36, points))],
        (*answered, *elastic),
        [
            VMEM((ROWS, points), F32),
            VMEM((3, 4, 16, size_z), F32),
            VMEM((2, 16, size_z), F32),
            VMEM((6, size_x + 1, 16, size_z), F32),
        ],
    )
    return (force, tangent)


def solution(mesh):
    return jax.shard_map(
        on_device,
        mesh=mesh,
        in_specs=(
            P(None, "macro", "micro", None),
            P("macro", "micro", None),
            P(("macro", "micro")),
            P(("macro", "micro")),
            P(("macro", "micro")),
            P(None, ("macro", "micro")),
            P("macro", None, None),
            P(),
            P(),
            P(),
        ),
        out_specs=(P(None, "macro", "micro", None), P(None, ("macro", "micro"))),
        check_vma=False,
    )
```

time: 53 us -> 37.5 us (0.71)
  the two profiles are of different devices: /device:TPU:6 before, /device:TPU:1 now
where the time goes in v2:
time: 37.5 us; the launch traced here: 37 us
  starting transfers between devices  16.1 us (43%)
  Pallas kernels  14.7 us (39%)
  waiting for transfers between devices  5.6 us (15%)
  between operations  0.69 us (2%)
    pallas_call x5, Pallas kernels, call(): pl.pallas_call(kernel, grid=(1,), out_shape=out_shape, in_specs=specs, ou...  14.7 us
    all_to_all x1, starting transfers between devices, on_device(): received = lax.all_to_all(payload[0], 'macro', 0, 0, tiled=True)  6.39 us
    all_to_all x1, starting transfers between devices, on_device(): answered = [lax.all_to_all(answer[0], 'macro', 0, 0, tiled=True)]  5.71 us
    all_to_all x1, waiting for transfers between devices, on_device(): answered = [lax.all_to_all(answer[0], 'macro', 0, 0, tiled=True)]  5.59 us
    ppermute x2, starting transfers between devices, swapped(): return lax.ppermute(value, 'micro', pairs + [(b, a) for a, b in pairs])  3.97 us
  transfers between devices with their start and end apart: 4, of which 1 were waited for; matrix products, arithmetic and copies ran while one was open for 0% of the time, Pallas kernels for 14%

profile of v2, /device:TPU:1, one launch (start us, length us, event | category | flops | bytes accessed | tf_op | source)
XLA Modules:
  0.0 37.0 jit_solution(6600307970406591118)
XLA Ops:
  0.6 2.3 %dispatch.1 = (bf16[8,72,128]{2,1,0:T(8,128)(2,1)}, f32[4,8,128]{2,1,0:T(8,128)S(1)}, f32[4,8,128]{2,1,0:T(8,128)S(1)}, f32[8,8,128]{2,1,0:T(8,128)S(1)}) custom-call(f32[3,8,8,128]{3,2,1,0:T(8,128)} %motion_ref.3, bf16[8,8,128]{2,1,0:T(8,128)(2,1)} %stiff_ref.3, s32[1,128]{1,0:T(1,128)} %bitcast.14, s32[1,128]{1,0:T(1,128)} %bitcast.16, s32[1,128]{1,0:T(1,128)} %bitcast.13, ...), custom_call_target="tpu_custom_call" | custom-call | flops 100000000 | bytes 1048576 | tf_op jit(solution)/shard_map/dispatch/pallas_call | solution.py:629
  2.9 6.4 %all-to-all-start = ((bf16[8,72,128]{2,1,0:T(8,128)(2,1)}), bf16[8,72,128]{2,1,0:T(8,128)(2,1)S(1)}, u32[]{:S(2)}, u32[]{:S(2)}) async-start(bf16[8,72,128]{2,1,0:T(8,128)(2,1)} %get-tuple-element.13), calls=%async_computation | async-start | bytes 294912 | tf_op jit(solution)/shard_map/all_to_all | solution.py:688
  9.3 1.0 %collective-permute-start = (f32[4,8,128]{2,1,0:T(8,128)S(1)}, f32[4,8,128]{2,1,0:T(8,128)S(1)}, u32[]{:S(2)}, u32[]{:S(2)}) collective-permute-start(f32[4,8,128]{2,1,0:T(8,128)S(1)} %get-tuple-element.14), channel_id=1, source_target_pairs={{0,1},{2,3},{1,0},{3,2},{4,5},{6,7},{5,4},{7,6},{8,9},{10,11},{9,8... | collective-permute-start | bytes 49160 | tf_op jit(solution)/shard_map/ppermute | solution.py:714
  10.2 3.0 %collective-permute-start.1 = (f32[4,8,128]{2,1,0:T(8,128)S(1)}, f32[4,8,128]{2,1,0:T(8,128)S(1)}, u32[]{:S(2)}, u32[]{:S(2)}) collective-permute-start(f32[4,8,128]{2,1,0:T(8,128)S(1)} %get-tuple-element.15), channel_id=1, source_target_pairs={{1,2},{2,1},{5,6},{6,5},{9,10},{10,9},{13,14},{14,13},{17,18},{18,... | collective-permute-start | bytes 49160 | tf_op jit(solution)/shard_map/ppermute | solution.py:714
  13.3 3.8 %tables.1 = (bf16[96,1024]{1,0:T(8,128)(2,1)S(1)}, f32[48,128]{1,0:T(8,128)S(1)}, f32[1024,128]{1,0:T(8,128)S(1)}, bf16[1024,64]{1,0:T(8,128)(2,1)S(1)}) custom-call(bf16[6,256]{1,0:T(8,128)(2,1)} %bitcast.11, f32[8,128]{1,0:T(8,128)} %bitcast.12, s32[35,64]{1,0:T(8,128)} %bitcast.9, bf16[6,1024,256]{2,1,0:T(8,128)(2,1)} %bitcast.7), custom_call_target="tpu_custom_call" | custom-call | flops 100000000 | bytes 1048576 | tf_op jit(solution)/shard_map/tables/pallas_call | solution.py:629
  17.0 0.0 collective-permute-done.first_ref
  17.0 0.0 collective-permute-done.1.second_ref
  17.0 0.0 all-to-all-done.received_ref
  17.1 6.0 %micro_response.1 = f32[8,48,128]{2,1,0:T(8,128)} custom-call(bf16[8,72,128]{2,1,0:T(8,128)(2,1)S(1)} %all-to-all-done.received_ref, f32[4,8,128]{2,1,0:T(8,128)S(1)} %collective-permute-done.first_ref, f32[4,8,128]{2,1,0:T(8,128)S(1)} %collective-permute-done.1.second_ref, f32[8,8,128]{2,1,0:T(8,128)S(1)} %get-tuple-element.16.face_ref, ...), custom_call_target="tpu_custom_call" | custom-call | flops 100000000 | bytes 1048576 | tf_op jit(solution)/shard_map/micro_response/pallas_call | solution.py:629
  23.1 5.7 %all-to-all-start.1 = ((f32[8,48,128]{2,1,0:T(8,128)}), f32[8,48,128]{2,1,0:T(8,128)S(1)}, u32[]{:S(2)}, u32[]{:S(2)}) async-start(f32[8,48,128]{2,1,0:T(8,128)} %micro_response.1), calls=%async_computation.1 | async-start | bytes 393216 | tf_op jit(solution)/shard_map/all_to_all | solution.py:771
  28.8 1.3 %elastic_forces.1 = (f32[3,8,8,128]{3,2,1,0:T(8,128)S(1)}, f32[7,16,128]{2,1,0:T(8,128)S(1)}, s32[8,128]{1,0:T(8,128)S(1)}) custom-call(f32[3,8,8,128]{3,2,1,0:T(8,128)} %motion_ref.3, bf16[8,8,128]{2,1,0:T(8,128)(2,1)} %stiff_ref.3, s32[1,128]{1,0:T(1,128)} %bitcast.15, s32[1,128]{1,0:T(1,128)} %bitcast.17, ...), custom_call_target="tpu_custom_call" | custom-call | flops 100000000 | bytes 1048576 | tf_op jit(solution)/shard_map/elastic_forces/pallas_call | solution.py:629
  30.1 5.6 %all-to-all-done.1.answer_ref = f32[8,48,128]{2,1,0:T(8,128)S(1)} async-done(((f32[8,48,128]{2,1,0:T(8,128)}), f32[8,48,128]{2,1,0:T(8,128)S(1)}, u32[]{:S(2)}, u32[]{:S(2)}) %all-to-all-start.1) | async-done | bytes 196640 | tf_op jit(solution)/shard_map/all_to_all | solution.py:771
  35.7 1.3 %final_forces.1 = (f32[3,8,8,128]{3,2,1,0:T(8,128)}, f32[36,128]{1,0:T(8,128)}) custom-call(f32[8,48,128]{2,1,0:T(8,128)S(1)} %all-to-all-done.1.answer_ref, f32[3,8,8,128]{3,2,1,0:T(8,128)S(1)} %get-tuple-element.21.rest_0_, f32[7,16,128]{2,1,0:T(8,128)S(1)} %get-tuple-element.22.rest_1_, s32[8,128]{1,0:T(8,128)S(1)} %get-tuple-element.23.rest_2_), custom_call_target="tpu_custom_call" | custom-call | flops 100000000 | bytes 1048576 | tf_op jit(solution)/shard_map/final_forces/pallas_call | solution.py:629
Async XLA Ops:
  2.9 14.1 %all-to-all-start = ((bf16[8,72,128]{2,1,0:T(8,128)(2,1)}), bf16[8,72,128]{2,1,0:T(8,128)(2,1)S(1)}, u32[]{:S(2)}, u32[]{:S(2)}) async-start(bf16[8,72,128]{2,1,0:T(8,128)(2,1)} %get-tuple-element.13), calls=%async_computation | async-start | bytes 294912 | tf_op jit(solution)/shard_map/all_to_all | solution.py:688
  9.3 7.7 %collective-permute-start = (f32[4,8,128]{2,1,0:T(8,128)S(1)}, f32[4,8,128]{2,1,0:T(8,128)S(1)}, u32[]{:S(2)}, u32[]{:S(2)}) collective-permute-start(f32[4,8,128]{2,1,0:T(8,128)S(1)} %get-tuple-element.14), channel_id=1, source_target_pairs={{0,1},{2,3},{1,0},{3,2},{4,5},{6,7},{5,4},{7,6},{8,9},{10,11},{9,8... | collective-permute-start | bytes 49160 | tf_op jit(solution)/shard_map/ppermute | solution.py:714
  10.2 6.8 %collective-permute-start.1 = (f32[4,8,128]{2,1,0:T(8,128)S(1)}, f32[4,8,128]{2,1,0:T(8,128)S(1)}, u32[]{:S(2)}, u32[]{:S(2)}) collective-permute-start(f32[4,8,128]{2,1,0:T(8,128)S(1)} %get-tuple-element.15), channel_id=1, source_target_pairs={{1,2},{2,1},{5,6},{6,5},{9,10},{10,9},{13,14},{14,13},{17,18},{18,... | collective-permute-start | bytes 49160 | tf_op jit(solution)/shard_map/ppermute | solution.py:714
  23.1 12.7 %all-to-all-start.1 = ((f32[8,48,128]{2,1,0:T(8,128)}), f32[8,48,128]{2,1,0:T(8,128)S(1)}, u32[]{:S(2)}, u32[]{:S(2)}) async-start(f32[8,48,128]{2,1,0:T(8,128)} %micro_response.1), calls=%async_computation.1 | async-start | bytes 393216 | tf_op jit(solution)/shard_map/all_to_all | solution.py:771

commit v3 on v2

--- a/solution.py
+++ b/solution.py
@@ -168,7 +168,7 @@
         payload_ref[...] = sent
         rest[0][...] = ids.astype(BF16)
         rest = rest[1:]
-    first_ref, second_ref, face_ref = rest
+    first_ref, second_ref, x_first_ref, x_second_ref = rest
     stiffness = stiff_ref[...].astype(F32)
     even = lax.rem(lax.axis_index("micro"), 2) == 0
     for i in range(size_x):
@@ -179,11 +179,14 @@
                 up = down = stiffness[i, size_y - 1 : size_y, :]
             first_ref[m, i : i + 1, :] = jnp.where(even, up, down)
             second_ref[m, i : i + 1, :] = jnp.where(even, down, up)
-    for m in range(3):
-        face_ref[m] = motion_ref[m, size_x - 1]
-        face_ref[4 + m] = motion_ref[m, 0]
-    face_ref[3] = stiffness[size_x - 1]
-    face_ref[7] = jnp.zeros_like(face_ref[7])
+    even = lax.rem(lax.axis_index("macro"), 2) == 0
+    for m in range(4):
+        if m < 3:
+            up, down = motion_ref[m, size_x - 1], motion_ref[m, 0]
+        else:
+            up = down = stiffness[size_x - 1]
+        x_first_ref[m] = jnp.where(even, up, down)
+        x_second_ref[m] = jnp.where(even, down, up)
 
 
 def table_kernel(
@@ -196,62 +199,70 @@
     column_ref,
     bits_ref,
     blocks_ref,
+    others_ref,
     sems,
 ):
-    hyper = basis_ref.shape[1]
+    hyper = weights_ref.shape[1]
     lanes = 128
-    count = hyper // lanes
-    copies = [
-        pltpu.make_async_copy(
-            basis_ref.at[:, pl.ds(b * lanes, lanes), :], blocks_ref.at[b], sems.at[b]
+    kept, _, wide, modes = blocks_ref.shape
+    count = hyper // wide
+    copies = []
+    for n in range(count):
+        target = blocks_ref.at[n] if n < kept else others_ref.at[n - kept]
+        copies.append(
+            pltpu.make_async_copy(basis_ref.at[:, pl.ds(n * wide, wide), :], target, sems.at[n])
         )
-        for b in range(count)
-    ]
-    for copy in copies:
-        copy.start()
+        copies[n].start()
+    weights = weights_ref[...]
+    split = [piece.astype(F32) for piece in pieces(weights, 3)]
+    row = iota((8, hyper), 0)
+    stack = jnp.where(
+        row == 0, split[0], jnp.where(row == 1, split[1], jnp.where(row == 2, split[2], 0.0))
+    )
+    column_ref[...] = lax.dot_general(
+        stack.astype(BF16),
+        jnp.ones((8, lanes), BF16),
+        (((0,), (0,)), ((), ())),
+        preferred_element_type=F32,
+    )
+    patterns = patterns_ref[...]
+    words, total = patterns.shape
+    parts = [((patterns >> (8 * k)) & 255).astype(F32) for k in range(4)]
+    spare = -4 * words % 8
+    parts = jnp.concatenate(parts + [jnp.zeros((spare, total), F32)] * (spare > 0), axis=0)
+    place = iota((1, 4 * words + spare), 1)
+    part = jnp.where(place >= words, 1, 0) + jnp.where(place >= 2 * words, 1, 0)
+    part = part + jnp.where(place >= 3 * words, 1, 0)
+    start = 30 * (place - words * part) + 8 * part
+    size = jnp.where(part == 3, 6, 8)
+    after = iota((hyper, 4 * words + spare), 0) - start
+    byte_hot = jnp.where((after >= 0) & (after < size), 1.0, 0.0).astype(BF16)
+    value = jnp.dot(byte_hot, parts.astype(BF16), preferred_element_type=F32).astype(jnp.int32)
+    index = iota((hyper, total), 0)
+    offset = index - 30 * ((index * 2185) >> 16)
+    bits_ref[...] = ((value >> (offset & 7)) & 1).astype(F32).astype(BF16)
+
     modes_map = map_ref[...]
     modes_map = jnp.concatenate(
-        [modes_map.astype(F32), jnp.zeros((2, modes_map.shape[1]), F32)], axis=0
+        [modes_map.astype(F32), jnp.zeros((2, modes), F32)], axis=0
     ).astype(BF16)
-    sums = jnp.zeros((48, lanes), F32)
-    patterns = patterns_ref[...]
-    parts = [((patterns >> (8 * k)) & 255).astype(F32).astype(BF16) for k in range(4)]
-    words, total = patterns.shape
-    for b in range(count):
-        part = pl.ds(b * lanes, lanes)
-        weight = weights_ref[b : b + 1, :]
-        square = (lanes, lanes)
-        diagonal = jnp.where(iota(square, 0) == iota(square, 1), weight, 0.0)
-        column_ref[part, :] = jnp.broadcast_to(jnp.sum(diagonal, axis=1, keepdims=True), square)
-        start = 30 * iota((lanes, words), 1)
-        index = iota((lanes, words), 0) + b * lanes
-        word_hot = jnp.where((index >= start) & (index < start + 30), 1.0, 0.0).astype(BF16)
-        bytes_of = [
-            jnp.dot(word_hot, part_k, preferred_element_type=F32) for part_k in parts
-        ]
-        row = iota((lanes, total), 0) + b * lanes
-        offset = row - 30 * ((row * 2185) >> 16)
-        value = jnp.where(
-            offset < 16,
-            jnp.where(offset < 8, bytes_of[0], bytes_of[1]),
-            jnp.where(offset < 24, bytes_of[2], bytes_of[3]),
-        ).astype(jnp.int32)
-        bits_ref[part, :] = ((value >> (offset & 7)) & 1).astype(F32).astype(BF16)
-    for b in range(count):
-        part = pl.ds(b * lanes, lanes)
-        copies[b].wait()
-        local = [dot_t(modes_map, blocks_ref[b, c]) for c in range(6)]
+    sums = jnp.zeros((48, wide), F32)
+    for n in range(count):
+        copies[n].wait()
+        source = blocks_ref.at[n] if n < kept else others_ref.at[n - kept]
+        part = slice(n * wide, (n + 1) * wide)
+        local = [dot_t(modes_map, source[c]) for c in range(6)]
         trace = local[0] + local[1] + local[2]
         third = trace / 3.0
         shaped = [local[c] - third for c in range(3)] + [0.5 * local[c] for c in range(3, 6)]
-        weight = weights_ref[b : b + 1, :]
+        weight = weights[:, part]
+        shaped = [weight * value for value in shaped]
         weighted_trace = weight * trace
         blocks, adds = [], []
         for i in range(6):
             entry = local[0][i : i + 1] * shaped[0]
             for c in range(1, 6):
                 entry = entry + local[c][i : i + 1] * shaped[c]
-            entry = entry * weight
             blocks.append(entry)
             adds.append(entry + trace[i : i + 1] * weighted_trace)
         sums = sums + jnp.concatenate(adds, axis=0)
@@ -261,9 +272,10 @@
     const_ref[...] = jnp.broadcast_to(jnp.sum(sums, axis=1, keepdims=True), const_ref.shape)
 
 
-def sides_of(first_ref, second_ref, m, at):
-    even = lax.rem(lax.axis_index("micro"), 2) == 0
-    first, second = first_ref[m, at : at + 1, :], second_ref[m, at : at + 1, :]
+def sides_of(first_ref, second_ref, axis, m, at=None):
+    even = lax.rem(lax.axis_index(axis), 2) == 0
+    rows = slice(None) if at is None else slice(at, at + 1)
+    first, second = first_ref[m, rows, :], second_ref[m, rows, :]
     return jnp.where(even, second, first), jnp.where(even, first, second)
 
 
@@ -274,55 +286,47 @@
     received_ref,
     first_ref,
     second_ref,
-    face_ref,
     const_ref,
-    basis_ref,
     bits_ref,
     column_ref,
     table_ref,
+    blocks_ref,
+    basis_ref,
     answer_ref,
     *rest,
 ):
     if packed:
-        faces_ref = None
+        corners_ref = None
     else:
-        faces_ref, *rest = rest
+        corners_ref, *rest = rest
     (
         state_ref,
         hot_ref,
-        basis_buf,
-        bits_buf,
-        column_buf,
-        table_buf,
-        even_ref,
-        odd_ref,
-        high_ref,
-        low_ref,
-        stress_ref,
-        tangent_ref,
+        others_ref,
+        strain_even,
+        strain_odd,
+        high_even,
+        high_odd,
+        low_even,
+        low_odd,
         result_ref,
         sems,
     ) = rest
+    strain_refs = (strain_even, strain_odd)
+    high_refs = (high_even, high_odd)
+    low_refs = (low_even, low_odd)
     groups = received_ref.shape[0]
     slots = groups * capacity
-    count, _, block, modes = basis_buf.shape
+    kept, _, block, modes = blocks_ref.shape
     half = modes // 2
-
-    def basis_copy(n):
-        return pltpu.make_async_copy(
-            basis_ref.at[:, pl.ds(n * block, block), :], basis_buf.at[n], sems.at[n]
+    count = kept + others_ref.shape[0]
+    copies = []
+    for n in range(count - kept):
+        part = pl.ds((kept + n) * block, block)
+        copies.append(
+            pltpu.make_async_copy(basis_ref.at[:, part, :], others_ref.at[n], sems.at[n])
         )
-
-    others = [
-        pltpu.make_async_copy(bits_ref, bits_buf, sems.at[count]),
-        pltpu.make_async_copy(column_ref, column_buf, sems.at[count + 1]),
-        pltpu.make_async_copy(table_ref, table_buf, sems.at[count + 2]),
-    ]
-    basis_copy(0).start()
-    for copy in others:
-        copy.start()
-    for n in range(1, count):
-        basis_copy(n).start()
+        copies[n].start()
 
     ids = jnp.zeros((8, half), F32)
     for h in range(groups):
@@ -332,18 +336,26 @@
         ids = ids + received_ref[h, 2 * capacity :, :].astype(F32)
     ids = jnp.concatenate([ids[0:1], ids[1:2]], axis=1).astype(jnp.int32)
     hot_ref[...] = jnp.where(iota(hot_ref.shape, 0) == ids, 1.0, 0.0).astype(BF16)
-    stress_ref[...] = jnp.zeros_like(stress_ref)
-    tangent_ref[...] = jnp.zeros_like(tangent_ref)
-
-    def rows_of(n, target):
-        rows = basis_buf[n].reshape(6 * block, modes)
-        target[...] = dot_t(rows, state_ref[...]).reshape(6, block, slots)
-
-    def respond(n, strain_ref):
-        part = pl.ds(pl.multiple_of(n * block, block), block)
-        flags = jnp.dot(bits_buf[part, :], hot_ref[...], preferred_element_type=F32)
+
+    def rows_of(n):
+        if n >= kept:
+            copies[n - kept].wait()
+        source = blocks_ref.at[n] if n < kept else others_ref.at[n - kept]
+        rows = source[...].reshape(6 * block, modes)
+        strain_refs[n % 2][...] = dot_t(rows, state_ref[...]).reshape(6, block, slots)
+
+    def tangent_of(n):
+        table = table_ref[:, n * block : (n + 1) * block]
+        one = jnp.dot(table, high_refs[n % 2][...], preferred_element_type=F32)
+        two = jnp.dot(table[:48], low_refs[n % 2][...], preferred_element_type=F32)
+        return one[:48] + (one[48:] + two)
+
+    def respond(n, sums):
+        sums = list(sums)
+        strain_ref, high_ref, low_ref = (refs[n % 2] for refs in (strain_refs, high_refs, low_refs))
+        part = pl.ds(n * block, block)
+        flags = jnp.dot(bits_ref[part, :], hot_ref[...], preferred_element_type=F32)
         strip = 16
-        sums = [jnp.zeros((8, slots), F32)] * 7
         for r in range(0, block, strip):
             at = pl.ds(r, strip)
             e = [strain_ref[c, at, :] for c in range(6)]
@@ -358,48 +370,33 @@
             high = change.astype(BF16)
             high_ref[at, :] = high
             low_ref[at, :] = (change - high.astype(F32)).astype(BF16)
-            column = column_buf[pl.ds(pl.multiple_of(n * block, block) + r, strip), :]
+            column = column_ref[pl.ds(n * block + r, strip), :]
             weight = jnp.concatenate([column] * (slots // column.shape[1]), axis=1)
             scaled = weight + weight * change
             terms = [scaled * d[c] for c in range(3)] + [scaled * e[c] for c in range(3, 6)]
             terms.append(weight * volume)
             for k in range(7):
                 sums[k] = sums[k] + (terms[k][:8] + terms[k][8:])
-        for k in range(7):
-            stress_ref[k] += sums[k]
-        table = table_buf[:, part]
-        one = jnp.dot(table, high_ref[...], preferred_element_type=F32)
-        two = jnp.dot(table[:48], low_ref[...], preferred_element_type=F32)
-        tangent_ref[...] += one[:48] + (one[48:] + two)
-
-    basis_copy(0).wait()
-    rows_of(0, even_ref)
-    for copy in others:
-        copy.wait()
-
-    def pair(i, carry):
-        n = 2 * i
-        basis_copy(n + 1).wait()
-        rows_of(n + 1, odd_ref)
-        respond(n, even_ref)
-
-        @pl.when(n + 2 < count)
-        def _():
-            basis_copy(n + 2).wait()
-
-        rows_of(jnp.minimum(n + 2, count - 1), even_ref)
-        respond(n + 1, odd_ref)
-        return carry
-
-    lax.fori_loop(0, count // 2, pair, 0)
-
-    volume = jnp.sum(stress_ref[6], axis=0, keepdims=True)
+        return sums
+
+    sums = [jnp.zeros((8, slots), F32)] * 7
+    tangent = jnp.zeros((48, slots), F32)
+    rows_of(0)
+    for n in range(count):
+        if n > 0:
+            tangent = tangent + tangent_of(n - 1)
+        sums = respond(n, sums)
+        if n + 1 < count:
+            rows_of(n + 1)
+    tangent = tangent + tangent_of(count - 1)
+
+    volume = jnp.sum(sums[6], axis=0, keepdims=True)
     for c in range(6):
-        total = jnp.sum(stress_ref[c], axis=0, keepdims=True)
+        total = jnp.sum(sums[c], axis=0, keepdims=True)
         result_ref[c : c + 1, :] = total + volume if c < 3 else 0.5 * total
     const = const_ref[...]
     const = jnp.concatenate([const] * (slots // const.shape[1]), axis=1)
-    tangent = tangent_ref[...] + const
+    tangent = tangent + const
     at = 6
     for i in range(6):
         result_ref[at : at + 6 - i, :] = tangent[8 * i + i : 8 * i + 6]
@@ -408,15 +405,13 @@
 
     last = first_ref.shape[1] - 1
 
-    def faces(write):
+    def corner_rows(write):
         for m in range(4):
-            write(0, 8 * m, 8, face_ref[m])
-            write(1, 8 * m, 8, face_ref[4 + m])
-            up = sides_of(first_ref, second_ref, m, last)
-            down = sides_of(first_ref, second_ref, m, 0)
+            up = sides_of(first_ref, second_ref, "micro", m, last)
+            down = sides_of(first_ref, second_ref, "micro", m, 0)
             for n in range(2):
-                write(0, 32 + 2 * m + n, 1, up[n])
-                write(1, 32 + 2 * m + n, 1, down[n])
+                write(0, 2 * m + n, up[n])
+                write(1, 2 * m + n, down[n])
 
     if packed:
         here = lax.axis_index("macro")
@@ -433,15 +428,15 @@
             answer_ref[h, 0:8, :] = chunk
         chunks = [jnp.minimum(here + 1, hosts - 1), jnp.maximum(here - 1, 0)]
 
-        def write(side, row, size, value):
-            answer_ref[chunks[side], 8 + row : 8 + row + size, :] = value
+        def write(side, row, value):
+            answer_ref[chunks[side], 8 + row : 9 + row, :] = value
     else:
         answer_ref[...] = result_ref[...]
 
-        def write(side, row, size, value):
-            faces_ref[side, row : row + size, :] = value
-
-    faces(write)
+        def write(side, row, value):
+            corners_ref[side, row : row + 1, :] = value
+
+    corner_rows(write)
 
 
 def assemble(stress):
@@ -499,11 +494,11 @@
     listed = dot_t(column_hot, depth_hot)
     for i in range(size_x):
         for m in range(3):
-            low, high = sides_of(first_ref, second_ref, m, i)
+            low, high = sides_of(first_ref, second_ref, "micro", m, i)
             node_ref[m, i, 0:1, :] = low
             node_ref[m, i, 1 : size_y + 1, :] = motion_ref[m, i]
             node_ref[m, i, size_y + 1 : size_y + 2, :] = high
-        low, _ = sides_of(first_ref, second_ref, 3, i)
+        low, _ = sides_of(first_ref, second_ref, "micro", 3, i)
         wide_ref[i, 0:1, :] = low
         keep = 1.0 - listed[i * size_y : (i + 1) * size_y]
         wide_ref[i, 1 : size_y + 1, :] = stiffness[i] * keep
@@ -526,10 +521,12 @@
 
 def final_kernel(packed, hosts, capacity, answer_ref, *rest):
     if packed:
-        faces_ref = None
+        corners_ref = None
     else:
-        faces_ref, *rest = rest
+        corners_ref, *rest = rest
     (
+        second_ref,
+        first_ref,
         elastic_ref,
         edge_ref,
         index_ref,
@@ -577,24 +574,25 @@
     inner = [here > 0, here < hosts - 1]
     from_chunk = [jnp.maximum(here - 1, 0), jnp.minimum(here + 1, hosts - 1)]
 
-    def face(side, row, size):
+    def corner(side, row):
         if packed:
-            value = answer_ref[from_chunk[side], 8 + row : 8 + row + size, :]
+            value = answer_ref[from_chunk[side], 8 + row : 9 + row, :]
         else:
-            value = faces_ref[side, row : row + size, :]
+            value = corners_ref[side, row : row + 1, :]
         return jnp.where(inner[side], value, 0.0)
 
     node_ref[...] = jnp.zeros_like(node_ref)
     wide_ref[...] = jnp.zeros_like(wide_ref)
     for m in range(3):
+        faces = sides_of(first_ref, second_ref, "macro", m)
         for side, at in ((0, 0), (1, 3)):
-            node_ref[m, at, 0:1, :] = face(side, 32 + 2 * m, 1)
-            node_ref[m, at, 1 : size_y + 1, :] = face(side, 8 * m, 8)
-            node_ref[m, at, size_y + 1 : size_y + 2, :] = face(side, 33 + 2 * m, 1)
+            node_ref[m, at, 0:1, :] = corner(side, 2 * m)
+            node_ref[m, at, 1 : size_y + 1, :] = faces[side]
+            node_ref[m, at, size_y + 1 : size_y + 2, :] = corner(side, 2 * m + 1)
         node_ref[m, 1] = edge_ref[m]
         node_ref[m, 2] = edge_ref[3 + m]
-    wide_ref[0, 0:1, :] = face(0, 38, 1)
-    wide_ref[0, 1 : size_y + 1, :] = face(0, 24, 8)
+    wide_ref[0, 0:1, :] = corner(0, 6)
+    wide_ref[0, 1 : size_y + 1, :] = sides_of(first_ref, second_ref, "macro", 3)[0]
     wide_ref[1] = edge_ref[6]
     lower, upper = [], []
     for m in range(3):
@@ -654,7 +652,6 @@
     size_x, size_y, size_z = motion.shape[1:]
     points = point_elem.shape[0]
     hosts = lax.axis_size("macro")
-    sides = lax.axis_size("micro")
     capacity = 2 * points // hosts
     slots = capacity * hosts
     modes = mode_map.shape[0]
@@ -676,11 +673,11 @@
         if direct
         else [shape_of((slots, modes), BF16), shape_of((hosts, modes), BF16)]
     )
-    swap = shape_of((4, size_x, size_z))
-    *payload, first, second, face = call(
+    swap, x_swap = shape_of((4, size_x, size_z)), shape_of((4, size_y, size_z))
+    *payload, first, second, x_first, x_second = call(
         functools.partial(dispatch_kernel, hosts, capacity, direct),
         "dispatch",
-        sent + [swap, swap, shape_of((8, size_y, size_z))],
+        sent + [swap, swap, x_swap, x_swap],
         (motion, stiffness, elem, owner, pattern, history, map_rows),
     )
 
@@ -709,15 +706,16 @@
         )
         groups, group = 1, slots
 
-    def swapped(value, start):
-        pairs = [(i, i + 1) for i in range(start, sides - 1, 2)]
-        return lax.ppermute(value, "micro", pairs + [(b, a) for a, b in pairs])
-
-    first, second = swapped(first, 0), swapped(second, 1)
+    def swapped(value, axis, start):
+        pairs = [(i, i + 1) for i in range(start, lax.axis_size(axis) - 1, 2)]
+        return lax.ppermute(value, axis, pairs + [(b, a) for a, b in pairs])
+
+    first, second = swapped(first, "micro", 0), swapped(second, "micro", 1)
+    x_first, x_second = swapped(x_first, "macro", 0), swapped(x_second, "macro", 1)
 
     rows = in_hbm(basis.reshape(6, hyper, modes))
-    count = hyper // lanes
-    table, const, column, bits = call(
+    wide, kept = 256, 2
+    table, const, column, bits, blocks = call(
         table_kernel,
         "tables",
         [
@@ -725,59 +723,56 @@
             shape_of((48, lanes)),
             shape_of((hyper, lanes)),
             shape_of((hyper, patterns.shape[0]), BF16),
+            shape_of((kept, 6, wide, modes), BF16),
         ],
-        (map_rows, in_hbm(weights.reshape(count, lanes)), in_hbm(patterns.T), rows),
-        [VMEM((count, 6, lanes, modes), BF16), pltpu.SemaphoreType.DMA((count,))],
+        (map_rows, in_hbm(weights.reshape(1, hyper)), in_hbm(patterns.T), rows),
+        [
+            VMEM((hyper // wide - kept, 6, wide, modes), BF16),
+            pltpu.SemaphoreType.DMA((hyper // wide,)),
+        ],
         raw=1,
     )
 
     answer = call(
         functools.partial(micro_kernel, packed, hosts, group),
         "micro_response",
-        [shape_of((hosts, 48, lanes))]
+        [shape_of((hosts, 16, lanes))]
         if packed
-        else [shape_of((ROWS, slots)), shape_of((2, 40, lanes))],
+        else [shape_of((ROWS, slots)), shape_of((2, 8, lanes))],
         (
             received,
             first,
             second,
-            face,
             const,
-            rows,
             bits,
             column,
             table,
+            blocks,
+            rows,
         ),
         [
             VMEM((slots, modes), BF16),
             VMEM((patterns.shape[0], slots), BF16),
-            VMEM((count, 6, lanes, modes), BF16),
-            VMEM(bits.shape, BF16),
-            VMEM(column.shape, F32),
-            VMEM(table.shape, BF16),
-            VMEM((6, lanes, slots), F32),
-            VMEM((6, lanes, slots), F32),
-            VMEM((lanes, slots), BF16),
-            VMEM((lanes, slots), BF16),
-            VMEM((7, 8, slots), F32),
-            VMEM((48, slots), F32),
+            VMEM((hyper // wide - kept, 6, wide, modes), BF16),
+            *[VMEM((6, wide, slots), F32)] * 2,
+            *[VMEM((wide, slots), BF16)] * 4,
             VMEM((ROWS, slots), F32),
-            pltpu.SemaphoreType.DMA((count + 3,)),
+            pltpu.SemaphoreType.DMA((hyper // wide - kept,)),
         ],
-        raw=4,
+        raw=1,
     )
 
     if packed:
         answered = [lax.all_to_all(answer[0], "macro", 0, 0, tiled=True)]
     else:
-        result, faces = answer
+        result, edges = answer
         here = lax.axis_index("macro")
         order = jnp.arange(hosts)[:, None, None]
         flat = result.reshape(ROWS, hosts, capacity).transpose(1, 0, 2).reshape(hosts, -1)
         tiles = pl.cdiv(flat.shape[1], lanes)
         flat = jnp.pad(flat, ((0, 0), (0, tiles * lanes - flat.shape[1])))
         joined = jnp.concatenate(
-            [flat.reshape(hosts, tiles, lanes), jnp.where(order > here, faces[0], faces[1])], axis=1
+            [flat.reshape(hosts, tiles, lanes), jnp.where(order > here, edges[0], edges[1])], axis=1
         )
         joined = lax.all_to_all(joined, "macro", 0, 0, tiled=True)
         flat = joined[:, :tiles].reshape(hosts, -1)[:, : ROWS * capacity]
@@ -802,7 +797,7 @@
         functools.partial(final_kernel, packed, hosts, capacity),
         "final_forces",
         [shape_of(motion.shape), shape_of((36, points))],
-        (*answered, *elastic),
+        (*answered, x_second, x_first, *elastic),
         [
             VMEM((ROWS, points), F32),
             VMEM((3, 4, 16, size_z), F32),

time: 37.5 us -> 33.9 us (0.904)
  the two profiles are of different devices: /device:TPU:1 before, /device:TPU:6 now
where the time goes in v3:
time: 33.9 us; the launch traced here: 33.5 us
  starting transfers between devices  18.3 us (54%)
  Pallas kernels  12.1 us (36%)
  waiting for transfers between devices  2.38 us (7%)
  between operations  0.7 us (2%)
    pallas_call x5, Pallas kernels, call(): pl.pallas_call(kernel, grid=(1,), out_shape=out_shape, in_specs=specs, ou...  12.1 us
    all_to_all x1, starting transfers between devices, on_device(): received = lax.all_to_all(payload[0], 'macro', 0, 0, tiled=True)  6.34 us
    all_to_all x1, starting transfers between devices, on_device(): answered = [lax.all_to_all(answer[0], 'macro', 0, 0, tiled=True)]  6.01 us
    ppermute x4, starting transfers between devices, swapped(): return lax.ppermute(value, axis, pairs + [(b, a) for a, b in pairs])  5.98 us
    ppermute x4, waiting for transfers between devices, swapped(): return lax.ppermute(value, axis, pairs + [(b, a) for a, b in pairs])  2.38 us
  transfers between devices with their start and end apart: 6, of which 2 were waited for; matrix products, arithmetic and copies ran while one was open for 0% of the time, Pallas kernels for 14%

profile of v3, /device:TPU:6, one launch (start us, length us, event | category | flops | bytes accessed | tf_op | source)
XLA Modules:
  0.0 33.5 jit_solution(11081325804935208059)
XLA Ops:
  0.6 2.3 %dispatch.1 = (bf16[8,72,128]{2,1,0:T(8,128)(2,1)}, f32[4,8,128]{2,1,0:T(8,128)S(1)}, f32[4,8,128]{2,1,0:T(8,128)S(1)}, f32[4,8,128]{2,1,0:T(8,128)S(1)}, f32[4,8,128]{2,1,0:T(8,128)S(1)}) custom-call(f32[3,8,8,128]{3,2,1,0:T(8,128)} %motion_ref.3, bf16[8,8,128]{2,1,0:T(8,128)(2,1)} %stiff_ref.3, s32[1,128]{1,0:T(1,128)} %bitcast.14, s32[1,128]{1,0:T(1,128)} %bitcast.16, ...), custom_call_target="tpu_custom_call" | custom-call | flops 100000000 | bytes 1048576 | tf_op jit(solution)/shard_map/dispatch/pallas_call | solution.py:627
  2.9 6.3 %all-to-all-start = ((bf16[8,72,128]{2,1,0:T(8,128)(2,1)}), bf16[8,72,128]{2,1,0:T(8,128)(2,1)S(1)}, u32[]{:S(2)}, u32[]{:S(2)}) async-start(bf16[8,72,128]{2,1,0:T(8,128)(2,1)} %get-tuple-element.15), calls=%async_computation | async-start | bytes 294912 | tf_op jit(solution)/shard_map/all_to_all | solution.py:685
  9.2 0.0 collective-permute-start
  9.2 2.5 %collective-permute-start.1 = (f32[4,8,128]{2,1,0:T(8,128)S(1)}, f32[4,8,128]{2,1,0:T(8,128)S(1)}, u32[]{:S(2)}, u32[]{:S(2)}) collective-permute-start(f32[4,8,128]{2,1,0:T(8,128)S(1)} %get-tuple-element.17), channel_id=1, source_target_pairs={{1,2},{2,1},{5,6},{6,5},{9,10},{10,9},{13,14},{14,13},{17,18},{18,... | collective-permute-start | bytes 49160 | tf_op jit(solution)/shard_map/ppermute | solution.py:711
  11.8 3.4 %tables.1 = (bf16[96,1024]{1,0:T(8,128)(2,1)S(1)}, f32[48,128]{1,0:T(8,128)S(1)}, f32[1024,128]{1,0:T(8,128)S(1)}, bf16[1024,64]{1,0:T(8,128)(2,1)S(1)}, bf16[2,6,256,256]{3,2,1,0:T(8,128)(2,1)S(1)}) custom-call(bf16[6,256]{1,0:T(8,128)(2,1)} %bitcast.11, f32[1,1024]{1,0:T(1,128)} %bitcast.12, s32[35,64]{1,0:T(8,128)} %bitcast.9, bf16[6,1024,256]{2,1,0:T(8,128)(2,1)} %bitcast.7), custom_call_target="tpu_custom_call" | custom-call | flops 100000000 | bytes 1048576 | tf_op jit(solution)/shard_map/tables/pallas_call | solution.py:627
  15.2 0.0 collective-permute-done.first_ref
  15.2 0.0 collective-permute-done.1.second_ref
  15.3 0.0 all-to-all-done.received_ref
  15.3 3.7 %micro_response.1 = f32[8,16,128]{2,1,0:T(8,128)} custom-call(bf16[8,72,128]{2,1,0:T(8,128)(2,1)S(1)} %all-to-all-done.received_ref, f32[4,8,128]{2,1,0:T(8,128)S(1)} %collective-permute-done.first_ref, f32[4,8,128]{2,1,0:T(8,128)S(1)} %collective-permute-done.1.second_ref, f32[48,128]{1,0:T(8,128)S(1)} %get-tuple-element.18.const_ref, ...), custom_call_target="tpu_custom_call" | custom-call | flops 100000000 | bytes 1048576 | tf_op jit(solution)/shard_map/micro_response/pallas_call | solution.py:627
  19.0 6.0 %all-to-all-start.1 = ((f32[8,16,128]{2,1,0:T(8,128)}), f32[8,16,128]{2,1,0:T(8,128)S(1)}, u32[]{:S(2)}, u32[]{:S(2)}) async-start(f32[8,16,128]{2,1,0:T(8,128)} %micro_response.1), calls=%async_computation.1 | async-start | bytes 131072 | tf_op jit(solution)/shard_map/all_to_all | solution.py:766
  25.0 3.4 %collective-permute-start.2 = (f32[4,8,128]{2,1,0:T(8,128)S(1)}, f32[4,8,128]{2,1,0:T(8,128)S(1)}, u32[]{:S(2)}, u32[]{:S(2)}) collective-permute-start(f32[4,8,128]{2,1,0:T(8,128)S(1)} %get-tuple-element.23), channel_id=1, source_target_pairs={{4,8},{12,16},{20,24},{8,4},{16,12},{24,20},{5,9},{13,17},{21,25},... | collective-permute-start | bytes 49160 | tf_op jit(solution)/shard_map/ppermute | solution.py:711
  28.3 0.1 collective-permute-start.3
  28.4 1.3 %elastic_forces.1 = (f32[3,8,8,128]{3,2,1,0:T(8,128)S(1)}, f32[7,16,128]{2,1,0:T(8,128)S(1)}, s32[8,128]{1,0:T(8,128)S(1)}) custom-call(f32[3,8,8,128]{3,2,1,0:T(8,128)} %motion_ref.3, bf16[8,8,128]{2,1,0:T(8,128)(2,1)} %stiff_ref.3, s32[1,128]{1,0:T(1,128)} %bitcast.15, s32[1,128]{1,0:T(1,128)} %bitcast.17, ...), custom_call_target="tpu_custom_call" | custom-call | flops 100000000 | bytes 1048576 | tf_op jit(solution)/shard_map/elastic_forces/pallas_call | solution.py:627
  29.8 1.7 %collective-permute-done.2.rest_0_ = f32[4,8,128]{2,1,0:T(8,128)S(1)} collective-permute-done((f32[4,8,128]{2,1,0:T(8,128)S(1)}, f32[4,8,128]{2,1,0:T(8,128)S(1)}, u32[]{:S(2)}, u32[]{:S(2)}) %collective-permute-start.2) | collective-permute-done | bytes 16416 | tf_op jit(solution)/shard_map/ppermute | solution.py:711
  31.5 0.7 %collective-permute-done.3.rest_1_ = f32[4,8,128]{2,1,0:T(8,128)S(1)} collective-permute-done((f32[4,8,128]{2,1,0:T(8,128)S(1)}, f32[4,8,128]{2,1,0:T(8,128)S(1)}, u32[]{:S(2)}, u32[]{:S(2)}) %collective-permute-start.3) | collective-permute-done | bytes 16416 | tf_op jit(solution)/shard_map/ppermute | solution.py:711
  32.1 0.0 all-to-all-done.1.answer_ref
  32.1 1.3 %final_forces.1 = (f32[3,8,8,128]{3,2,1,0:T(8,128)}, f32[36,128]{1,0:T(8,128)}) custom-call(f32[8,16,128]{2,1,0:T(8,128)S(1)} %all-to-all-done.1.answer_ref, f32[4,8,128]{2,1,0:T(8,128)S(1)} %collective-permute-done.2.rest_0_, f32[4,8,128]{2,1,0:T(8,128)S(1)} %collective-permute-done.3.rest_1_, f32[3,8,8,128]{3,2,1,0:T(8,128)S(1)} %get-tuple-element.25.rest_2_, ...), custom_call_target="tpu_custom_call" | custom-call | flops 100000000 | bytes 1048576 | tf_op jit(solution)/shard_map/final_forces/pallas_call | solution.py:627
Async XLA Ops:
  2.9 12.4 %all-to-all-start = ((bf16[8,72,128]{2,1,0:T(8,128)(2,1)}), bf16[8,72,128]{2,1,0:T(8,128)(2,1)S(1)}, u32[]{:S(2)}, u32[]{:S(2)}) async-start(bf16[8,72,128]{2,1,0:T(8,128)(2,1)} %get-tuple-element.15), calls=%async_computation | async-start | bytes 294912 | tf_op jit(solution)/shard_map/all_to_all | solution.py:685
  9.2 6.0 %collective-permute-start = (f32[4,8,128]{2,1,0:T(8,128)S(1)}, f32[4,8,128]{2,1,0:T(8,128)S(1)}, u32[]{:S(2)}, u32[]{:S(2)}) collective-permute-start(f32[4,8,128]{2,1,0:T(8,128)S(1)} %get-tuple-element.16), channel_id=1, source_target_pairs={{0,1},{2,3},{1,0},{3,2},{4,5},{6,7},{5,4},{7,6},{8,9},{10,11},{9,8... | collective-permute-start | bytes 49160 | tf_op jit(solution)/shard_map/ppermute | solution.py:711
  9.2 6.0 %collective-permute-start.1 = (f32[4,8,128]{2,1,0:T(8,128)S(1)}, f32[4,8,128]{2,1,0:T(8,128)S(1)}, u32[]{:S(2)}, u32[]{:S(2)}) collective-permute-start(f32[4,8,128]{2,1,0:T(8,128)S(1)} %get-tuple-element.17), channel_id=1, source_target_pairs={{1,2},{2,1},{5,6},{6,5},{9,10},{10,9},{13,14},{14,13},{17,18},{18,... | collective-permute-start | bytes 49160 | tf_op jit(solution)/shard_map/ppermute | solution.py:711
  19.0 13.2 %all-to-all-start.1 = ((f32[8,16,128]{2,1,0:T(8,128)}), f32[8,16,128]{2,1,0:T(8,128)S(1)}, u32[]{:S(2)}, u32[]{:S(2)}) async-start(f32[8,16,128]{2,1,0:T(8,128)} %micro_response.1), calls=%async_computation.1 | async-start | bytes 131072 | tf_op jit(solution)/shard_map/all_to_all | solution.py:766
  25.0 6.5 %collective-permute-start.2 = (f32[4,8,128]{2,1,0:T(8,128)S(1)}, f32[4,8,128]{2,1,0:T(8,128)S(1)}, u32[]{:S(2)}, u32[]{:S(2)}) collective-permute-start(f32[4,8,128]{2,1,0:T(8,128)S(1)} %get-tuple-element.23), channel_id=1, source_target_pairs={{4,8},{12,16},{20,24},{8,4},{16,12},{24,20},{5,9},{13,17},{21,25},... | collective-permute-start | bytes 49160 | tf_op jit(solution)/shard_map/ppermute | solution.py:711
  28.3 3.8 %collective-permute-start.3 = (f32[4,8,128]{2,1,0:T(8,128)S(1)}, f32[4,8,128]{2,1,0:T(8,128)S(1)}, u32[]{:S(2)}, u32[]{:S(2)}) collective-permute-start(f32[4,8,128]{2,1,0:T(8,128)S(1)} %get-tuple-element.24), channel_id=1, source_target_pairs={{0,4},{8,12},{16,20},{24,28},{4,0},{12,8},{20,16},{28,24},{1,5},{9... | collective-permute-start | bytes 49160 | tf_op jit(solution)/shard_map/ppermute | solution.py:711

commit v4 on v3

--- a/solution.py
+++ b/solution.py
@@ -106,31 +106,45 @@
     return host_hot, position, owner * capacity + position
 
 
-def dispatch_kernel(
-    hosts,
-    capacity,
-    direct,
-    motion_ref,
-    stiff_ref,
-    elem_ref,
-    owner_ref,
-    pattern_ref,
-    history_ref,
-    map_ref,
-    payload_ref,
-    *rest,
-):
+def dispatch_kernel(hosts, capacity, direct, *refs):
+    inputs, basis_ref, payload_out, refs = refs[:7], refs[7], refs[8], list(refs[9:])
+    ids_ref = None if direct else refs.pop(0)
+    first_ref, second_ref, x_first_ref, x_second_ref, blocks_ref = refs[:5]
+    buffers, payload_ref, sems = refs[5:12], refs[12], refs[13]
+    arrivals = [
+        pltpu.make_async_copy(value, buffer, sems.at[n])
+        for n, (value, buffer) in enumerate(zip(inputs, buffers))
+    ]
+    for copy in arrivals:
+        copy.start()
+    kept, _, wide, _ = blocks_ref.shape
+    later = [
+        pltpu.make_async_copy(
+            basis_ref.at[:, pl.ds(n * wide, wide), :], blocks_ref.at[n], sems.at[8 + n]
+        )
+        for n in range(kept)
+    ]
+    for copy in later:
+        copy.start()
+    owner_ref, elem_ref, motion_ref, map_ref, history_ref, pattern_ref, stiff_ref = buffers
     size_x, size_y, size_z = motion_ref.shape[1:]
-    elem, owner = elem_ref[...], owner_ref[...]
-    points = elem.shape[1]
-    strain = block_strains([motion_ref[m] for m in range(3)])
-    rows = (size_x - 1) * size_y
-    field = jnp.concatenate([value.reshape(rows, size_z) for value in strain], axis=0)
+    arrivals[0].wait()
+    owner = owner_ref[...]
+    points = owner.shape[1]
+    host_hot, position, slot = slots_of(owner, hosts, capacity)
+    slot_total = hosts * capacity
+    slot_hot = jnp.where(iota((slot_total, points), 0) == slot, 1.0, 0.0).astype(BF16)
+    arrivals[1].wait()
+    elem = elem_ref[...]
     column = elem // size_z
     depth = elem - column * size_z
     depth_hot = jnp.where(iota((size_z, points), 0) == depth, 1.0, 0.0).astype(BF16)
+    rows = (size_x - 1) * size_y
+    column_hot = iota((rows, points), 0) == column
+    arrivals[2].wait()
+    strain = block_strains([motion_ref[m] for m in range(3)])
+    field = jnp.concatenate([value.reshape(rows, size_z) for value in strain], axis=0)
     picked = jnp.dot(field.astype(BF16), depth_hot, preferred_element_type=F32)
-    column_hot = iota((rows, points), 0) == column
     macro_strain = jnp.concatenate(
         [
             jnp.sum(
@@ -142,13 +156,12 @@
         ],
         axis=0,
     ).astype(BF16)
+    for copy in arrivals[3:]:
+        copy.wait()
     mapped = lax.dot_general(
         map_ref[...], macro_strain, (((0,), (0,)), ((), ())), preferred_element_type=F32
     )
     coefficients = (mapped + history_ref[...].astype(F32)).astype(BF16)
-    host_hot, position, slot = slots_of(owner, hosts, capacity)
-    slot_total = hosts * capacity
-    slot_hot = jnp.where(iota((slot_total, points), 0) == slot, 1.0, 0.0).astype(BF16)
     sent = dot_t(slot_hot, coefficients).astype(BF16)
     place = position + lax.axis_index("macro") * capacity
     modes = sent.shape[1]
@@ -166,9 +179,9 @@
             payload_ref[h, 2 * capacity :, :] = tile.astype(BF16)
     else:
         payload_ref[...] = sent
-        rest[0][...] = ids.astype(BF16)
-        rest = rest[1:]
-    first_ref, second_ref, x_first_ref, x_second_ref = rest
+        ids_ref[...] = ids.astype(BF16)
+    leave = pltpu.make_async_copy(payload_ref, payload_out, sems.at[7])
+    leave.start()
     stiffness = stiff_ref[...].astype(F32)
     even = lax.rem(lax.axis_index("micro"), 2) == 0
     for i in range(size_x):
@@ -187,18 +200,21 @@
             up = down = stiffness[size_x - 1]
         x_first_ref[m] = jnp.where(even, up, down)
         x_second_ref[m] = jnp.where(even, down, up)
+    leave.wait()
+    for copy in later:
+        copy.wait()
 
 
 def table_kernel(
     map_ref,
     weights_ref,
     patterns_ref,
+    blocks_ref,
     basis_ref,
     table_ref,
     const_ref,
     column_ref,
     bits_ref,
-    blocks_ref,
     others_ref,
     sems,
 ):
@@ -207,12 +223,12 @@
     kept, _, wide, modes = blocks_ref.shape
     count = hyper // wide
     copies = []
-    for n in range(count):
-        target = blocks_ref.at[n] if n < kept else others_ref.at[n - kept]
-        copies.append(
-            pltpu.make_async_copy(basis_ref.at[:, pl.ds(n * wide, wide), :], target, sems.at[n])
+    for n in range(kept, count):
+        copy = pltpu.make_async_copy(
+            basis_ref.at[:, pl.ds(n * wide, wide), :], others_ref.at[n - kept], sems.at[n - kept]
         )
-        copies[n].start()
+        copy.start()
+        copies.append(copy)
     weights = weights_ref[...]
     split = [piece.astype(F32) for piece in pieces(weights, 3)]
     row = iota((8, hyper), 0)
@@ -230,6 +246,7 @@
     parts = [((patterns >> (8 * k)) & 255).astype(F32) for k in range(4)]
     spare = -4 * words % 8
     parts = jnp.concatenate(parts + [jnp.zeros((spare, total), F32)] * (spare > 0), axis=0)
+    parts = jnp.concatenate([parts, jnp.zeros((parts.shape[0], lanes - total), F32)], axis=1)
     place = iota((1, 4 * words + spare), 1)
     part = jnp.where(place >= words, 1, 0) + jnp.where(place >= 2 * words, 1, 0)
     part = part + jnp.where(place >= 3 * words, 1, 0)
@@ -238,7 +255,7 @@
     after = iota((hyper, 4 * words + spare), 0) - start
     byte_hot = jnp.where((after >= 0) & (after < size), 1.0, 0.0).astype(BF16)
     value = jnp.dot(byte_hot, parts.astype(BF16), preferred_element_type=F32).astype(jnp.int32)
-    index = iota((hyper, total), 0)
+    index = iota((hyper, lanes), 0)
     offset = index - 30 * ((index * 2185) >> 16)
     bits_ref[...] = ((value >> (offset & 7)) & 1).astype(F32).astype(BF16)
 
@@ -248,7 +265,8 @@
     ).astype(BF16)
     sums = jnp.zeros((48, wide), F32)
     for n in range(count):
-        copies[n].wait()
+        if n >= kept:
+            copies[n - kept].wait()
         source = blocks_ref.at[n] if n < kept else others_ref.at[n - kept]
         part = slice(n * wide, (n + 1) * wide)
         local = [dot_t(modes_map, source[c]) for c in range(6)]
@@ -303,18 +321,12 @@
         state_ref,
         hot_ref,
         others_ref,
-        strain_even,
-        strain_odd,
-        high_even,
-        high_odd,
-        low_even,
-        low_odd,
+        flags_ref,
+        high_ref,
+        low_ref,
         result_ref,
         sems,
     ) = rest
-    strain_refs = (strain_even, strain_odd)
-    high_refs = (high_even, high_odd)
-    low_refs = (low_even, low_odd)
     groups = received_ref.shape[0]
     slots = groups * capacity
     kept, _, block, modes = blocks_ref.shape
@@ -337,28 +349,42 @@
     ids = jnp.concatenate([ids[0:1], ids[1:2]], axis=1).astype(jnp.int32)
     hot_ref[...] = jnp.where(iota(hot_ref.shape, 0) == ids, 1.0, 0.0).astype(BF16)
 
-    def rows_of(n):
-        if n >= kept:
-            copies[n - kept].wait()
-        source = blocks_ref.at[n] if n < kept else others_ref.at[n - kept]
-        rows = source[...].reshape(6 * block, modes)
-        strain_refs[n % 2][...] = dot_t(rows, state_ref[...]).reshape(6, block, slots)
-
-    def tangent_of(n):
-        table = table_ref[:, n * block : (n + 1) * block]
-        one = jnp.dot(table, high_refs[n % 2][...], preferred_element_type=F32)
-        two = jnp.dot(table[:48], low_refs[n % 2][...], preferred_element_type=F32)
-        return one[:48] + (one[48:] + two)
-
-    def respond(n, sums):
-        sums = list(sums)
-        strain_ref, high_ref, low_ref = (refs[n % 2] for refs in (strain_refs, high_refs, low_refs))
-        part = pl.ds(n * block, block)
-        flags = jnp.dot(bits_ref[part, :], hot_ref[...], preferred_element_type=F32)
+    def solve(*accumulators):
+        mains, spares = accumulators[:8], accumulators[8:12]
+        tangent_high, tangent_low = accumulators[12:]
+        hyper = bits_ref.shape[0]
+        both = range(2)
+        for unit in both:
+            pltpu.matmul_push_rhs(hot_ref[...], 0, unit)
+        empty = jnp.zeros((128, modes - bits_ref.shape[1]), BF16)
+
+        def flags_of(j):
+            rows = jnp.concatenate([bits_ref[128 * j : 128 * j + 128, :], empty], axis=1)
+            pltpu.matmul_acc_lhs(spares[j % 4], rows, load_staged_rhs=0 if j < 2 else None)
+
+        blocks_of_flags = hyper // 128
+        for j in range(blocks_of_flags + 2):
+            if j < blocks_of_flags:
+                flags_of(j)
+            if j >= 2:
+                flags_ref[128 * (j - 2) : 128 * (j - 1), :] = pltpu.matmul_pop(spares[(j - 2) % 4])
+        for unit in both:
+            pltpu.matmul_push_rhs(state_ref[...], 0, unit, transpose=True)
         strip = 16
-        for r in range(0, block, strip):
-            at = pl.ds(r, strip)
-            e = [strain_ref[c, at, :] for c in range(6)]
+        strips = hyper // strip
+
+        def issue(i):
+            n, r = divmod(i * strip, block)
+            if n >= kept and r == 0:
+                copies[n - kept].wait()
+            source = blocks_ref.at[n] if n < kept else others_ref.at[n - kept]
+            rows = jnp.concatenate([source[c, r : r + strip, :] for c in range(6)], axis=0)
+            pltpu.matmul_acc_lhs(mains[i % 8], rows, load_staged_rhs=0 if i < 2 else None)
+
+        def respond(i, sums):
+            strain = pltpu.matmul_pop(mains[i % 8])
+            e = [strain[c * strip : (c + 1) * strip] for c in range(6)]
+            at = slice(i * strip, (i + 1) * strip)
             volume = e[0] + e[1] + e[2]
             third = volume * (1.0 / 3.0)
             d = [e[c] - third for c in range(3)]
@@ -366,29 +392,42 @@
             shear = e[3] * e[3] + e[4] * e[4] + e[5] * e[5]
             square = jnp.maximum(normal + 0.5 * shear, YIELD_STRESS * YIELD_STRESS)
             factor = (YIELD_STRESS * (1.0 - HARDENING)) * lax.rsqrt(square) + (HARDENING - 1.0)
-            change = flags[r : r + strip] * factor
+            change = flags_ref[at, :] * factor
             high = change.astype(BF16)
             high_ref[at, :] = high
             low_ref[at, :] = (change - high.astype(F32)).astype(BF16)
-            column = column_ref[pl.ds(n * block + r, strip), :]
+            column = column_ref[at, :]
             weight = jnp.concatenate([column] * (slots // column.shape[1]), axis=1)
             scaled = weight + weight * change
             terms = [scaled * d[c] for c in range(3)] + [scaled * e[c] for c in range(3, 6)]
             terms.append(weight * volume)
-            for k in range(7):
-                sums[k] = sums[k] + (terms[k][:8] + terms[k][8:])
-        return sums
-
-    sums = [jnp.zeros((8, slots), F32)] * 7
-    tangent = jnp.zeros((48, slots), F32)
-    rows_of(0)
-    for n in range(count):
-        if n > 0:
-            tangent = tangent + tangent_of(n - 1)
-        sums = respond(n, sums)
-        if n + 1 < count:
-            rows_of(n + 1)
-    tangent = tangent + tangent_of(count - 1)
+            return [total + (term[:8] + term[8:]) for total, term in zip(sums, terms)]
+
+        sums = [jnp.zeros((8, slots), F32)] * 7
+        ahead = 7
+        for i in range(ahead):
+            issue(i)
+        for i in range(strips):
+            if i + ahead < strips:
+                issue(i + ahead)
+            sums = respond(i, sums)
+        for n in range(hyper // modes):
+            part = slice(n * modes, (n + 1) * modes)
+            pltpu.matmul_push_rhs(high_ref[part, :], 0, 0)
+            pltpu.matmul_push_rhs(low_ref[part, :], 0, 1)
+            pltpu.matmul_acc_lhs(tangent_high, table_ref[:, part], load_staged_rhs=0)
+            pltpu.matmul_acc_lhs(tangent_low, table_ref[0:48, part], load_staged_rhs=0)
+        both_parts = pltpu.matmul_pop(tangent_high)
+        tangent = both_parts[:48] + (both_parts[48:] + pltpu.matmul_pop(tangent_low))
+        return tangent, sums
+
+    tangent, sums = pl.run_scoped(
+        solve,
+        *[pltpu.ACC(n % 2)((96, slots), F32) for n in range(8)],
+        *[pltpu.ACC(n % 2)((128, slots), F32) for n in range(4)],
+        pltpu.ACC(0)((96, slots), F32),
+        pltpu.ACC(1)((48, slots), F32),
+    )
 
     volume = jnp.sum(sums[6], axis=0, keepdims=True)
     for c in range(6):
@@ -604,10 +643,11 @@
     depth_hot = jnp.where(iota((size_z, points), 0) == depth, 1.0, 0.0).astype(BF16)
     column_hot = iota((rows, points), 0) == column
     stress_ref[:, 1:size_x, 0:1, :] = jnp.zeros((6, size_x - 1, 1, size_z), F32)
+    placed = [jnp.where(column_hot, result[c : c + 1], 0.0) for c in range(6)]
+    placed = jnp.concatenate(pieces(jnp.concatenate(placed, axis=0), 2), axis=0)
+    fields = dot_t(placed, depth_hot)
     for c in range(6):
-        placed = jnp.where(column_hot, result[c : c + 1], 0.0)
-        high, low = pieces(placed, 2)
-        field = dot_t(high, depth_hot) + dot_t(low, depth_hot)
+        field = fields[c * rows : (c + 1) * rows] + fields[(6 + c) * rows : (7 + c) * rows]
         stress_ref[c, 1:size_x, 1 : size_y + 1, :] = field.reshape(size_x - 1, size_y, size_z)
         stress_ref[c, 0] = edge[c][0]
         stress_ref[c, size_x] = edge[c][1]
@@ -622,14 +662,14 @@
     return jax.ShapeDtypeStruct(shape, dtype)
 
 
-def call(kernel, name, out_shape, args, scratch=(), flops=10**8, raw=0):
+def call(kernel, name, out_shape, args, scratch=(), flops=10**8, raw=0, raw_out=0):
     specs = whole(*args[: len(args) - raw]) + [pl.BlockSpec(memory_space=pl.ANY)] * raw
     return pl.pallas_call(
         kernel,
         grid=(1,),
         out_shape=out_shape,
         in_specs=specs,
-        out_specs=whole(*out_shape),
+        out_specs=[pl.BlockSpec(memory_space=pl.ANY)] * raw_out + whole(*out_shape[raw_out:]),
         scratch_shapes=scratch,
         compiler_params=pltpu.CompilerParams(vmem_limit_bytes=24 * 2**20),
         cost_estimate=pl.CostEstimate(flops=flops, bytes_accessed=2**20, transcendentals=0),
@@ -668,28 +708,35 @@
     history = in_hbm(history)
     map_rows = in_hbm(mode_map.T)
 
+    rows = in_hbm(basis.reshape(6, hyper, modes))
+    wide, kept = 256, 2
     sent = (
         [shape_of((hosts, 2 * capacity + 8, half), BF16)]
         if direct
         else [shape_of((slots, modes), BF16), shape_of((hosts, modes), BF16)]
     )
     swap, x_swap = shape_of((4, size_x, size_z)), shape_of((4, size_y, size_z))
-    *payload, first, second, x_first, x_second = call(
+    arguments = (owner, elem, motion, map_rows, history, pattern, stiffness)
+    *payload, first, second, x_first, x_second, blocks = call(
         functools.partial(dispatch_kernel, hosts, capacity, direct),
         "dispatch",
-        sent + [swap, swap, x_swap, x_swap],
-        (motion, stiffness, elem, owner, pattern, history, map_rows),
+        sent + [swap, swap, x_swap, x_swap, shape_of((kept, 6, wide, modes), BF16)],
+        (*arguments, rows),
+        [VMEM(value.shape, value.dtype) for value in (*arguments, sent[0])]
+        + [pltpu.SemaphoreType.DMA((8 + kept,))],
+        raw=8,
+        raw_out=1,
     )
 
     if direct:
         received = lax.all_to_all(payload[0], "macro", 0, 0, tiled=True)
         groups, group = hosts, capacity
     else:
-        rows, ids = payload
+        slot_rows, ids = payload
         joined = jnp.concatenate(
             [
-                rows[:, :half].reshape(hosts, capacity, half),
-                rows[:, half:].reshape(hosts, capacity, half),
+                slot_rows[:, :half].reshape(hosts, capacity, half),
+                slot_rows[:, half:].reshape(hosts, capacity, half),
                 ids.reshape(hosts, 2, half),
             ],
             axis=1,
@@ -713,22 +760,19 @@
     first, second = swapped(first, "micro", 0), swapped(second, "micro", 1)
     x_first, x_second = swapped(x_first, "macro", 0), swapped(x_second, "macro", 1)
 
-    rows = in_hbm(basis.reshape(6, hyper, modes))
-    wide, kept = 256, 2
-    table, const, column, bits, blocks = call(
+    table, const, column, bits = call(
         table_kernel,
         "tables",
         [
             shape_of((96, hyper), BF16),
             shape_of((48, lanes)),
             shape_of((hyper, lanes)),
-            shape_of((hyper, patterns.shape[0]), BF16),
-            shape_of((kept, 6, wide, modes), BF16),
+            shape_of((hyper, lanes), BF16),
         ],
-        (map_rows, in_hbm(weights.reshape(1, hyper)), in_hbm(patterns.T), rows),
+        (map_rows, in_hbm(weights.reshape(1, hyper)), in_hbm(patterns.T), blocks, rows),
         [
             VMEM((hyper // wide - kept, 6, wide, modes), BF16),
-            pltpu.SemaphoreType.DMA((hyper // wide,)),
+            pltpu.SemaphoreType.DMA((hyper // wide - kept,)),
         ],
         raw=1,
     )
@@ -752,10 +796,10 @@
         ),
         [
             VMEM((slots, modes), BF16),
-            VMEM((patterns.shape[0], slots), BF16),
+            VMEM((modes, slots), BF16),
             VMEM((hyper // wide - kept, 6, wide, modes), BF16),
-            *[VMEM((6, wide, slots), F32)] * 2,
-            *[VMEM((wide, slots), BF16)] * 4,
+            VMEM((hyper, slots), F32),
+            *[VMEM((hyper, slots), BF16)] * 2,
             VMEM((ROWS, slots), F32),
             pltpu.SemaphoreType.DMA((hyper // wide - kept,)),
         ],

time: 33.9 us -> 33.5 us (0.988)
  the two profiles are of different devices: /device:TPU:6 before, /device:TPU:0 now
where the time goes in v4:
time: 33.5 us; the launch traced here: 33.1 us
  starting transfers between devices  16.7 us (50%)
  Pallas kernels  11 us (33%)
  waiting for transfers between devices  4.69 us (14%)
  between operations  0.72 us (2%)
    pallas_call x5, Pallas kernels, call(): pl.pallas_call(kernel, grid=(1,), out_shape=out_shape, in_specs=specs, ou...  11 us
    all_to_all x1, starting transfers between devices, on_device(): received = lax.all_to_all(payload[0], 'macro', 0, 0, tiled=True)  7.29 us
    ppermute x4, starting transfers between devices, swapped(): return lax.ppermute(value, axis, pairs + [(b, a) for a, b in pairs])  6.02 us
    all_to_all x1, waiting for transfers between devices, on_device(): received = lax.all_to_all(payload[0], 'macro', 0, 0, tiled=True)  4.07 us
    all_to_all x1, starting transfers between devices, on_device(): answered = [lax.all_to_all(answer[0], 'macro', 0, 0, tiled=True)]  3.36 us
  transfers between devices with their start and end apart: 6, of which 2 were waited for; matrix products, arithmetic and copies ran while one was open for 0% of the time, Pallas kernels for 12%

profile of v4, /device:TPU:0, one launch (start us, length us, event | category | flops | bytes accessed | tf_op | source)
XLA Modules:
  0.0 33.1 jit_solution(6725541451364816247)
XLA Ops:
  0.6 2.4 %dispatch.1 = (bf16[8,72,128]{2,1,0:T(8,128)(2,1)}, f32[4,8,128]{2,1,0:T(8,128)S(1)}, f32[4,8,128]{2,1,0:T(8,128)S(1)}, f32[4,8,128]{2,1,0:T(8,128)S(1)}, f32[4,...) custom-call(s32[1,128]{1,0:T(1,128)} %bitcast.15, s32[1,128]{1,0:T(1,128)} %bitcast.17, ...), custom_call_target="tpu_custom_call" | custom-call | flops 100000000 | bytes 1048576 | tf_op jit(solution)/shard_map/dispatch/pallas_call | solution.py:667
  3.0 7.3 %all-to-all-start = ((bf16[8,72,128]{2,1,0:T(8,128)(2,1)}), bf16[8,72,128]{2,1,0:T(8,128)(2,1)S(1)}, u32[]{:S(2)}, u32[]{:S(2)}) async-start(bf16[8,72,128]{2,1,0:T(8,128)(2,1)} %get-tuple-element.15), calls=%async_computation | async-start | bytes 294912 | tf_op jit(solution)/shard_map/all_to_all | solution.py:732
  10.3 0.0 collective-permute-start
  10.3 0.7 %collective-permute-start.1 = (f32[4,8,128]{2,1,0:T(8,128)S(1)}, f32[4,8,128]{2,1,0:T(8,128)S(1)}, u32[]{:S(2)}, u32[]{:S(2)}) collective-permute-start(f32[4,8,128]{2,1,0:T(8,128)S(1)} %get-tuple-element.17), channel_id=1, source_target_pairs={{1,2},{2,1},{5,6},{6,5},{9,10},{10,9},{13,14},{14,13},{17,18},{18,... | collective-permute-start | bytes 49160 | tf_op jit(solution)/shard_map/ppermute | solution.py:758
  11.0 2.7 %tables.1 = (bf16[96,1024]{1,0:T(8,128)(2,1)S(1)}, f32[48,128]{1,0:T(8,128)S(1)}, f32[1024,128]{1,0:T(8,128)S(1)}, bf16[1024,128]{1,0:T(8,128)(2,1)S(1)}) custom-call(bf16[6,256]{1,0:T(8,128)(2,1)} %bitcast.12, f32[1,1024]{1,0:T(1,128)} %bitcast.13, s32[35,64]{1,0:T(8,128)} %bitcast.10, bf16[2,6,256,256]{3,2,1,0:T(8,128)(2,1)S(1)} %get-tuple-element.18.blocks_ref, ...), custom_call_target="tpu_custom_call" | custom-call | flops 100000000 | bytes 1048576 | tf_op jit(solution)/shard_map/tables/pallas_call | solution.py:667
  13.7 0.0 collective-permute-done.first_ref
  13.7 0.0 collective-permute-done.1.second_ref
  13.7 4.1 %all-to-all-done.received_ref = bf16[8,72,128]{2,1,0:T(8,128)(2,1)S(1)} async-done(((bf16[8,72,128]{2,1,0:T(8,128)(2,1)}), bf16[8,72,128]{2,1,0:T(8,128)(2,1)S(1)}, u32[]{:S(2)}, u32[]{:S(2)}) %all-to-all-start) | async-done | bytes 147488 | tf_op jit(solution)/shard_map/all_to_all | solution.py:732
  17.8 3.4 %micro_response.1 = f32[8,16,128]{2,1,0:T(8,128)} custom-call(bf16[8,72,128]{2,1,0:T(8,128)(2,1)S(1)} %all-to-all-done.received_ref, f32[4,8,128]{2,1,0:T(8,128)S(1)} %collective-permute-done.first_ref, f32[4,8,128]{2,1,0:T(8,128)S(1)} %collective-permute-done.1.second_ref, f32[48,128]{1,0:T(8,128)S(1)} %get-tuple-element.19.const_ref, ...), custom_call_target="tpu_custom_call" | custom-call | flops 100000000 | bytes 1048576 | tf_op jit(solution)/shard_map/micro_response/pallas_call | solution.py:667
  21.1 3.4 %all-to-all-start.1 = ((f32[8,16,128]{2,1,0:T(8,128)}), f32[8,16,128]{2,1,0:T(8,128)S(1)}, u32[]{:S(2)}, u32[]{:S(2)}) async-start(f32[8,16,128]{2,1,0:T(8,128)} %micro_response.1), calls=%async_computation.1 | async-start | bytes 131072 | tf_op jit(solution)/shard_map/all_to_all | solution.py:810
  24.5 0.7 %collective-permute-start.2 = (f32[4,8,128]{2,1,0:T(8,128)S(1)}, f32[4,8,128]{2,1,0:T(8,128)S(1)}, u32[]{:S(2)}, u32[]{:S(2)}) collective-permute-start(f32[4,8,128]{2,1,0:T(8,128)S(1)} %get-tuple-element.23), channel_id=1, source_target_pairs={{4,8},{12,16},{20,24},{8,4},{16,12},{24,20},{5,9},{13,17},{21,25},... | collective-permute-start | bytes 49160 | tf_op jit(solution)/shard_map/ppermute | solution.py:758
  25.2 4.7 %collective-permute-start.3 = (f32[4,8,128]{2,1,0:T(8,128)S(1)}, f32[4,8,128]{2,1,0:T(8,128)S(1)}, u32[]{:S(2)}, u32[]{:S(2)}) collective-permute-start(f32[4,8,128]{2,1,0:T(8,128)S(1)} %get-tuple-element.24), channel_id=1, source_target_pairs={{0,4},{8,12},{16,20},{24,28},{4,0},{12,8},{20,16},{28,24},{1,5},{9... | collective-permute-start | bytes 49160 | tf_op jit(solution)/shard_map/ppermute | solution.py:758
  29.9 1.3 %elastic_forces.1 = (f32[3,8,8,128]{3,2,1,0:T(8,128)S(1)}, f32[7,16,128]{2,1,0:T(8,128)S(1)}, s32[8,128]{1,0:T(8,128)S(1)}) custom-call(f32[3,8,8,128]{3,2,1,0:T(8,128)} %motion_ref.1, bf16[8,8,128]{2,1,0:T(8,128)(2,1)} %stiff_ref.1, s32[1,128]{1,0:T(1,128)} %bitcast.18, s32[1,128]{1,0:T(1,128)} %bitcast.16, ...), custom_call_target="tpu_custom_call" | custom-call | flops 100000000 | bytes 1048576 | tf_op jit(solution)/shard_map/elastic_forces/pallas_call | solution.py:667
  31.2 0.0 collective-permute-done.2.rest_0_
  31.2 0.6 %collective-permute-done.3.rest_1_ = f32[4,8,128]{2,1,0:T(8,128)S(1)} collective-permute-done((f32[4,8,128]{2,1,0:T(8,128)S(1)}, f32[4,8,128]{2,1,0:T(8,128)S(1)}, u32[]{:S(2)}, u32[]{:S(2)}) %collective-permute-start.3) | collective-permute-done | bytes 16416 | tf_op jit(solution)/shard_map/ppermute | solution.py:758
  31.9 0.0 all-to-all-done.1.answer_ref
  31.9 1.2 %final_forces.1 = (f32[3,8,8,128]{3,2,1,0:T(8,128)}, f32[36,128]{1,0:T(8,128)}) custom-call(f32[8,16,128]{2,1,0:T(8,128)S(1)} %all-to-all-done.1.answer_ref, f32[4,8,128]{2,1,0:T(8,128)S(1)} %collective-permute-done.2.rest_0_, f32[4,8,128]{2,1,0:T(8,128)S(1)} %collective-permute-done.3.rest_1_, f32[3,8,8,128]{3,2,1,0:T(8,128)S(1)} %get-tuple-element.25.rest_2_, ...), custom_call_target="tpu_custom_call" | custom-call | flops 100000000 | bytes 1048576 | tf_op jit(solution)/shard_map/final_forces/pallas_call | solution.py:667
Async XLA Ops:
  3.0 14.7 %all-to-all-start = ((bf16[8,72,128]{2,1,0:T(8,128)(2,1)}), bf16[8,72,128]{2,1,0:T(8,128)(2,1)S(1)}, u32[]{:S(2)}, u32[]{:S(2)}) async-start(bf16[8,72,128]{2,1,0:T(8,128)(2,1)} %get-tuple-element.15), calls=%async_computation | async-start | bytes 294912 | tf_op jit(solution)/shard_map/all_to_all | solution.py:732
  10.3 3.4 %collective-permute-start = (f32[4,8,128]{2,1,0:T(8,128)S(1)}, f32[4,8,128]{2,1,0:T(8,128)S(1)}, u32[]{:S(2)}, u32[]{:S(2)}) collective-permute-start(f32[4,8,128]{2,1,0:T(8,128)S(1)} %get-tuple-element.16), channel_id=1, source_target_pairs={{0,1},{2,3},{1,0},{3,2},{4,5},{6,7},{5,4},{7,6},{8,9},{10,11},{9,8... | collective-permute-start | bytes 49160 | tf_op jit(solution)/shard_map/ppermute | solution.py:758
  10.3 3.4 %collective-permute-start.1 = (f32[4,8,128]{2,1,0:T(8,128)S(1)}, f32[4,8,128]{2,1,0:T(8,128)S(1)}, u32[]{:S(2)}, u32[]{:S(2)}) collective-permute-start(f32[4,8,128]{2,1,0:T(8,128)S(1)} %get-tuple-element.17), channel_id=1, source_target_pairs={{1,2},{2,1},{5,6},{6,5},{9,10},{10,9},{13,14},{14,13},{17,18},{18,... | collective-permute-start | bytes 49160 | tf_op jit(solution)/shard_map/ppermute | solution.py:758
  21.1 10.7 %all-to-all-start.1 = ((f32[8,16,128]{2,1,0:T(8,128)}), f32[8,16,128]{2,1,0:T(8,128)S(1)}, u32[]{:S(2)}, u32[]{:S(2)}) async-start(f32[8,16,128]{2,1,0:T(8,128)} %micro_response.1), calls=%async_computation.1 | async-start | bytes 131072 | tf_op jit(solution)/shard_map/all_to_all | solution.py:810
  24.5 6.7 %collective-permute-start.2 = (f32[4,8,128]{2,1,0:T(8,128)S(1)}, f32[4,8,128]{2,1,0:T(8,128)S(1)}, u32[]{:S(2)}, u32[]{:S(2)}) collective-permute-start(f32[4,8,128]{2,1,0:T(8,128)S(1)} %get-tuple-element.23), channel_id=1, source_target_pairs={{4,8},{12,16},{20,24},{8,4},{16,12},{24,20},{5,9},{13,17},{21,25},... | collective-permute-start | bytes 49160 | tf_op jit(solution)/shard_map/ppermute | solution.py:758
  25.2 6.7 %collective-permute-start.3 = (f32[4,8,128]{2,1,0:T(8,128)S(1)}, f32[4,8,128]{2,1,0:T(8,128)S(1)}, u32[]{:S(2)}, u32[]{:S(2)}) collective-permute-start(f32[4,8,128]{2,1,0:T(8,128)S(1)} %get-tuple-element.24), channel_id=1, source_target_pairs={{0,4},{8,12},{16,20},{24,28},{4,0},{12,8},{20,16},{28,24},{1,5},{9... | collective-permute-start | bytes 49160 | tf_op jit(solution)/shard_map/ppermute | solution.py:758

commit v5 on v4

--- a/solution.py
+++ b/solution.py
@@ -128,20 +128,19 @@
         copy.start()
     owner_ref, elem_ref, motion_ref, map_ref, history_ref, pattern_ref, stiff_ref = buffers
     size_x, size_y, size_z = motion_ref.shape[1:]
-    arrivals[0].wait()
+    for copy in arrivals:
+        copy.wait()
     owner = owner_ref[...]
     points = owner.shape[1]
     host_hot, position, slot = slots_of(owner, hosts, capacity)
     slot_total = hosts * capacity
     slot_hot = jnp.where(iota((slot_total, points), 0) == slot, 1.0, 0.0).astype(BF16)
-    arrivals[1].wait()
     elem = elem_ref[...]
     column = elem // size_z
     depth = elem - column * size_z
     depth_hot = jnp.where(iota((size_z, points), 0) == depth, 1.0, 0.0).astype(BF16)
     rows = (size_x - 1) * size_y
     column_hot = iota((rows, points), 0) == column
-    arrivals[2].wait()
     strain = block_strains([motion_ref[m] for m in range(3)])
     field = jnp.concatenate([value.reshape(rows, size_z) for value in strain], axis=0)
     picked = jnp.dot(field.astype(BF16), depth_hot, preferred_element_type=F32)
@@ -156,13 +155,10 @@
         ],
         axis=0,
     ).astype(BF16)
-    for copy in arrivals[3:]:
-        copy.wait()
-    mapped = lax.dot_general(
-        map_ref[...], macro_strain, (((0,), (0,)), ((), ())), preferred_element_type=F32
-    )
-    coefficients = (mapped + history_ref[...].astype(F32)).astype(BF16)
-    sent = dot_t(slot_hot, coefficients).astype(BF16)
+    held = dot_t(slot_hot, history_ref[...])
+    slot_strain = dot_t(slot_hot, macro_strain).astype(BF16)
+    mapped = jnp.dot(slot_strain, map_ref[...], preferred_element_type=F32)
+    sent = (mapped + held).astype(BF16)
     place = position + lax.axis_index("macro") * capacity
     modes = sent.shape[1]
     half = modes // 2
@@ -206,18 +202,25 @@
 
 
 def table_kernel(
-    map_ref,
-    weights_ref,
-    patterns_ref,
     blocks_ref,
+    map_in,
+    weights_in,
+    patterns_in,
     basis_ref,
     table_ref,
     const_ref,
     column_ref,
     bits_ref,
     others_ref,
+    map_ref,
+    weights_ref,
+    patterns_ref,
     sems,
 ):
+    pairs = ((weights_in, weights_ref), (patterns_in, patterns_ref), (map_in, map_ref))
+    arrivals = [pltpu.make_async_copy(*pair, sems.at[n]) for n, pair in enumerate(pairs)]
+    for copy in arrivals:
+        copy.start()
     hyper = weights_ref.shape[1]
     lanes = 128
     kept, _, wide, modes = blocks_ref.shape
@@ -225,10 +228,12 @@
     copies = []
     for n in range(kept, count):
         copy = pltpu.make_async_copy(
-            basis_ref.at[:, pl.ds(n * wide, wide), :], others_ref.at[n - kept], sems.at[n - kept]
+            basis_ref.at[:, pl.ds(n * wide, wide), :], others_ref.at[n - kept], sems.at[3 + n - kept]
         )
         copy.start()
         copies.append(copy)
+    for copy in arrivals:
+        copy.wait()
     weights = weights_ref[...]
     split = [piece.astype(F32) for piece in pieces(weights, 3)]
     row = iota((8, hyper), 0)
@@ -760,6 +765,7 @@
     first, second = swapped(first, "micro", 0), swapped(second, "micro", 1)
     x_first, x_second = swapped(x_first, "macro", 0), swapped(x_second, "macro", 1)
 
+    small = (map_rows, in_hbm(weights.reshape(1, hyper)), in_hbm(patterns.T))
     table, const, column, bits = call(
         table_kernel,
         "tables",
@@ -769,12 +775,13 @@
             shape_of((hyper, lanes)),
             shape_of((hyper, lanes), BF16),
         ],
-        (map_rows, in_hbm(weights.reshape(1, hyper)), in_hbm(patterns.T), blocks, rows),
+        (blocks, *small, rows),
         [
             VMEM((hyper // wide - kept, 6, wide, modes), BF16),
-            pltpu.SemaphoreType.DMA((hyper // wide - kept,)),
+            *[VMEM(value.shape, value.dtype) for value in small],
+            pltpu.SemaphoreType.DMA((3 + hyper // wide - kept,)),
         ],
-        raw=1,
+        raw=4,
     )
 
     answer = call(

time: 33.5 us -> 33.3 us (level)
  Pallas kernels: 11 us -> 10.5 us
    pallas_call x5, Pallas kernels: 11 us -> 10.5 us  [call(): pl.pallas_call(kernel, grid=(1,), out_shape=out_shape, in_specs=specs, ou...]
  transfers between devices with their start and end apart: 6 -> 6, of which waited for: 2 -> 3; matrix products, arithmetic and copies ran while one was open for 0% -> 0% of each run, Pallas kernels for 12% -> 11%
where the time goes in v5:
time: 33.3 us; the launch traced here: 32.9 us
  starting transfers between devices  16.7 us (50%)
  Pallas kernels  10.5 us (32%)
  waiting for transfers between devices  4.96 us (15%)
  between operations  0.72 us (2%)
    pallas_call x5, Pallas kernels, call(): pl.pallas_call(kernel, grid=(1,), out_shape=out_shape, in_specs=specs, ou...  10.5 us
    all_to_all x1, starting transfers between devices, on_device(): received = lax.all_to_all(payload[0], 'macro', 0, 0, tiled=True)  7.29 us
    ppermute x4, starting transfers between devices, swapped(): return lax.ppermute(value, axis, pairs + [(b, a) for a, b in pairs])  6.02 us
    all_to_all x1, waiting for transfers between devices, on_device(): received = lax.all_to_all(payload[0], 'macro', 0, 0, tiled=True)  4.4 us
    all_to_all x1, starting transfers between devices, on_device(): answered = [lax.all_to_all(answer[0], 'macro', 0, 0, tiled=True)]  3.36 us
  transfers between devices with their start and end apart: 6, of which 3 were waited for; matrix products, arithmetic and copies ran while one was open for 0% of the time, Pallas kernels for 11%

profile of v5, /device:TPU:0, one launch (start us, length us, event | category | flops | bytes accessed | tf_op | source)
XLA Modules:
  0.0 32.9 jit_solution(4348236651196790470)
XLA Ops:
  0.6 2.3 %dispatch.1 = (bf16[8,72,128]{2,1,0:T(8,128)(2,1)}, f32[4,8,128]{2,1,0:T(8,128)S(1)}, f32[4,8,128]{2,1,0:T(8,128)S(1)}, f32[4,8,128]{2,1,0:T(8,128)S(1)}, f32[4,...) custom-call(s32[1,128]{1,0:T(1,128)} %bitcast.15, s32[1,128]{1,0:T(1,128)} %bitcast.17, ...), custom_call_target="tpu_custom_call" | custom-call | flops 100000000 | bytes 1048576 | tf_op jit(solution)/shard_map/dispatch/pallas_call | solution.py:672
  2.9 7.3 %all-to-all-start = ((bf16[8,72,128]{2,1,0:T(8,128)(2,1)}), bf16[8,72,128]{2,1,0:T(8,128)(2,1)S(1)}, u32[]{:S(2)}, u32[]{:S(2)}) async-start(bf16[8,72,128]{2,1,0:T(8,128)(2,1)} %get-tuple-element.15), calls=%async_computation | async-start | bytes 294912 | tf_op jit(solution)/shard_map/all_to_all | solution.py:737
  10.2 0.0 collective-permute-start
  10.2 0.7 %collective-permute-start.1 = (f32[4,8,128]{2,1,0:T(8,128)S(1)}, f32[4,8,128]{2,1,0:T(8,128)S(1)}, u32[]{:S(2)}, u32[]{:S(2)}) collective-permute-start(f32[4,8,128]{2,1,0:T(8,128)S(1)} %get-tuple-element.17), channel_id=1, source_target_pairs={{1,2},{2,1},{5,6},{6,5},{9,10},{10,9},{13,14},{14,13},{17,18},{18,... | collective-permute-start | bytes 49160 | tf_op jit(solution)/shard_map/ppermute | solution.py:763
  10.9 2.3 %tables.1 = (bf16[96,1024]{1,0:T(8,128)(2,1)S(1)}, f32[48,128]{1,0:T(8,128)S(1)}, f32[1024,128]{1,0:T(8,128)S(1)}, bf16[1024,128]{1,0:T(8,128)(2,1)S(1)}) custom-call(bf16[2,6,256,256]{3,2,1,0:T(8,128)(2,1)S(1)} %get-tuple-element.18.blocks_ref, bf16[6,256]{1,0:T(8,128)(2,1)} %bitcast.12, f32[1,1024]{1,0:T(1,128)} %bitcast.13, s32[35,64]{1,0:T(8,128)} %bitcast.10, ...), custom_call_target="tpu_custom_call" | custom-call | flops 100000000 | bytes 1048576 | tf_op jit(solution)/shard_map/tables/pallas_call | solution.py:672
  13.3 0.0 collective-permute-done.first_ref
  13.3 0.0 collective-permute-done.1.second_ref
  13.3 4.4 %all-to-all-done.received_ref = bf16[8,72,128]{2,1,0:T(8,128)(2,1)S(1)} async-done(((bf16[8,72,128]{2,1,0:T(8,128)(2,1)}), bf16[8,72,128]{2,1,0:T(8,128)(2,1)S(1)}, u32[]{:S(2)}, u32[]{:S(2)}) %all-to-all-start) | async-done | bytes 147488 | tf_op jit(solution)/shard_map/all_to_all | solution.py:737
  17.7 3.4 %micro_response.1 = f32[8,16,128]{2,1,0:T(8,128)} custom-call(bf16[8,72,128]{2,1,0:T(8,128)(2,1)S(1)} %all-to-all-done.received_ref, f32[4,8,128]{2,1,0:T(8,128)S(1)} %collective-permute-done.first_ref, f32[4,8,128]{2,1,0:T(8,128)S(1)} %collective-permute-done.1.second_ref, f32[48,128]{1,0:T(8,128)S(1)} %get-tuple-element.19.const_ref, ...), custom_call_target="tpu_custom_call" | custom-call | flops 100000000 | bytes 1048576 | tf_op jit(solution)/shard_map/micro_response/pallas_call | solution.py:672
  21.0 3.4 %all-to-all-start.1 = ((f32[8,16,128]{2,1,0:T(8,128)}), f32[8,16,128]{2,1,0:T(8,128)S(1)}, u32[]{:S(2)}, u32[]{:S(2)}) async-start(f32[8,16,128]{2,1,0:T(8,128)} %micro_response.1), calls=%async_computation.1 | async-start | bytes 131072 | tf_op jit(solution)/shard_map/all_to_all | solution.py:817
  24.4 0.7 %collective-permute-start.2 = (f32[4,8,128]{2,1,0:T(8,128)S(1)}, f32[4,8,128]{2,1,0:T(8,128)S(1)}, u32[]{:S(2)}, u32[]{:S(2)}) collective-permute-start(f32[4,8,128]{2,1,0:T(8,128)S(1)} %get-tuple-element.23), channel_id=1, source_target_pairs={{4,8},{12,16},{20,24},{8,4},{16,12},{24,20},{5,9},{13,17},{21,25},... | collective-permute-start | bytes 49160 | tf_op jit(solution)/shard_map/ppermute | solution.py:763
  25.1 4.7 %collective-permute-start.3 = (f32[4,8,128]{2,1,0:T(8,128)S(1)}, f32[4,8,128]{2,1,0:T(8,128)S(1)}, u32[]{:S(2)}, u32[]{:S(2)}) collective-permute-start(f32[4,8,128]{2,1,0:T(8,128)S(1)} %get-tuple-element.24), channel_id=1, source_target_pairs={{0,4},{8,12},{16,20},{24,28},{4,0},{12,8},{20,16},{28,24},{1,5},{9... | collective-permute-start | bytes 49160 | tf_op jit(solution)/shard_map/ppermute | solution.py:763
  29.8 1.3 %elastic_forces.1 = (f32[3,8,8,128]{3,2,1,0:T(8,128)S(1)}, f32[7,16,128]{2,1,0:T(8,128)S(1)}, s32[8,128]{1,0:T(8,128)S(1)}) custom-call(f32[3,8,8,128]{3,2,1,0:T(8,128)} %motion_ref.1, bf16[8,8,128]{2,1,0:T(8,128)(2,1)} %stiff_ref.1, s32[1,128]{1,0:T(1,128)} %bitcast.18, s32[1,128]{1,0:T(1,128)} %bitcast.16, ...), custom_call_target="tpu_custom_call" | custom-call | flops 100000000 | bytes 1048576 | tf_op jit(solution)/shard_map/elastic_forces/pallas_call | solution.py:672
  31.1 0.0 collective-permute-done.2.rest_0_
  31.1 0.5 %collective-permute-done.3.rest_1_ = f32[4,8,128]{2,1,0:T(8,128)S(1)} collective-permute-done((f32[4,8,128]{2,1,0:T(8,128)S(1)}, f32[4,8,128]{2,1,0:T(8,128)S(1)}, u32[]{:S(2)}, u32[]{:S(2)}) %collective-permute-start.3) | collective-permute-done | bytes 16416 | tf_op jit(solution)/shard_map/ppermute | solution.py:763
  31.6 0.1 all-to-all-done.1.answer_ref
  31.7 1.2 %final_forces.1 = (f32[3,8,8,128]{3,2,1,0:T(8,128)}, f32[36,128]{1,0:T(8,128)}) custom-call(f32[8,16,128]{2,1,0:T(8,128)S(1)} %all-to-all-done.1.answer_ref, f32[4,8,128]{2,1,0:T(8,128)S(1)} %collective-permute-done.2.rest_0_, f32[4,8,128]{2,1,0:T(8,128)S(1)} %collective-permute-done.3.rest_1_, f32[3,8,8,128]{3,2,1,0:T(8,128)S(1)} %get-tuple-element.25.rest_2_, ...), custom_call_target="tpu_custom_call" | custom-call | flops 100000000 | bytes 1048576 | tf_op jit(solution)/shard_map/final_forces/pallas_call | solution.py:672
Async XLA Ops:
  2.9 14.7 %all-to-all-start = ((bf16[8,72,128]{2,1,0:T(8,128)(2,1)}), bf16[8,72,128]{2,1,0:T(8,128)(2,1)S(1)}, u32[]{:S(2)}, u32[]{:S(2)}) async-start(bf16[8,72,128]{2,1,0:T(8,128)(2,1)} %get-tuple-element.15), calls=%async_computation | async-start | bytes 294912 | tf_op jit(solution)/shard_map/all_to_all | solution.py:737
  10.2 3.0 %collective-permute-start = (f32[4,8,128]{2,1,0:T(8,128)S(1)}, f32[4,8,128]{2,1,0:T(8,128)S(1)}, u32[]{:S(2)}, u32[]{:S(2)}) collective-permute-start(f32[4,8,128]{2,1,0:T(8,128)S(1)} %get-tuple-element.16), channel_id=1, source_target_pairs={{0,1},{2,3},{1,0},{3,2},{4,5},{6,7},{5,4},{7,6},{8,9},{10,11},{9,8... | collective-permute-start | bytes 49160 | tf_op jit(solution)/shard_map/ppermute | solution.py:763
  10.2 3.0 %collective-permute-start.1 = (f32[4,8,128]{2,1,0:T(8,128)S(1)}, f32[4,8,128]{2,1,0:T(8,128)S(1)}, u32[]{:S(2)}, u32[]{:S(2)}) collective-permute-start(f32[4,8,128]{2,1,0:T(8,128)S(1)} %get-tuple-element.17), channel_id=1, source_target_pairs={{1,2},{2,1},{5,6},{6,5},{9,10},{10,9},{13,14},{14,13},{17,18},{18,... | collective-permute-start | bytes 49160 | tf_op jit(solution)/shard_map/ppermute | solution.py:763
  21.0 10.6 %all-to-all-start.1 = ((f32[8,16,128]{2,1,0:T(8,128)}), f32[8,16,128]{2,1,0:T(8,128)S(1)}, u32[]{:S(2)}, u32[]{:S(2)}) async-start(f32[8,16,128]{2,1,0:T(8,128)} %micro_response.1), calls=%async_computation.1 | async-start | bytes 131072 | tf_op jit(solution)/shard_map/all_to_all | solution.py:817
  24.4 6.7 %collective-permute-start.2 = (f32[4,8,128]{2,1,0:T(8,128)S(1)}, f32[4,8,128]{2,1,0:T(8,128)S(1)}, u32[]{:S(2)}, u32[]{:S(2)}) collective-permute-start(f32[4,8,128]{2,1,0:T(8,128)S(1)} %get-tuple-element.23), channel_id=1, source_target_pairs={{4,8},{12,16},{20,24},{8,4},{16,12},{24,20},{5,9},{13,17},{21,25},... | collective-permute-start | bytes 49160 | tf_op jit(solution)/shard_map/ppermute | solution.py:763
  25.1 6.6 %collective-permute-start.3 = (f32[4,8,128]{2,1,0:T(8,128)S(1)}, f32[4,8,128]{2,1,0:T(8,128)S(1)}, u32[]{:S(2)}, u32[]{:S(2)}) collective-permute-start(f32[4,8,128]{2,1,0:T(8,128)S(1)} %get-tuple-element.24), channel_id=1, source_target_pairs={{0,4},{8,12},{16,20},{24,28},{4,0},{12,8},{20,16},{28,24},{1,5},{9... | collective-permute-start | bytes 49160 | tf_op jit(solution)/shard_map/ppermute | solution.py:763

commit v6 on v4

--- a/solution.py
+++ b/solution.py
@@ -107,10 +107,10 @@
 
 
 def dispatch_kernel(hosts, capacity, direct, *refs):
-    inputs, basis_ref, payload_out, refs = refs[:7], refs[7], refs[8], list(refs[9:])
+    inputs, basis_ref, payload_out, refs = refs[:9], refs[9], refs[10], list(refs[11:])
     ids_ref = None if direct else refs.pop(0)
     first_ref, second_ref, x_first_ref, x_second_ref, blocks_ref = refs[:5]
-    buffers, payload_ref, sems = refs[5:12], refs[12], refs[13]
+    buffers, payload_ref, sems = refs[8:14] + refs[5:8], refs[14], refs[15]
     arrivals = [
         pltpu.make_async_copy(value, buffer, sems.at[n])
         for n, (value, buffer) in enumerate(zip(inputs, buffers))
@@ -120,28 +120,27 @@
     kept, _, wide, _ = blocks_ref.shape
     later = [
         pltpu.make_async_copy(
-            basis_ref.at[:, pl.ds(n * wide, wide), :], blocks_ref.at[n], sems.at[8 + n]
+            basis_ref.at[:, pl.ds(n * wide, wide), :], blocks_ref.at[n], sems.at[10 + n]
         )
         for n in range(kept)
     ]
     for copy in later:
         copy.start()
-    owner_ref, elem_ref, motion_ref, map_ref, history_ref, pattern_ref, stiff_ref = buffers
+    owner_ref, elem_ref, motion_ref, history_ref, pattern_ref, stiff_ref, map_ref, _, _ = buffers
     size_x, size_y, size_z = motion_ref.shape[1:]
-    arrivals[0].wait()
+    for copy in arrivals:
+        copy.wait()
     owner = owner_ref[...]
     points = owner.shape[1]
     host_hot, position, slot = slots_of(owner, hosts, capacity)
     slot_total = hosts * capacity
     slot_hot = jnp.where(iota((slot_total, points), 0) == slot, 1.0, 0.0).astype(BF16)
-    arrivals[1].wait()
     elem = elem_ref[...]
     column = elem // size_z
     depth = elem - column * size_z
     depth_hot = jnp.where(iota((size_z, points), 0) == depth, 1.0, 0.0).astype(BF16)
     rows = (size_x - 1) * size_y
     column_hot = iota((rows, points), 0) == column
-    arrivals[2].wait()
     strain = block_strains([motion_ref[m] for m in range(3)])
     field = jnp.concatenate([value.reshape(rows, size_z) for value in strain], axis=0)
     picked = jnp.dot(field.astype(BF16), depth_hot, preferred_element_type=F32)
@@ -156,13 +155,10 @@
         ],
         axis=0,
     ).astype(BF16)
-    for copy in arrivals[3:]:
-        copy.wait()
-    mapped = lax.dot_general(
-        map_ref[...], macro_strain, (((0,), (0,)), ((), ())), preferred_element_type=F32
-    )
-    coefficients = (mapped + history_ref[...].astype(F32)).astype(BF16)
-    sent = dot_t(slot_hot, coefficients).astype(BF16)
+    held = dot_t(slot_hot, history_ref[...])
+    slot_strain = dot_t(slot_hot, macro_strain).astype(BF16)
+    mapped = jnp.dot(slot_strain, map_ref[...], preferred_element_type=F32)
+    sent = (mapped + held).astype(BF16)
     place = position + lax.axis_index("macro") * capacity
     modes = sent.shape[1]
     half = modes // 2
@@ -180,7 +176,7 @@
     else:
         payload_ref[...] = sent
         ids_ref[...] = ids.astype(BF16)
-    leave = pltpu.make_async_copy(payload_ref, payload_out, sems.at[7])
+    leave = pltpu.make_async_copy(payload_ref, payload_out, sems.at[9])
     leave.start()
     stiffness = stiff_ref[...].astype(F32)
     even = lax.rem(lax.axis_index("micro"), 2) == 0
@@ -206,14 +202,13 @@
 
 
 def table_kernel(
+    blocks_ref,
     map_ref,
     weights_ref,
     patterns_ref,
-    blocks_ref,
     basis_ref,
     table_ref,
     const_ref,
-    column_ref,
     bits_ref,
     others_ref,
     sems,
@@ -235,9 +230,10 @@
     stack = jnp.where(
         row == 0, split[0], jnp.where(row == 1, split[1], jnp.where(row == 2, split[2], 0.0))
     )
-    column_ref[...] = lax.dot_general(
+    choice = jnp.where(iota((8, lanes), 1) == iota((8, lanes), 0) + patterns_ref.shape[1], 1.0, 0.0)
+    weight_lanes = lax.dot_general(
         stack.astype(BF16),
-        jnp.ones((8, lanes), BF16),
+        choice.astype(BF16),
         (((0,), (0,)), ((), ())),
         preferred_element_type=F32,
     )
@@ -257,7 +253,7 @@
     value = jnp.dot(byte_hot, parts.astype(BF16), preferred_element_type=F32).astype(jnp.int32)
     index = iota((hyper, lanes), 0)
     offset = index - 30 * ((index * 2185) >> 16)
-    bits_ref[...] = ((value >> (offset & 7)) & 1).astype(F32).astype(BF16)
+    bits_ref[...] = (((value >> (offset & 7)) & 1).astype(F32) + weight_lanes).astype(BF16)
 
     modes_map = map_ref[...]
     modes_map = jnp.concatenate(
@@ -301,12 +297,12 @@
     packed,
     hosts,
     capacity,
+    flag_lanes,
     received_ref,
     first_ref,
     second_ref,
     const_ref,
     bits_ref,
-    column_ref,
     table_ref,
     blocks_ref,
     basis_ref,
@@ -396,8 +392,10 @@
             high = change.astype(BF16)
             high_ref[at, :] = high
             low_ref[at, :] = (change - high.astype(F32)).astype(BF16)
-            column = column_ref[at, :]
-            weight = jnp.concatenate([column] * (slots // column.shape[1]), axis=1)
+            packed_row = bits_ref[at, :].astype(F32)
+            lane = iota(packed_row.shape, 1)
+            packed_row = jnp.where((lane >= flag_lanes) & (lane < flag_lanes + 3), packed_row, 0.0)
+            weight = jnp.sum(packed_row, axis=1, keepdims=True)
             scaled = weight + weight * change
             terms = [scaled * d[c] for c in range(3)] + [scaled * e[c] for c in range(3, 6)]
             terms.append(weight * volume)
@@ -709,22 +707,25 @@
     map_rows = in_hbm(mode_map.T)
 
     rows = in_hbm(basis.reshape(6, hyper, modes))
-    wide, kept = 256, 2
+    wide, kept = 256, 3
     sent = (
         [shape_of((hosts, 2 * capacity + 8, half), BF16)]
         if direct
         else [shape_of((slots, modes), BF16), shape_of((hosts, modes), BF16)]
     )
     swap, x_swap = shape_of((4, size_x, size_z)), shape_of((4, size_y, size_z))
-    arguments = (owner, elem, motion, map_rows, history, pattern, stiffness)
-    *payload, first, second, x_first, x_second, blocks = call(
+    arguments = (owner, elem, motion, history, pattern, stiffness)
+    small = (map_rows, in_hbm(weights.reshape(1, hyper)), in_hbm(patterns.T))
+    *payload, first, second, x_first, x_second, blocks, map_here, weights, bit_words = call(
         functools.partial(dispatch_kernel, hosts, capacity, direct),
         "dispatch",
-        sent + [swap, swap, x_swap, x_swap, shape_of((kept, 6, wide, modes), BF16)],
-        (*arguments, rows),
+        sent
+        + [swap, swap, x_swap, x_swap, shape_of((kept, 6, wide, modes), BF16)]
+        + [shape_of(value.shape, value.dtype) for value in small],
+        (*arguments, *small, rows),
         [VMEM(value.shape, value.dtype) for value in (*arguments, sent[0])]
-        + [pltpu.SemaphoreType.DMA((8 + kept,))],
-        raw=8,
+        + [pltpu.SemaphoreType.DMA((10 + kept,))],
+        raw=10,
         raw_out=1,
     )
 
@@ -760,16 +761,15 @@
     first, second = swapped(first, "micro", 0), swapped(second, "micro", 1)
     x_first, x_second = swapped(x_first, "macro", 0), swapped(x_second, "macro", 1)
 
-    table, const, column, bits = call(
+    table, const, bits = call(
         table_kernel,
         "tables",
         [
             shape_of((96, hyper), BF16),
             shape_of((48, lanes)),
-            shape_of((hyper, lanes)),
             shape_of((hyper, lanes), BF16),
         ],
-        (map_rows, in_hbm(weights.reshape(1, hyper)), in_hbm(patterns.T), blocks, rows),
+        (blocks, map_here, weights, bit_words, rows),
         [
             VMEM((hyper // wide - kept, 6, wide, modes), BF16),
             pltpu.SemaphoreType.DMA((hyper // wide - kept,)),
@@ -778,7 +778,7 @@
     )
 
     answer = call(
-        functools.partial(micro_kernel, packed, hosts, group),
+        functools.partial(micro_kernel, packed, hosts, group, patterns.shape[0]),
         "micro_response",
         [shape_of((hosts, 16, lanes))]
         if packed
@@ -789,7 +789,6 @@
             second,
             const,
             bits,
-            column,
             table,
             blocks,
             rows,

time: 33.5 us -> 33 us (0.985)
  Pallas kernels: 11 us -> 9.65 us
  waiting for transfers between devices: 4.69 us -> 5.58 us
    pallas_call x5, Pallas kernels: 11 us -> 9.65 us  [call(): pl.pallas_call(kernel, grid=(1,), out_shape=out_shape, in_specs=specs, ou...]
    all_to_all x1, waiting for transfers between devices: 4.07 us -> 5.18 us  [on_device(): received = lax.all_to_all(payload[0], 'macro', 0, 0, tiled=True)]
  transfers between devices with their start and end apart: 6 -> 6, of which waited for: 2 -> 2; matrix products, arithmetic and copies ran while one was open for 0% -> 0% of each run, Pallas kernels for 12% -> 9%
where the time goes in v6:
time: 33 us; the launch traced here: 32.6 us
  starting transfers between devices  16.7 us (51%)
  Pallas kernels  9.65 us (29%)
  waiting for transfers between devices  5.58 us (17%)
  between operations  0.72 us (2%)
    pallas_call x5, Pallas kernels, call(): pl.pallas_call(kernel, grid=(1,), out_shape=out_shape, in_specs=specs, ou...  9.65 us
    all_to_all x1, starting transfers between devices, on_device(): received = lax.all_to_all(payload[0], 'macro', 0, 0, tiled=True)  7.29 us
    ppermute x4, starting transfers between devices, swapped(): return lax.ppermute(value, axis, pairs + [(b, a) for a, b in pairs])  6.02 us
    all_to_all x1, waiting for transfers between devices, on_device(): received = lax.all_to_all(payload[0], 'macro', 0, 0, tiled=True)  5.18 us
    all_to_all x1, starting transfers between devices, on_device(): answered = [lax.all_to_all(answer[0], 'macro', 0, 0, tiled=True)]  3.36 us
  transfers between devices with their start and end apart: 6, of which 2 were waited for; matrix products, arithmetic and copies ran while one was open for 0% of the time, Pallas kernels for 9%

profile of v6, /device:TPU:0, one launch (start us, length us, event | category | flops | bytes accessed | tf_op | source)
XLA Modules:
  0.0 32.6 jit_solution(2795216212001212154)
XLA Ops:
  0.6 2.3 %dispatch.1 = (bf16[8,72,128]{2,1,0:T(8,128)(2,1)}, f32[4,8,128]{2,1,0:T(8,128)S(1)}, f32[4,8,128]{2,1,0:T(8,128)S(1)}, f32[4,8,128]{2,1,0:T(8,128)S(1)}, f32[4,...) custom-call(s32[1,128]{1,0:T(1,128)} %bitcast.14, ...), custom_call_target="tpu_custom_call" | custom-call | flops 100000000 | bytes 1048576 | tf_op jit(solution)/shard_map/dispatch/pallas_call | solution.py:665
  3.0 7.3 %all-to-all-start = ((bf16[8,72,128]{2,1,0:T(8,128)(2,1)}), bf16[8,72,128]{2,1,0:T(8,128)(2,1)S(1)}, u32[]{:S(2)}, u32[]{:S(2)}) async-start(bf16[8,72,128]{2,1,0:T(8,128)(2,1)} %get-tuple-element.17), calls=%async_computation | async-start | bytes 294912 | tf_op jit(solution)/shard_map/all_to_all | solution.py:733
  10.3 0.0 collective-permute-start
  10.3 0.7 %collective-permute-start.1 = (f32[4,8,128]{2,1,0:T(8,128)S(1)}, f32[4,8,128]{2,1,0:T(8,128)S(1)}, u32[]{:S(2)}, u32[]{:S(2)}) collective-permute-start(f32[4,8,128]{2,1,0:T(8,128)S(1)} %get-tuple-element.19), channel_id=1, source_target_pairs={{1,2},{2,1},{5,6},{6,5},{9,10},{10,9},{13,14},{14,13},{17,18},{18,... | collective-permute-start | bytes 49160 | tf_op jit(solution)/shard_map/ppermute | solution.py:759
  10.9 1.6 %tables.1 = (bf16[96,1024]{1,0:T(8,128)(2,1)S(1)}, f32[48,128]{1,0:T(8,128)S(1)}, bf16[1024,128]{1,0:T(8,128)(2,1)S(1)}) custom-call(bf16[3,6,256,256]{3,2,1,0:T(8,128)(2,1)S(1)} %get-tuple-element.20.blocks_ref, bf16[6,256]{1,0:T(8,128)(2,1)S(1)} %get-tuple-element.21.map_ref, f32[1,1024]{1,0:T(1,128)S(1)} %get-tuple-element.22.weights_ref, ...), custom_call_target="tpu_custom_call" | custom-call | flops 100000000 | bytes 1048576 | tf_op jit(solution)/shard_map/tables/pallas_call | solution.py:665
  12.5 0.0 collective-permute-done.first_ref
  12.5 0.0 collective-permute-done.1.second_ref
  12.5 5.2 %all-to-all-done.received_ref = bf16[8,72,128]{2,1,0:T(8,128)(2,1)S(1)} async-done(((bf16[8,72,128]{2,1,0:T(8,128)(2,1)}), bf16[8,72,128]{2,1,0:T(8,128)(2,1)S(1)}, u32[]{:S(2)}, u32[]{:S(2)}) %all-to-all-start) | async-done | bytes 147488 | tf_op jit(solution)/shard_map/all_to_all | solution.py:733
  17.7 3.2 %micro_response.1 = f32[8,16,128]{2,1,0:T(8,128)} custom-call(bf16[8,72,128]{2,1,0:T(8,128)(2,1)S(1)} %all-to-all-done.received_ref, f32[4,8,128]{2,1,0:T(8,128)S(1)} %collective-permute-done.first_ref, f32[4,8,128]{2,1,0:T(8,128)S(1)} %collective-permute-done.1.second_ref, f32[48,128]{1,0:T(8,128)S(1)} %get-tuple-element.24.const_ref, ...), custom_call_target="tpu_custom_call" | custom-call | flops 100000000 | bytes 1048576 | tf_op jit(solution)/shard_map/micro_response/pallas_call | solution.py:665
  20.9 3.4 %all-to-all-start.1 = ((f32[8,16,128]{2,1,0:T(8,128)}), f32[8,16,128]{2,1,0:T(8,128)S(1)}, u32[]{:S(2)}, u32[]{:S(2)}) async-start(f32[8,16,128]{2,1,0:T(8,128)} %micro_response.1), calls=%async_computation.1 | async-start | bytes 131072 | tf_op jit(solution)/shard_map/all_to_all | solution.py:809
  24.3 0.7 %collective-permute-start.2 = (f32[4,8,128]{2,1,0:T(8,128)S(1)}, f32[4,8,128]{2,1,0:T(8,128)S(1)}, u32[]{:S(2)}, u32[]{:S(2)}) collective-permute-start(f32[4,8,128]{2,1,0:T(8,128)S(1)} %get-tuple-element.27), channel_id=1, source_target_pairs={{4,8},{12,16},{20,24},{8,4},{16,12},{24,20},{5,9},{13,17},{21,25},... | collective-permute-start | bytes 49160 | tf_op jit(solution)/shard_map/ppermute | solution.py:759
  25.0 4.7 %collective-permute-start.3 = (f32[4,8,128]{2,1,0:T(8,128)S(1)}, f32[4,8,128]{2,1,0:T(8,128)S(1)}, u32[]{:S(2)}, u32[]{:S(2)}) collective-permute-start(f32[4,8,128]{2,1,0:T(8,128)S(1)} %get-tuple-element.28), channel_id=1, source_target_pairs={{0,4},{8,12},{16,20},{24,28},{4,0},{12,8},{20,16},{28,24},{1,5},{9... | collective-permute-start | bytes 49160 | tf_op jit(solution)/shard_map/ppermute | solution.py:759
  29.7 1.3 %elastic_forces.1 = (f32[3,8,8,128]{3,2,1,0:T(8,128)S(1)}, f32[7,16,128]{2,1,0:T(8,128)S(1)}, s32[8,128]{1,0:T(8,128)S(1)}) custom-call(f32[3,8,8,128]{3,2,1,0:T(8,128)} %motion_ref.1, bf16[8,8,128]{2,1,0:T(8,128)(2,1)} %stiff_ref.1, s32[1,128]{1,0:T(1,128)} %bitcast.17, s32[1,128]{1,0:T(1,128)} %bitcast.15, ...), custom_call_target="tpu_custom_call" | custom-call | flops 100000000 | bytes 1048576 | tf_op jit(solution)/shard_map/elastic_forces/pallas_call | solution.py:665
  31.0 0.0 collective-permute-done.2.rest_0_
  31.0 0.4 %collective-permute-done.3.rest_1_ = f32[4,8,128]{2,1,0:T(8,128)S(1)} collective-permute-done((f32[4,8,128]{2,1,0:T(8,128)S(1)}, f32[4,8,128]{2,1,0:T(8,128)S(1)}, u32[]{:S(2)}, u32[]{:S(2)}) %collective-permute-start.3) | collective-permute-done | bytes 16416 | tf_op jit(solution)/shard_map/ppermute | solution.py:759
  31.4 0.0 all-to-all-done.1.answer_ref
  31.4 1.2 %final_forces.1 = (f32[3,8,8,128]{3,2,1,0:T(8,128)}, f32[36,128]{1,0:T(8,128)}) custom-call(f32[8,16,128]{2,1,0:T(8,128)S(1)} %all-to-all-done.1.answer_ref, f32[4,8,128]{2,1,0:T(8,128)S(1)} %collective-permute-done.2.rest_0_, f32[4,8,128]{2,1,0:T(8,128)S(1)} %collective-permute-done.3.rest_1_, f32[3,8,8,128]{3,2,1,0:T(8,128)S(1)} %get-tuple-element.29.rest_2_, ...), custom_call_target="tpu_custom_call" | custom-call | flops 100000000 | bytes 1048576 | tf_op jit(solution)/shard_map/final_forces/pallas_call | solution.py:665
Async XLA Ops:
  3.0 14.7 %all-to-all-start = ((bf16[8,72,128]{2,1,0:T(8,128)(2,1)}), bf16[8,72,128]{2,1,0:T(8,128)(2,1)S(1)}, u32[]{:S(2)}, u32[]{:S(2)}) async-start(bf16[8,72,128]{2,1,0:T(8,128)(2,1)} %get-tuple-element.17), calls=%async_computation | async-start | bytes 294912 | tf_op jit(solution)/shard_map/all_to_all | solution.py:733
  10.3 2.3 %collective-permute-start = (f32[4,8,128]{2,1,0:T(8,128)S(1)}, f32[4,8,128]{2,1,0:T(8,128)S(1)}, u32[]{:S(2)}, u32[]{:S(2)}) collective-permute-start(f32[4,8,128]{2,1,0:T(8,128)S(1)} %get-tuple-element.18), channel_id=1, source_target_pairs={{0,1},{2,3},{1,0},{3,2},{4,5},{6,7},{5,4},{7,6},{8,9},{10,11},{9,8... | collective-permute-start | bytes 49160 | tf_op jit(solution)/shard_map/ppermute | solution.py:759
  10.3 2.3 %collective-permute-start.1 = (f32[4,8,128]{2,1,0:T(8,128)S(1)}, f32[4,8,128]{2,1,0:T(8,128)S(1)}, u32[]{:S(2)}, u32[]{:S(2)}) collective-permute-start(f32[4,8,128]{2,1,0:T(8,128)S(1)} %get-tuple-element.19), channel_id=1, source_target_pairs={{1,2},{2,1},{5,6},{6,5},{9,10},{10,9},{13,14},{14,13},{17,18},{18,... | collective-permute-start | bytes 49160 | tf_op jit(solution)/shard_map/ppermute | solution.py:759
  20.9 10.5 %all-to-all-start.1 = ((f32[8,16,128]{2,1,0:T(8,128)}), f32[8,16,128]{2,1,0:T(8,128)S(1)}, u32[]{:S(2)}, u32[]{:S(2)}) async-start(f32[8,16,128]{2,1,0:T(8,128)} %micro_response.1), calls=%async_computation.1 | async-start | bytes 131072 | tf_op jit(solution)/shard_map/all_to_all | solution.py:809
  24.3 6.7 %collective-permute-start.2 = (f32[4,8,128]{2,1,0:T(8,128)S(1)}, f32[4,8,128]{2,1,0:T(8,128)S(1)}, u32[]{:S(2)}, u32[]{:S(2)}) collective-permute-start(f32[4,8,128]{2,1,0:T(8,128)S(1)} %get-tuple-element.27), channel_id=1, source_target_pairs={{4,8},{12,16},{20,24},{8,4},{16,12},{24,20},{5,9},{13,17},{21,25},... | collective-permute-start | bytes 49160 | tf_op jit(solution)/shard_map/ppermute | solution.py:759
  25.0 6.4 %collective-permute-start.3 = (f32[4,8,128]{2,1,0:T(8,128)S(1)}, f32[4,8,128]{2,1,0:T(8,128)S(1)}, u32[]{:S(2)}, u32[]{:S(2)}) collective-permute-start(f32[4,8,128]{2,1,0:T(8,128)S(1)} %get-tuple-element.28), channel_id=1, source_target_pairs={{0,4},{8,12},{16,20},{24,28},{4,0},{12,8},{20,16},{28,24},{1,5},{9... | collective-permute-start | bytes 49160 | tf_op jit(solution)/shard_map/ppermute | solution.py:759

commit v7 on v6

--- a/solution.py
+++ b/solution.py
@@ -346,26 +346,26 @@
     hot_ref[...] = jnp.where(iota(hot_ref.shape, 0) == ids, 1.0, 0.0).astype(BF16)
 
     def solve(*accumulators):
-        mains, spares = accumulators[:8], accumulators[8:12]
-        tangent_high, tangent_low = accumulators[12:]
+        mains = (accumulators[:8], accumulators[8:12])
+        spares = accumulators[12:16]
+        tangent_high, tangent_low = accumulators[16:]
         hyper = bits_ref.shape[0]
-        both = range(2)
-        for unit in both:
-            pltpu.matmul_push_rhs(hot_ref[...], 0, unit)
         empty = jnp.zeros((128, modes - bits_ref.shape[1]), BF16)
+        blocks_of_flags = hyper // 128
 
         def flags_of(j):
             rows = jnp.concatenate([bits_ref[128 * j : 128 * j + 128, :], empty], axis=1)
-            pltpu.matmul_acc_lhs(spares[j % 4], rows, load_staged_rhs=0 if j < 2 else None)
-
-        blocks_of_flags = hyper // 128
-        for j in range(blocks_of_flags + 2):
-            if j < blocks_of_flags:
-                flags_of(j)
-            if j >= 2:
-                flags_ref[128 * (j - 2) : 128 * (j - 1), :] = pltpu.matmul_pop(spares[(j - 2) % 4])
-        for unit in both:
-            pltpu.matmul_push_rhs(state_ref[...], 0, unit, transpose=True)
+            pltpu.matmul_acc_lhs(spares[j % 4], rows, load_staged_rhs=None if j else 0)
+
+        def keep_flags(j):
+            flags_ref[128 * j : 128 * j + 128, :] = pltpu.matmul_pop(spares[j % 4])
+
+        def place(i):
+            if i < 8:
+                return mains[0][i]
+            k = (i - 8) // 2
+            return mains[0][k % 8] if i % 2 else mains[1][k % 4]
+
         strip = 16
         strips = hyper // strip
 
@@ -375,10 +375,10 @@
                 copies[n - kept].wait()
             source = blocks_ref.at[n] if n < kept else others_ref.at[n - kept]
             rows = jnp.concatenate([source[c, r : r + strip, :] for c in range(6)], axis=0)
-            pltpu.matmul_acc_lhs(mains[i % 8], rows, load_staged_rhs=0 if i < 2 else None)
+            pltpu.matmul_acc_lhs(place(i), rows, load_staged_rhs=0 if i in (0, 8) else None)
 
         def respond(i, sums):
-            strain = pltpu.matmul_pop(mains[i % 8])
+            strain = pltpu.matmul_pop(place(i))
             e = [strain[c * strip : (c + 1) * strip] for c in range(6)]
             at = slice(i * strip, (i + 1) * strip)
             volume = e[0] + e[1] + e[2]
@@ -403,10 +403,19 @@
 
         sums = [jnp.zeros((8, slots), F32)] * 7
         ahead = 7
-        for i in range(ahead):
+        pltpu.matmul_push_rhs(hot_ref[...], 0, 1)
+        pltpu.matmul_push_rhs(state_ref[...], 0, 0, transpose=True)
+        for j in range(4):
+            flags_of(j)
+        for i in range(8):
             issue(i)
+        for j in range(blocks_of_flags):
+            keep_flags(j)
+            if j + 4 < blocks_of_flags:
+                flags_of(j + 4)
+        pltpu.matmul_push_rhs(state_ref[...], 0, 1, transpose=True)
         for i in range(strips):
-            if i + ahead < strips:
+            if 8 <= i + ahead < strips:
                 issue(i + ahead)
             sums = respond(i, sums)
         for n in range(hyper // modes):
@@ -421,8 +430,9 @@
 
     tangent, sums = pl.run_scoped(
         solve,
-        *[pltpu.ACC(n % 2)((96, slots), F32) for n in range(8)],
-        *[pltpu.ACC(n % 2)((128, slots), F32) for n in range(4)],
+        *[pltpu.ACC(0)((96, slots), F32) for _ in range(8)],
+        *[pltpu.ACC(1)((96, slots), F32) for _ in range(4)],
+        *[pltpu.ACC(1)((128, slots), F32) for _ in range(4)],
         pltpu.ACC(0)((96, slots), F32),
         pltpu.ACC(1)((48, slots), F32),
     )

time: 33 us -> 32.8 us (level)
  no operation moved by 1% of the time
where the time goes in v7:
time: 32.8 us; the launch traced here: 32.3 us
  starting transfers between devices  16.7 us (51%)
  Pallas kernels  9.38 us (29%)
  waiting for transfers between devices  5.57 us (17%)
  between operations  0.72 us (2%)
    pallas_call x5, Pallas kernels, call(): pl.pallas_call(kernel, grid=(1,), out_shape=out_shape, in_specs=specs, ou...  9.38 us
    all_to_all x1, starting transfers between devices, on_device(): received = lax.all_to_all(payload[0], 'macro', 0, 0, tiled=True)  7.29 us
    ppermute x4, starting transfers between devices, swapped(): return lax.ppermute(value, axis, pairs + [(b, a) for a, b in pairs])  6.02 us
    all_to_all x1, waiting for transfers between devices, on_device(): received = lax.all_to_all(payload[0], 'macro', 0, 0, tiled=True)  5.18 us
    all_to_all x1, starting transfers between devices, on_device(): answered = [lax.all_to_all(answer[0], 'macro', 0, 0, tiled=True)]  3.36 us
  transfers between devices with their start and end apart: 6, of which 2 were waited for; matrix products, arithmetic and copies ran while one was open for 0% of the time, Pallas kernels for 9%

profile of v7, /device:TPU:0, one launch (start us, length us, event | category | flops | bytes accessed | tf_op | source)
XLA Modules:
  0.0 32.3 jit_solution(14592875572619579416)
XLA Ops:
  0.6 2.3 %dispatch.1 = (bf16[8,72,128]{2,1,0:T(8,128)(2,1)}, f32[4,8,128]{2,1,0:T(8,128)S(1)}, f32[4,8,128]{2,1,0:T(8,128)S(1)}, f32[4,8,128]{2,1,0:T(8,128)S(1)}, f32[4,...) custom-call(s32[1,128]{1,0:T(1,128)} %bitcast.14, ...), custom_call_target="tpu_custom_call" | custom-call | flops 100000000 | bytes 1048576 | tf_op jit(solution)/shard_map/dispatch/pallas_call | solution.py:675
  3.0 7.3 %all-to-all-start = ((bf16[8,72,128]{2,1,0:T(8,128)(2,1)}), bf16[8,72,128]{2,1,0:T(8,128)(2,1)S(1)}, u32[]{:S(2)}, u32[]{:S(2)}) async-start(bf16[8,72,128]{2,1,0:T(8,128)(2,1)} %get-tuple-element.17), calls=%async_computation | async-start | bytes 294912 | tf_op jit(solution)/shard_map/all_to_all | solution.py:743
  10.3 0.0 collective-permute-start
  10.3 0.7 %collective-permute-start.1 = (f32[4,8,128]{2,1,0:T(8,128)S(1)}, f32[4,8,128]{2,1,0:T(8,128)S(1)}, u32[]{:S(2)}, u32[]{:S(2)}) collective-permute-start(f32[4,8,128]{2,1,0:T(8,128)S(1)} %get-tuple-element.19), channel_id=1, source_target_pairs={{1,2},{2,1},{5,6},{6,5},{9,10},{10,9},{13,14},{14,13},{17,18},{18,... | collective-permute-start | bytes 49160 | tf_op jit(solution)/shard_map/ppermute | solution.py:769
  10.9 1.6 %tables.1 = (bf16[96,1024]{1,0:T(8,128)(2,1)S(1)}, f32[48,128]{1,0:T(8,128)S(1)}, bf16[1024,128]{1,0:T(8,128)(2,1)S(1)}) custom-call(bf16[3,6,256,256]{3,2,1,0:T(8,128)(2,1)S(1)} %get-tuple-element.20.blocks_ref, bf16[6,256]{1,0:T(8,128)(2,1)S(1)} %get-tuple-element.21.map_ref, f32[1,1024]{1,0:T(1,128)S(1)} %get-tuple-element.22.weights_ref, ...), custom_call_target="tpu_custom_call" | custom-call | flops 100000000 | bytes 1048576 | tf_op jit(solution)/shard_map/tables/pallas_call | solution.py:675
  12.5 0.0 collective-permute-done.first_ref
  12.5 0.0 collective-permute-done.1.second_ref
  12.5 5.2 %all-to-all-done.received_ref = bf16[8,72,128]{2,1,0:T(8,128)(2,1)S(1)} async-done(((bf16[8,72,128]{2,1,0:T(8,128)(2,1)}), bf16[8,72,128]{2,1,0:T(8,128)(2,1)S(1)}, u32[]{:S(2)}, u32[]{:S(2)}) %all-to-all-start) | async-done | bytes 147488 | tf_op jit(solution)/shard_map/all_to_all | solution.py:743
  17.7 3.0 %micro_response.1 = f32[8,16,128]{2,1,0:T(8,128)} custom-call(bf16[8,72,128]{2,1,0:T(8,128)(2,1)S(1)} %all-to-all-done.received_ref, f32[4,8,128]{2,1,0:T(8,128)S(1)} %collective-permute-done.first_ref, f32[4,8,128]{2,1,0:T(8,128)S(1)} %collective-permute-done.1.second_ref, f32[48,128]{1,0:T(8,128)S(1)} %get-tuple-element.24.const_ref, ...), custom_call_target="tpu_custom_call" | custom-call | flops 100000000 | bytes 1048576 | tf_op jit(solution)/shard_map/micro_response/pallas_call | solution.py:675
  20.7 3.4 %all-to-all-start.1 = ((f32[8,16,128]{2,1,0:T(8,128)}), f32[8,16,128]{2,1,0:T(8,128)S(1)}, u32[]{:S(2)}, u32[]{:S(2)}) async-start(f32[8,16,128]{2,1,0:T(8,128)} %micro_response.1), calls=%async_computation.1 | async-start | bytes 131072 | tf_op jit(solution)/shard_map/all_to_all | solution.py:819
  24.0 0.7 %collective-permute-start.2 = (f32[4,8,128]{2,1,0:T(8,128)S(1)}, f32[4,8,128]{2,1,0:T(8,128)S(1)}, u32[]{:S(2)}, u32[]{:S(2)}) collective-permute-start(f32[4,8,128]{2,1,0:T(8,128)S(1)} %get-tuple-element.27), channel_id=1, source_target_pairs={{4,8},{12,16},{20,24},{8,4},{16,12},{24,20},{5,9},{13,17},{21,25},... | collective-permute-start | bytes 49160 | tf_op jit(solution)/shard_map/ppermute | solution.py:769
  24.7 4.7 %collective-permute-start.3 = (f32[4,8,128]{2,1,0:T(8,128)S(1)}, f32[4,8,128]{2,1,0:T(8,128)S(1)}, u32[]{:S(2)}, u32[]{:S(2)}) collective-permute-start(f32[4,8,128]{2,1,0:T(8,128)S(1)} %get-tuple-element.28), channel_id=1, source_target_pairs={{0,4},{8,12},{16,20},{24,28},{4,0},{12,8},{20,16},{28,24},{1,5},{9... | collective-permute-start | bytes 49160 | tf_op jit(solution)/shard_map/ppermute | solution.py:769
  29.4 1.3 %elastic_forces.1 = (f32[3,8,8,128]{3,2,1,0:T(8,128)S(1)}, f32[7,16,128]{2,1,0:T(8,128)S(1)}, s32[8,128]{1,0:T(8,128)S(1)}) custom-call(f32[3,8,8,128]{3,2,1,0:T(8,128)} %motion_ref.1, bf16[8,8,128]{2,1,0:T(8,128)(2,1)} %stiff_ref.1, s32[1,128]{1,0:T(1,128)} %bitcast.17, s32[1,128]{1,0:T(1,128)} %bitcast.15, ...), custom_call_target="tpu_custom_call" | custom-call | flops 100000000 | bytes 1048576 | tf_op jit(solution)/shard_map/elastic_forces/pallas_call | solution.py:675
  30.8 0.0 collective-permute-done.2.rest_0_
  30.8 0.4 %collective-permute-done.3.rest_1_ = f32[4,8,128]{2,1,0:T(8,128)S(1)} collective-permute-done((f32[4,8,128]{2,1,0:T(8,128)S(1)}, f32[4,8,128]{2,1,0:T(8,128)S(1)}, u32[]{:S(2)}, u32[]{:S(2)}) %collective-permute-start.3) | collective-permute-done | bytes 16416 | tf_op jit(solution)/shard_map/ppermute | solution.py:769
  31.1 0.0 all-to-all-done.1.answer_ref
  31.1 1.2 %final_forces.1 = (f32[3,8,8,128]{3,2,1,0:T(8,128)}, f32[36,128]{1,0:T(8,128)}) custom-call(f32[8,16,128]{2,1,0:T(8,128)S(1)} %all-to-all-done.1.answer_ref, f32[4,8,128]{2,1,0:T(8,128)S(1)} %collective-permute-done.2.rest_0_, f32[4,8,128]{2,1,0:T(8,128)S(1)} %collective-permute-done.3.rest_1_, f32[3,8,8,128]{3,2,1,0:T(8,128)S(1)} %get-tuple-element.29.rest_2_, ...), custom_call_target="tpu_custom_call" | custom-call | flops 100000000 | bytes 1048576 | tf_op jit(solution)/shard_map/final_forces/pallas_call | solution.py:675
Async XLA Ops:
  3.0 14.7 %all-to-all-start = ((bf16[8,72,128]{2,1,0:T(8,128)(2,1)}), bf16[8,72,128]{2,1,0:T(8,128)(2,1)S(1)}, u32[]{:S(2)}, u32[]{:S(2)}) async-start(bf16[8,72,128]{2,1,0:T(8,128)(2,1)} %get-tuple-element.17), calls=%async_computation | async-start | bytes 294912 | tf_op jit(solution)/shard_map/all_to_all | solution.py:743
  10.3 2.3 %collective-permute-start = (f32[4,8,128]{2,1,0:T(8,128)S(1)}, f32[4,8,128]{2,1,0:T(8,128)S(1)}, u32[]{:S(2)}, u32[]{:S(2)}) collective-permute-start(f32[4,8,128]{2,1,0:T(8,128)S(1)} %get-tuple-element.18), channel_id=1, source_target_pairs={{0,1},{2,3},{1,0},{3,2},{4,5},{6,7},{5,4},{7,6},{8,9},{10,11},{9,8... | collective-permute-start | bytes 49160 | tf_op jit(solution)/shard_map/ppermute | solution.py:769
  10.3 2.3 %collective-permute-start.1 = (f32[4,8,128]{2,1,0:T(8,128)S(1)}, f32[4,8,128]{2,1,0:T(8,128)S(1)}, u32[]{:S(2)}, u32[]{:S(2)}) collective-permute-start(f32[4,8,128]{2,1,0:T(8,128)S(1)} %get-tuple-element.19), channel_id=1, source_target_pairs={{1,2},{2,1},{5,6},{6,5},{9,10},{10,9},{13,14},{14,13},{17,18},{18,... | collective-permute-start | bytes 49160 | tf_op jit(solution)/shard_map/ppermute | solution.py:769
  20.7 10.5 %all-to-all-start.1 = ((f32[8,16,128]{2,1,0:T(8,128)}), f32[8,16,128]{2,1,0:T(8,128)S(1)}, u32[]{:S(2)}, u32[]{:S(2)}) async-start(f32[8,16,128]{2,1,0:T(8,128)} %micro_response.1), calls=%async_computation.1 | async-start | bytes 131072 | tf_op jit(solution)/shard_map/all_to_all | solution.py:819
  24.0 6.7 %collective-permute-start.2 = (f32[4,8,128]{2,1,0:T(8,128)S(1)}, f32[4,8,128]{2,1,0:T(8,128)S(1)}, u32[]{:S(2)}, u32[]{:S(2)}) collective-permute-start(f32[4,8,128]{2,1,0:T(8,128)S(1)} %get-tuple-element.27), channel_id=1, source_target_pairs={{4,8},{12,16},{20,24},{8,4},{16,12},{24,20},{5,9},{13,17},{21,25},... | collective-permute-start | bytes 49160 | tf_op jit(solution)/shard_map/ppermute | solution.py:769
  24.7 6.4 %collective-permute-start.3 = (f32[4,8,128]{2,1,0:T(8,128)S(1)}, f32[4,8,128]{2,1,0:T(8,128)S(1)}, u32[]{:S(2)}, u32[]{:S(2)}) collective-permute-start(f32[4,8,128]{2,1,0:T(8,128)S(1)} %get-tuple-element.28), channel_id=1, source_target_pairs={{0,4},{8,12},{16,20},{24,28},{4,0},{12,8},{20,16},{28,24},{1,5},{9... | collective-permute-start | bytes 49160 | tf_op jit(solution)/shard_map/ppermute | solution.py:769

commit v8 on v7

--- a/solution.py
+++ b/solution.py
@@ -9,6 +9,7 @@
 
 YIELD_STRESS = 1.5
 HARDENING = 0.2
+FACTOR = YIELD_STRESS * (1.0 - HARDENING) * 0.5**0.5
 F32 = jnp.float32
 BF16 = jnp.bfloat16
 VMEM = pltpu.VMEM
@@ -299,6 +300,7 @@
     capacity,
     flag_lanes,
     received_ref,
+    x_face_ref,
     first_ref,
     second_ref,
     const_ref,
@@ -309,6 +311,7 @@
     answer_ref,
     *rest,
 ):
+    del x_face_ref
     if packed:
         corners_ref = None
     else:
@@ -383,11 +386,11 @@
             at = slice(i * strip, (i + 1) * strip)
             volume = e[0] + e[1] + e[2]
             third = volume * (1.0 / 3.0)
-            d = [e[c] - third for c in range(3)]
-            normal = d[0] * d[0] + d[1] * d[1] + d[2] * d[2]
+            d = [e[c] - third for c in range(2)]
+            normal = d[0] * (d[0] + d[1]) + d[1] * d[1]
             shear = e[3] * e[3] + e[4] * e[4] + e[5] * e[5]
-            square = jnp.maximum(normal + 0.5 * shear, YIELD_STRESS * YIELD_STRESS)
-            factor = (YIELD_STRESS * (1.0 - HARDENING)) * lax.rsqrt(square) + (HARDENING - 1.0)
+            square = jnp.maximum(normal + 0.25 * shear, 0.5 * YIELD_STRESS * YIELD_STRESS)
+            factor = FACTOR * lax.rsqrt(square) + (HARDENING - 1.0)
             change = flags_ref[at, :] * factor
             high = change.astype(BF16)
             high_ref[at, :] = high
@@ -397,12 +400,12 @@
             packed_row = jnp.where((lane >= flag_lanes) & (lane < flag_lanes + 3), packed_row, 0.0)
             weight = jnp.sum(packed_row, axis=1, keepdims=True)
             scaled = weight + weight * change
-            terms = [scaled * d[c] for c in range(3)] + [scaled * e[c] for c in range(3, 6)]
+            terms = [scaled * d[c] for c in range(2)] + [scaled * e[c] for c in range(3, 6)]
             terms.append(weight * volume)
             return [total + (term[:8] + term[8:]) for total, term in zip(sums, terms)]
 
-        sums = [jnp.zeros((8, slots), F32)] * 7
-        ahead = 7
+        sums = [jnp.zeros((8, slots), F32)] * 6
+        ahead = 6
         pltpu.matmul_push_rhs(hot_ref[...], 0, 1)
         pltpu.matmul_push_rhs(state_ref[...], 0, 0, transpose=True)
         for j in range(4):
@@ -437,10 +440,11 @@
         pltpu.ACC(1)((48, slots), F32),
     )
 
-    volume = jnp.sum(sums[6], axis=0, keepdims=True)
+    totals = [jnp.sum(value, axis=0, keepdims=True) for value in sums]
+    normals = [totals[0], totals[1], -(totals[0] + totals[1])]
     for c in range(6):
-        total = jnp.sum(sums[c], axis=0, keepdims=True)
-        result_ref[c : c + 1, :] = total + volume if c < 3 else 0.5 * total
+        value = normals[c] + totals[5] if c < 3 else 0.5 * totals[c - 1]
+        result_ref[c : c + 1, :] = value
     const = const_ref[...]
     const = jnp.concatenate([const] * (slots // const.shape[1]), axis=1)
     tangent = tangent + const
@@ -520,6 +524,8 @@
     force_ref,
     edge_ref,
     index_ref,
+    slot_hot_ref,
+    depth_hot_ref,
     node_ref,
     wide_ref,
     stress_ref,
@@ -532,11 +538,12 @@
     points = elem.shape[1]
     column = elem // size_z
     depth = elem - column * size_z
-    index_ref[0:1, :] = slots_of(owner, hosts, capacity)[2]
-    index_ref[1:2, :] = column
-    index_ref[2:3, :] = depth
-    index_ref[3:, :] = jnp.zeros((5, points), jnp.int32)
+    slot = slots_of(owner, hosts, capacity)[2]
+    slot_hot = iota(slot_hot_ref.shape, 0) == slot
+    slot_hot_ref[...] = jnp.where(slot_hot, 1.0, 0.0).astype(BF16)
+    index_ref[...] = jnp.broadcast_to(column, index_ref.shape)
     depth_hot = jnp.where(iota((size_z, points), 0) == depth, 1.0, 0.0).astype(BF16)
+    depth_hot_ref[...] = depth_hot
     column_hot = jnp.where(iota((size_x * size_y, points), 0) == column, 1.0, 0.0).astype(BF16)
     listed = dot_t(column_hot, depth_hot)
     for i in range(size_x):
@@ -577,6 +584,8 @@
         elastic_ref,
         edge_ref,
         index_ref,
+        slot_hot_ref,
+        depth_hot_ref,
         force_ref,
         tangent_ref,
         result_ref,
@@ -585,9 +594,8 @@
         stress_ref,
     ) = rest
     size_x, size_y, size_z = elastic_ref.shape[1:]
-    slot, column, depth = index_ref[0:1, :], index_ref[1:2, :], index_ref[2:3, :]
-    points = slot.shape[1]
-    slot_total = hosts * capacity
+    column = index_ref[0:1, :]
+    points = column.shape[1]
     if packed:
         group_of = iota((8, 128), 1) // capacity
         per_tile = 128 // capacity
@@ -607,9 +615,8 @@
         answer = jnp.concatenate(groups, axis=0)
     else:
         answer = answer_ref[...]
-    slot_hot = jnp.where(iota((slot_total, points), 0) == slot, 1.0, 0.0).astype(BF16)
     parts = jnp.concatenate(pieces(answer, 3), axis=0)
-    chosen = jnp.dot(parts, slot_hot, preferred_element_type=F32)
+    chosen = jnp.dot(parts, slot_hot_ref[...], preferred_element_type=F32)
     result = chosen[:ROWS] + (chosen[ROWS : 2 * ROWS] + chosen[2 * ROWS :])
     result_ref[...] = result
     for i in range(6):
@@ -648,12 +655,11 @@
         upper.append([jnp.stack([value[1], value[3]]) for value in four])
     edge = elastic_of(strains(lower, upper), wide_ref[...])
     rows = (size_x - 1) * size_y
-    depth_hot = jnp.where(iota((size_z, points), 0) == depth, 1.0, 0.0).astype(BF16)
     column_hot = iota((rows, points), 0) == column
     stress_ref[:, 1:size_x, 0:1, :] = jnp.zeros((6, size_x - 1, 1, size_z), F32)
     placed = [jnp.where(column_hot, result[c : c + 1], 0.0) for c in range(6)]
     placed = jnp.concatenate(pieces(jnp.concatenate(placed, axis=0), 2), axis=0)
-    fields = dot_t(placed, depth_hot)
+    fields = dot_t(placed, depth_hot_ref[...])
     for c in range(6):
         field = fields[c * rows : (c + 1) * rows] + fields[(6 + c) * rows : (7 + c) * rows]
         stress_ref[c, 1:size_x, 1 : size_y + 1, :] = field.reshape(size_x - 1, size_y, size_z)
@@ -795,6 +801,7 @@
         else [shape_of((ROWS, slots)), shape_of((2, 8, lanes))],
         (
             received,
+            x_first,
             first,
             second,
             const,
@@ -837,7 +844,13 @@
     elastic = call(
         functools.partial(elastic_kernel, hosts, capacity),
         "elastic_forces",
-        [shape_of(motion.shape), shape_of((7, 16, size_z)), shape_of((8, points), jnp.int32)],
+        [
+            shape_of(motion.shape),
+            shape_of((7, 16, size_z)),
+            shape_of((8, points), jnp.int32),
+            shape_of((slots, points), BF16),
+            shape_of((size_z, points), BF16),
+        ],
         (motion, stiffness, elem, owner, first, second),
         [
             VMEM((3, size_x, 16, size_z), F32),

time: 32.8 us -> 32.8 us (level)
  waiting for transfers between devices: 5.57 us -> 8.28 us
  starting transfers between devices: 16.7 us -> 14 us
    all_to_all x1, waiting for transfers between devices: 0.01 us -> 5.1 us  [on_device(): answered = [lax.all_to_all(answer[0], 'macro', 0, 0, tiled=True)]]
    ppermute x4, starting transfers between devices: 6.02 us -> 3.34 us  [swapped(): return lax.ppermute(value, axis, pairs + [(b, a) for a, b in pairs])]
    all_to_all x1, waiting for transfers between devices: 5.18 us -> 3.17 us  [on_device(): received = lax.all_to_all(payload[0], 'macro', 0, 0, tiled=True)]
    ppermute x4, waiting for transfers between devices: 0.39 us -> 0.01 us  [swapped(): return lax.ppermute(value, axis, pairs + [(b, a) for a, b in pairs])]
where the time goes in v8:
time: 32.8 us; the launch traced here: 32.3 us
  starting transfers between devices  14 us (43%)
  Pallas kernels  9.32 us (28%)
  waiting for transfers between devices  8.28 us (25%)
  between operations  0.72 us (2%)
    pallas_call x5, Pallas kernels, call(): pl.pallas_call(kernel, grid=(1,), out_shape=out_shape, in_specs=specs, ou...  9.32 us
    all_to_all x1, starting transfers between devices, on_device(): received = lax.all_to_all(payload[0], 'macro', 0, 0, tiled=True)  7.29 us
    all_to_all x1, waiting for transfers between devices, on_device(): answered = [lax.all_to_all(answer[0], 'macro', 0, 0, tiled=True)]  5.1 us
    all_to_all x1, starting transfers between devices, on_device(): answered = [lax.all_to_all(answer[0], 'macro', 0, 0, tiled=True)]  3.36 us
    ppermute x4, starting transfers between devices, swapped(): return lax.ppermute(value, axis, pairs + [(b, a) for a, b in pairs])  3.34 us
    all_to_all x1, waiting for transfers between devices, on_device(): received = lax.all_to_all(payload[0], 'macro', 0, 0, tiled=True)  3.17 us
  transfers between devices with their start and end apart: 6, of which 2 were waited for; matrix products, arithmetic and copies ran while one was open for 0% of the time, Pallas kernels for 9%

profile of v8, /device:TPU:0, one launch (start us, length us, event | category | flops | bytes accessed | tf_op | source)
XLA Modules:
  0.0 32.3 jit_solution(4023141752620871742)
XLA Ops:
  0.6 2.3 %dispatch.1 = (bf16[8,72,128]{2,1,0:T(8,128)(2,1)}, f32[4,8,128]{2,1,0:T(8,128)S(1)}, f32[4,8,128]{2,1,0:T(8,128)S(1)}, f32[4,8,128]{2,1,0:T(8,128)S(1)}, f32[4,...) custom-call(s32[1,128]{1,0:T(1,128)} %bitcast.14, ...), custom_call_target="tpu_custom_call" | custom-call | flops 100000000 | bytes 1048576 | tf_op jit(solution)/shard_map/dispatch/pallas_call | solution.py:681
  3.0 7.3 %all-to-all-start = ((bf16[8,72,128]{2,1,0:T(8,128)(2,1)}), bf16[8,72,128]{2,1,0:T(8,128)(2,1)S(1)}, u32[]{:S(2)}, u32[]{:S(2)}) async-start(bf16[8,72,128]{2,1,0:T(8,128)(2,1)} %get-tuple-element.19), calls=%async_computation | async-start | bytes 294912 | tf_op jit(solution)/shard_map/all_to_all | solution.py:749
  10.3 2.0 %collective-permute-start = (f32[4,8,128]{2,1,0:T(8,128)S(1)}, f32[4,8,128]{2,1,0:T(8,128)S(1)}, u32[]{:S(2)}, u32[]{:S(2)}) collective-permute-start(f32[4,8,128]{2,1,0:T(8,128)S(1)} %get-tuple-element.20), channel_id=1, source_target_pairs={{0,4},{8,12},{16,20},{24,28},{4,0},{12,8},{20,16},{28,24},{1,5},{9... | collective-permute-start | bytes 49160 | tf_op jit(solution)/shard_map/ppermute | solution.py:775
  12.3 0.0 collective-permute-start.1
  12.3 0.7 %collective-permute-start.2 = (f32[4,8,128]{2,1,0:T(8,128)S(1)}, f32[4,8,128]{2,1,0:T(8,128)S(1)}, u32[]{:S(2)}, u32[]{:S(2)}) collective-permute-start(f32[4,8,128]{2,1,0:T(8,128)S(1)} %get-tuple-element.22), channel_id=1, source_target_pairs={{1,2},{2,1},{5,6},{6,5},{9,10},{10,9},{13,14},{14,13},{17,18},{18,... | collective-permute-start | bytes 49160 | tf_op jit(solution)/shard_map/ppermute | solution.py:775
  12.9 1.6 %tables.1 = (bf16[96,1024]{1,0:T(8,128)(2,1)S(1)}, f32[48,128]{1,0:T(8,128)S(1)}, bf16[1024,128]{1,0:T(8,128)(2,1)S(1)}) custom-call(bf16[3,6,256,256]{3,2,1,0:T(8,128)(2,1)S(1)} %get-tuple-element.23.blocks_ref, bf16[6,256]{1,0:T(8,128)(2,1)S(1)} %get-tuple-element.24.map_ref, f32[1,1024]{1,0:T(1,128)S(1)} %get-tuple-element.25.weights_ref, ...), custom_call_target="tpu_custom_call" | custom-call | flops 100000000 | bytes 1048576 | tf_op jit(solution)/shard_map/tables/pallas_call | solution.py:681
  14.5 0.0 collective-permute-done.x_face_ref.rest_1_
  14.5 0.0 collective-permute-done.1.first_ref
  14.5 0.0 collective-permute-done.2.second_ref
  14.5 3.2 %all-to-all-done.received_ref = bf16[8,72,128]{2,1,0:T(8,128)(2,1)S(1)} async-done(((bf16[8,72,128]{2,1,0:T(8,128)(2,1)}), bf16[8,72,128]{2,1,0:T(8,128)(2,1)S(1)}, u32[]{:S(2)}, u32[]{:S(2)}) %all-to-all-start) | async-done | bytes 147488 | tf_op jit(solution)/shard_map/all_to_all | solution.py:749
  17.7 2.9 %micro_response.1 = f32[8,16,128]{2,1,0:T(8,128)} custom-call(bf16[8,72,128]{2,1,0:T(8,128)(2,1)S(1)} %all-to-all-done.received_ref, f32[4,8,128]{2,1,0:T(8,128)S(1)} %collective-permute-done.x_face_ref.rest_1_, f32[4,8,128]{2,1,0:T(8,128)S(1)} %collective-permute-done.1.first_ref, f32[4,8,128]{2,1,0:T(8,128)S(1)} %collective-permute-done.2.second_ref, ...), custom_call_target="tpu_custom_call" | custom-call | flops 100000000 | bytes 1048576 | tf_op jit(solution)/shard_map/micro_response/pallas_call | solution.py:681
  20.6 3.4 %all-to-all-start.1 = ((f32[8,16,128]{2,1,0:T(8,128)}), f32[8,16,128]{2,1,0:T(8,128)S(1)}, u32[]{:S(2)}, u32[]{:S(2)}) async-start(f32[8,16,128]{2,1,0:T(8,128)} %micro_response.1), calls=%async_computation.1 | async-start | bytes 131072 | tf_op jit(solution)/shard_map/all_to_all | solution.py:826
  24.0 0.7 %collective-permute-start.3 = (f32[4,8,128]{2,1,0:T(8,128)S(1)}, f32[4,8,128]{2,1,0:T(8,128)S(1)}, u32[]{:S(2)}, u32[]{:S(2)}) collective-permute-start(f32[4,8,128]{2,1,0:T(8,128)S(1)} %get-tuple-element.30), channel_id=1, source_target_pairs={{4,8},{12,16},{20,24},{8,4},{16,12},{24,20},{5,9},{13,17},{21,25},... | collective-permute-start | bytes 49160 | tf_op jit(solution)/shard_map/ppermute | solution.py:775
  24.6 1.4 %elastic_forces.1 = (f32[3,8,8,128]{3,2,1,0:T(8,128)S(1)}, f32[7,16,128]{2,1,0:T(8,128)S(1)}, s32[8,128]{1,0:T(8,128)S(1)}, bf16[256,128]{1,0:T(8,128)(2,1)S(1)}, bf16[128,128]{1,0:T(8,128)(2,1)S(1)}) custom-call(f32[3,8,8,128]{3,2,1,0:T(8,128)} %motion_ref.1, bf16[8,8,128]{2,1,0:T(8,128)(2,1)} %stiff_ref.1, s32[1,128]{1,0:T(1,128)} %bitcast.17, ...), custom_call_target="tpu_custom_call" | custom-call | flops 100000000 | bytes 1048576 | tf_op jit(solution)/shard_map/elastic_forces/pallas_call | solution.py:681
  26.0 0.0 collective-permute-done.3.rest_0_
  26.0 5.1 %all-to-all-done.1.answer_ref = f32[8,16,128]{2,1,0:T(8,128)S(1)} async-done(((f32[8,16,128]{2,1,0:T(8,128)}), f32[8,16,128]{2,1,0:T(8,128)S(1)}, u32[]{:S(2)}, u32[]{:S(2)}) %all-to-all-start.1) | async-done | bytes 65568 | tf_op jit(solution)/shard_map/all_to_all | solution.py:826
  31.1 1.2 %final_forces.1 = (f32[3,8,8,128]{3,2,1,0:T(8,128)}, f32[36,128]{1,0:T(8,128)}) custom-call(f32[8,16,128]{2,1,0:T(8,128)S(1)} %all-to-all-done.1.answer_ref, f32[4,8,128]{2,1,0:T(8,128)S(1)} %collective-permute-done.3.rest_0_, f32[4,8,128]{2,1,0:T(8,128)S(1)} %collective-permute-done.x_face_ref.rest_1_, f32[3,8,8,128]{3,2,1,0:T(8,128)S(1)} %get-tuple-element.31.rest_2_, ...), custom_call_target="tpu_custom_call" | custom-call | flops 100000000 | bytes 1048576 | tf_op jit(solution)/shard_map/final_forces/pallas_call | solution.py:681
Async XLA Ops:
  3.0 14.7 %all-to-all-start = ((bf16[8,72,128]{2,1,0:T(8,128)(2,1)}), bf16[8,72,128]{2,1,0:T(8,128)(2,1)S(1)}, u32[]{:S(2)}, u32[]{:S(2)}) async-start(bf16[8,72,128]{2,1,0:T(8,128)(2,1)} %get-tuple-element.19), calls=%async_computation | async-start | bytes 294912 | tf_op jit(solution)/shard_map/all_to_all | solution.py:749
  10.3 4.3 %collective-permute-start = (f32[4,8,128]{2,1,0:T(8,128)S(1)}, f32[4,8,128]{2,1,0:T(8,128)S(1)}, u32[]{:S(2)}, u32[]{:S(2)}) collective-permute-start(f32[4,8,128]{2,1,0:T(8,128)S(1)} %get-tuple-element.20), channel_id=1, source_target_pairs={{0,4},{8,12},{16,20},{24,28},{4,0},{12,8},{20,16},{28,24},{1,5},{9... | collective-permute-start | bytes 49160 | tf_op jit(solution)/shard_map/ppermute | solution.py:775
  12.3 2.2 %collective-permute-start.1 = (f32[4,8,128]{2,1,0:T(8,128)S(1)}, f32[4,8,128]{2,1,0:T(8,128)S(1)}, u32[]{:S(2)}, u32[]{:S(2)}) collective-permute-start(f32[4,8,128]{2,1,0:T(8,128)S(1)} %get-tuple-element.21), channel_id=1, source_target_pairs={{0,1},{2,3},{1,0},{3,2},{4,5},{6,7},{5,4},{7,6},{8,9},{10,11},{9,8... | collective-permute-start | bytes 49160 | tf_op jit(solution)/shard_map/ppermute | solution.py:775
  12.3 2.3 %collective-permute-start.2 = (f32[4,8,128]{2,1,0:T(8,128)S(1)}, f32[4,8,128]{2,1,0:T(8,128)S(1)}, u32[]{:S(2)}, u32[]{:S(2)}) collective-permute-start(f32[4,8,128]{2,1,0:T(8,128)S(1)} %get-tuple-element.22), channel_id=1, source_target_pairs={{1,2},{2,1},{5,6},{6,5},{9,10},{10,9},{13,14},{14,13},{17,18},{18,... | collective-permute-start | bytes 49160 | tf_op jit(solution)/shard_map/ppermute | solution.py:775
  20.6 10.5 %all-to-all-start.1 = ((f32[8,16,128]{2,1,0:T(8,128)}), f32[8,16,128]{2,1,0:T(8,128)S(1)}, u32[]{:S(2)}, u32[]{:S(2)}) async-start(f32[8,16,128]{2,1,0:T(8,128)} %micro_response.1), calls=%async_computation.1 | async-start | bytes 131072 | tf_op jit(solution)/shard_map/all_to_all | solution.py:826
  24.0 2.0 %collective-permute-start.3 = (f32[4,8,128]{2,1,0:T(8,128)S(1)}, f32[4,8,128]{2,1,0:T(8,128)S(1)}, u32[]{:S(2)}, u32[]{:S(2)}) collective-permute-start(f32[4,8,128]{2,1,0:T(8,128)S(1)} %get-tuple-element.30), channel_id=1, source_target_pairs={{4,8},{12,16},{20,24},{8,4},{16,12},{24,20},{5,9},{13,17},{21,25},... | collective-permute-start | bytes 49160 | tf_op jit(solution)/shard_map/ppermute | solution.py:775

commit v9 on v8

--- a/solution.py
+++ b/solution.py
@@ -111,7 +111,7 @@
     inputs, basis_ref, payload_out, refs = refs[:9], refs[9], refs[10], list(refs[11:])
     ids_ref = None if direct else refs.pop(0)
     first_ref, second_ref, x_first_ref, x_second_ref, blocks_ref = refs[:5]
-    buffers, payload_ref, sems = refs[8:14] + refs[5:8], refs[14], refs[15]
+    buffers, payload_ref, sems = refs[8:13] + [refs[5], refs[13]] + refs[6:8], refs[14], refs[15]
     arrivals = [
         pltpu.make_async_copy(value, buffer, sems.at[n])
         for n, (value, buffer) in enumerate(zip(inputs, buffers))
@@ -127,9 +127,9 @@
     ]
     for copy in later:
         copy.start()
-    owner_ref, elem_ref, motion_ref, history_ref, pattern_ref, stiff_ref, map_ref, _, _ = buffers
+    motion_ref, elem_ref, owner_ref, history_ref, pattern_ref, map_ref, stiff_ref, _, _ = buffers
     size_x, size_y, size_z = motion_ref.shape[1:]
-    for copy in arrivals:
+    for copy in arrivals[:6]:
         copy.wait()
     owner = owner_ref[...]
     points = owner.shape[1]
@@ -179,6 +179,8 @@
         ids_ref[...] = ids.astype(BF16)
     leave = pltpu.make_async_copy(payload_ref, payload_out, sems.at[9])
     leave.start()
+    for copy in arrivals[6:]:
+        copy.wait()
     stiffness = stiff_ref[...].astype(F32)
     even = lax.rem(lax.axis_index("micro"), 2) == 0
     for i in range(size_x):
@@ -730,7 +732,7 @@
         else [shape_of((slots, modes), BF16), shape_of((hosts, modes), BF16)]
     )
     swap, x_swap = shape_of((4, size_x, size_z)), shape_of((4, size_y, size_z))
-    arguments = (owner, elem, motion, history, pattern, stiffness)
+    arguments = (motion, elem, owner, history, pattern, map_rows, stiffness)
     small = (map_rows, in_hbm(weights.reshape(1, hyper)), in_hbm(patterns.T))
     *payload, first, second, x_first, x_second, blocks, map_here, weights, bit_words = call(
         functools.partial(dispatch_kernel, hosts, capacity, direct),
@@ -738,8 +740,8 @@
         sent
         + [swap, swap, x_swap, x_swap, shape_of((kept, 6, wide, modes), BF16)]
         + [shape_of(value.shape, value.dtype) for value in small],
-        (*arguments, *small, rows),
-        [VMEM(value.shape, value.dtype) for value in (*arguments, sent[0])]
+        (*arguments, *small[1:], rows),
+        [VMEM(value.shape, value.dtype) for value in (*arguments[:5], stiffness, sent[0])]
         + [pltpu.SemaphoreType.DMA((10 + kept,))],
         raw=10,
         raw_out=1,

time: 32.8 us -> 32.7 us (level)
  no operation moved by 1% of the time
where the time goes in v9:
time: 32.7 us; the launch traced here: 32.3 us
  starting transfers between devices  14 us (43%)
  Pallas kernels  9.31 us (28%)
  waiting for transfers between devices  8.28 us (25%)
  between operations  0.72 us (2%)
    pallas_call x5, Pallas kernels, call(): pl.pallas_call(kernel, grid=(1,), out_shape=out_shape, in_specs=specs, ou...  9.31 us
    all_to_all x1, starting transfers between devices, on_device(): received = lax.all_to_all(payload[0], 'macro', 0, 0, tiled=True)  7.29 us
    all_to_all x1, waiting for transfers between devices, on_device(): answered = [lax.all_to_all(answer[0], 'macro', 0, 0, tiled=True)]  5.1 us
    all_to_all x1, starting transfers between devices, on_device(): answered = [lax.all_to_all(answer[0], 'macro', 0, 0, tiled=True)]  3.36 us
    ppermute x4, starting transfers between devices, swapped(): return lax.ppermute(value, axis, pairs + [(b, a) for a, b in pairs])  3.34 us
    all_to_all x1, waiting for transfers between devices, on_device(): received = lax.all_to_all(payload[0], 'macro', 0, 0, tiled=True)  3.17 us
  transfers between devices with their start and end apart: 6, of which 2 were waited for; matrix products, arithmetic and copies ran while one was open for 0% of the time, Pallas kernels for 9%

profile of v9, /device:TPU:0, one launch (start us, length us, event | category | flops | bytes accessed | tf_op | source)
XLA Modules:
  0.0 32.3 jit_solution(17240324739287453917)
XLA Ops:
  0.6 2.3 %dispatch.1 = (bf16[8,72,128]{2,1,0:T(8,128)(2,1)}, f32[4,8,128]{2,1,0:T(8,128)S(1)}, f32[4,8,128]{2,1,0:T(8,128)S(1)}, f32[4,8,128]{2,1,0:T(8,128)S(1)}, f32[4,...) custom-call(f32[3,8,8,128]{3,2,1,0:T(8,128)} %motion_ref.1, ...), custom_call_target="tpu_custom_call" | custom-call | flops 100000000 | bytes 1048576 | tf_op jit(solution)/shard_map/dispatch/pallas_call | solution.py:683
  2.9 7.3 %all-to-all-start = ((bf16[8,72,128]{2,1,0:T(8,128)(2,1)}), bf16[8,72,128]{2,1,0:T(8,128)(2,1)S(1)}, u32[]{:S(2)}, u32[]{:S(2)}) async-start(bf16[8,72,128]{2,1,0:T(8,128)(2,1)} %get-tuple-element.19), calls=%async_computation | async-start | bytes 294912 | tf_op jit(solution)/shard_map/all_to_all | solution.py:751
  10.2 2.0 %collective-permute-start = (f32[4,8,128]{2,1,0:T(8,128)S(1)}, f32[4,8,128]{2,1,0:T(8,128)S(1)}, u32[]{:S(2)}, u32[]{:S(2)}) collective-permute-start(f32[4,8,128]{2,1,0:T(8,128)S(1)} %get-tuple-element.20), channel_id=1, source_target_pairs={{0,4},{8,12},{16,20},{24,28},{4,0},{12,8},{20,16},{28,24},{1,5},{9... | collective-permute-start | bytes 49160 | tf_op jit(solution)/shard_map/ppermute | solution.py:777
  12.3 0.0 collective-permute-start.1
  12.3 0.7 %collective-permute-start.2 = (f32[4,8,128]{2,1,0:T(8,128)S(1)}, f32[4,8,128]{2,1,0:T(8,128)S(1)}, u32[]{:S(2)}, u32[]{:S(2)}) collective-permute-start(f32[4,8,128]{2,1,0:T(8,128)S(1)} %get-tuple-element.22), channel_id=1, source_target_pairs={{1,2},{2,1},{5,6},{6,5},{9,10},{10,9},{13,14},{14,13},{17,18},{18,... | collective-permute-start | bytes 49160 | tf_op jit(solution)/shard_map/ppermute | solution.py:777
  12.9 1.6 %tables.1 = (bf16[96,1024]{1,0:T(8,128)(2,1)S(1)}, f32[48,128]{1,0:T(8,128)S(1)}, bf16[1024,128]{1,0:T(8,128)(2,1)S(1)}) custom-call(bf16[3,6,256,256]{3,2,1,0:T(8,128)(2,1)S(1)} %get-tuple-element.23.blocks_ref, bf16[6,256]{1,0:T(8,128)(2,1)S(1)} %get-tuple-element.24.map_ref, f32[1,1024]{1,0:T(1,128)S(1)} %get-tuple-element.25.weights_ref, ...), custom_call_target="tpu_custom_call" | custom-call | flops 100000000 | bytes 1048576 | tf_op jit(solution)/shard_map/tables/pallas_call | solution.py:683
  14.5 0.0 collective-permute-done.x_face_ref.rest_1_
  14.5 0.0 collective-permute-done.1.first_ref
  14.5 0.0 collective-permute-done.2.second_ref
  14.5 3.2 %all-to-all-done.received_ref = bf16[8,72,128]{2,1,0:T(8,128)(2,1)S(1)} async-done(((bf16[8,72,128]{2,1,0:T(8,128)(2,1)}), bf16[8,72,128]{2,1,0:T(8,128)(2,1)S(1)}, u32[]{:S(2)}, u32[]{:S(2)}) %all-to-all-start) | async-done | bytes 147488 | tf_op jit(solution)/shard_map/all_to_all | solution.py:751
  17.7 2.9 %micro_response.1 = f32[8,16,128]{2,1,0:T(8,128)} custom-call(bf16[8,72,128]{2,1,0:T(8,128)(2,1)S(1)} %all-to-all-done.received_ref, f32[4,8,128]{2,1,0:T(8,128)S(1)} %collective-permute-done.x_face_ref.rest_1_, f32[4,8,128]{2,1,0:T(8,128)S(1)} %collective-permute-done.1.first_ref, f32[4,8,128]{2,1,0:T(8,128)S(1)} %collective-permute-done.2.second_ref, ...), custom_call_target="tpu_custom_call" | custom-call | flops 100000000 | bytes 1048576 | tf_op jit(solution)/shard_map/micro_response/pallas_call | solution.py:683
  20.6 3.4 %all-to-all-start.1 = ((f32[8,16,128]{2,1,0:T(8,128)}), f32[8,16,128]{2,1,0:T(8,128)S(1)}, u32[]{:S(2)}, u32[]{:S(2)}) async-start(f32[8,16,128]{2,1,0:T(8,128)} %micro_response.1), calls=%async_computation.1 | async-start | bytes 131072 | tf_op jit(solution)/shard_map/all_to_all | solution.py:828
  24.0 0.7 %collective-permute-start.3 = (f32[4,8,128]{2,1,0:T(8,128)S(1)}, f32[4,8,128]{2,1,0:T(8,128)S(1)}, u32[]{:S(2)}, u32[]{:S(2)}) collective-permute-start(f32[4,8,128]{2,1,0:T(8,128)S(1)} %get-tuple-element.30), channel_id=1, source_target_pairs={{4,8},{12,16},{20,24},{8,4},{16,12},{24,20},{5,9},{13,17},{21,25},... | collective-permute-start | bytes 49160 | tf_op jit(solution)/shard_map/ppermute | solution.py:777
  24.6 1.4 %elastic_forces.1 = (f32[3,8,8,128]{3,2,1,0:T(8,128)S(1)}, f32[7,16,128]{2,1,0:T(8,128)S(1)}, s32[8,128]{1,0:T(8,128)S(1)}, bf16[256,128]{1,0:T(8,128)(2,1)S(1)}, bf16[128,128]{1,0:T(8,128)(2,1)S(1)}) custom-call(f32[3,8,8,128]{3,2,1,0:T(8,128)} %motion_ref.1, bf16[8,8,128]{2,1,0:T(8,128)(2,1)} %stiff_ref.1, s32[1,128]{1,0:T(1,128)} %bitcast.15, ...), custom_call_target="tpu_custom_call" | custom-call | flops 100000000 | bytes 1048576 | tf_op jit(solution)/shard_map/elastic_forces/pallas_call | solution.py:683
  26.0 0.0 collective-permute-done.3.rest_0_
  26.0 5.1 %all-to-all-done.1.answer_ref = f32[8,16,128]{2,1,0:T(8,128)S(1)} async-done(((f32[8,16,128]{2,1,0:T(8,128)}), f32[8,16,128]{2,1,0:T(8,128)S(1)}, u32[]{:S(2)}, u32[]{:S(2)}) %all-to-all-start.1) | async-done | bytes 65568 | tf_op jit(solution)/shard_map/all_to_all | solution.py:828
  31.1 1.2 %final_forces.1 = (f32[3,8,8,128]{3,2,1,0:T(8,128)}, f32[36,128]{1,0:T(8,128)}) custom-call(f32[8,16,128]{2,1,0:T(8,128)S(1)} %all-to-all-done.1.answer_ref, f32[4,8,128]{2,1,0:T(8,128)S(1)} %collective-permute-done.3.rest_0_, f32[4,8,128]{2,1,0:T(8,128)S(1)} %collective-permute-done.x_face_ref.rest_1_, f32[3,8,8,128]{3,2,1,0:T(8,128)S(1)} %get-tuple-element.31.rest_2_, ...), custom_call_target="tpu_custom_call" | custom-call | flops 100000000 | bytes 1048576 | tf_op jit(solution)/shard_map/final_forces/pallas_call | solution.py:683
Async XLA Ops:
  2.9 14.7 %all-to-all-start = ((bf16[8,72,128]{2,1,0:T(8,128)(2,1)}), bf16[8,72,128]{2,1,0:T(8,128)(2,1)S(1)}, u32[]{:S(2)}, u32[]{:S(2)}) async-start(bf16[8,72,128]{2,1,0:T(8,128)(2,1)} %get-tuple-element.19), calls=%async_computation | async-start | bytes 294912 | tf_op jit(solution)/shard_map/all_to_all | solution.py:751
  10.2 4.3 %collective-permute-start = (f32[4,8,128]{2,1,0:T(8,128)S(1)}, f32[4,8,128]{2,1,0:T(8,128)S(1)}, u32[]{:S(2)}, u32[]{:S(2)}) collective-permute-start(f32[4,8,128]{2,1,0:T(8,128)S(1)} %get-tuple-element.20), channel_id=1, source_target_pairs={{0,4},{8,12},{16,20},{24,28},{4,0},{12,8},{20,16},{28,24},{1,5},{9... | collective-permute-start | bytes 49160 | tf_op jit(solution)/shard_map/ppermute | solution.py:777
  12.3 2.2 %collective-permute-start.1 = (f32[4,8,128]{2,1,0:T(8,128)S(1)}, f32[4,8,128]{2,1,0:T(8,128)S(1)}, u32[]{:S(2)}, u32[]{:S(2)}) collective-permute-start(f32[4,8,128]{2,1,0:T(8,128)S(1)} %get-tuple-element.21), channel_id=1, source_target_pairs={{0,1},{2,3},{1,0},{3,2},{4,5},{6,7},{5,4},{7,6},{8,9},{10,11},{9,8... | collective-permute-start | bytes 49160 | tf_op jit(solution)/shard_map/ppermute | solution.py:777
  12.3 2.3 %collective-permute-start.2 = (f32[4,8,128]{2,1,0:T(8,128)S(1)}, f32[4,8,128]{2,1,0:T(8,128)S(1)}, u32[]{:S(2)}, u32[]{:S(2)}) collective-permute-start(f32[4,8,128]{2,1,0:T(8,128)S(1)} %get-tuple-element.22), channel_id=1, source_target_pairs={{1,2},{2,1},{5,6},{6,5},{9,10},{10,9},{13,14},{14,13},{17,18},{18,... | collective-permute-start | bytes 49160 | tf_op jit(solution)/shard_map/ppermute | solution.py:777
  20.6 10.5 %all-to-all-start.1 = ((f32[8,16,128]{2,1,0:T(8,128)}), f32[8,16,128]{2,1,0:T(8,128)S(1)}, u32[]{:S(2)}, u32[]{:S(2)}) async-start(f32[8,16,128]{2,1,0:T(8,128)} %micro_response.1), calls=%async_computation.1 | async-start | bytes 131072 | tf_op jit(solution)/shard_map/all_to_all | solution.py:828
  24.0 2.0 %collective-permute-start.3 = (f32[4,8,128]{2,1,0:T(8,128)S(1)}, f32[4,8,128]{2,1,0:T(8,128)S(1)}, u32[]{:S(2)}, u32[]{:S(2)}) collective-permute-start(f32[4,8,128]{2,1,0:T(8,128)S(1)} %get-tuple-element.30), channel_id=1, source_target_pairs={{4,8},{12,16},{20,24},{8,4},{16,12},{24,20},{5,9},{13,17},{21,25},... | collective-permute-start | bytes 49160 | tf_op jit(solution)/shard_map/ppermute | solution.py:777
